TPU v7x, 256 devices: a whole 4x4x8 slice. The times are simulated.
256 devices in a mesh: loop: 128 (over z, y, x_lo, core), rhs: 2 (over x_hi).
Axes of the slice: x: 4 (x_hi: 2, x_lo: 2; x = x_hi * 2 + x_lo), y: 4, z: 8, core: 2. Of those that a mesh axis runs over, the one named last changes fastest.
Arguments:
- signals: bfloat16 [128, 262144], P('rhs', 'loop'), may hold values from -6 to 6
- near_tiles: bfloat16 [1024, 8, 256, 256], P('loop', 'rhs'), may hold values from -0.125 to 0.125
- near_list: int32 [1024, 8], P('loop'), may hold values from 0 to 1023, as said below
- leaf_basis: bfloat16 [1024, 64, 256], P('loop'), may hold values from -0.375 to 0.375
- transfer: bfloat16 [1024, 64, 64], P('loop'), may hold values from -0.75 to 0.75
- parent: int32 [1024], P('loop'), may hold values from 0 to 255, as said below
- coupling: bfloat16 [1024, 64, 1536], P('loop'), may hold values from -0.15625 to 0.15625
- far_list: int32 [1024, 24], P('loop'), may hold values from 0 to 1023, as said below
- parent_coupling: bfloat16 [256, 64, 1024], P('loop'), may hold values from -0.1875 to 0.1875
- parent_far: int32 [256, 16], P('loop'), may hold values from 0 to 255, as said below
Outputs:
- potentials: bfloat16 [128, 262144], P('rhs', 'loop')
Inputs may be any that keep to these rules, and one draw needn't show every extreme that they name: `near_list`: entry 0 of each row is the leaf itself; the other entries of a row are distinct leaves at most 4 leaves away from it along the closed cycle of 1024 leaves, on either side; in every device's rows some leaf names the leaves exactly 4 away on both sides. Leaves of one device have parents of that device only (ids d * 2 and d * 2 + 1), and the parent ids never decrease along a device's leaves; every parent has 1 to 7 consecutive leaves, and some parent of every device has exactly 7. `far_list`: leaf d * 8 + i lies on device d. Among all entries of the rows of one device's 8 leaves, at most 2 name leaves of any one device, and in every draw each device's rows name some device's leaves exactly 2 times. `parent_far`: parent d * 2 + i lies on device d. Among all entries of the rows of one device's 2 parents, at most 2 name parents of any one device, and in every draw each device's rows name some device's parents exactly 2 times.
All inputs are finite; a program needn't handle non-finite values.
Results may differ from a plain program's by a relative error of at most 0.011.
Values may be sent and summed in bfloat16 or wider, within the bound.
No kernel may reach another device: no remote copies, remote signals or barrier semaphores. Data moves between devices by JAX's collectives and lax.ppermute only.
A program may use at most 128 MiB of HBM per device.

v0:
```python
import jax
import jax.numpy as jnp
from jax import lax
from jax.sharding import PartitionSpec as P


def with_halo(cells, sides, width):
    for axis, dim in sides:
        count = lax.axis_size(axis)
        head = lax.slice_in_dim(cells, 0, width, axis=dim)
        tail = lax.slice_in_dim(cells, cells.shape[dim] - width, cells.shape[dim], axis=dim)
        cells = jnp.concatenate(
            [
                lax.ppermute(tail, axis, [(i, (i + 1) % count) for i in range(count)]),
                cells,
                lax.ppermute(head, axis, [((i + 1) % count, i) for i in range(count)]),
            ],
            axis=dim,
        )
    return cells


def near_product(extended, tile_set, source_index, leaf_size):
    row_count = extended.shape[0]
    point_blocks = extended.reshape(row_count, extended.shape[1] // leaf_size, leaf_size)
    picked = jnp.take(point_blocks, source_index, axis=1)
    product = jnp.einsum("tjab,rtjb->rta", tile_set, picked, preferred_element_type=jnp.float32)
    return product.reshape(row_count, -1)


def shards(
    signals,
    near_tiles,
    near_list,
    leaf_basis,
    transfer,
    parent,
    coupling,
    far_list,
    parent_coupling,
    parent_far,
):
    leaf_count = leaf_basis.shape[0]
    basis_rank = leaf_basis.shape[1]
    leaf_size = leaf_basis.shape[2]
    column_count = signals.shape[0]
    parent_count = parent_coupling.shape[0]
    far_count = far_list.shape[1]
    pfar_count = parent_far.shape[1]
    cycle_size = lax.axis_size("loop")
    own_index = lax.axis_index("loop")
    near_reach = leaf_count // 2
    halo_width = near_reach * leaf_size
    total_leaves = leaf_count * cycle_size
    start_leaf = own_index * leaf_count - near_reach
    near_index = jnp.mod(near_list - start_leaf, total_leaves)
    tile_set = lax.all_gather(near_tiles, "rhs", axis=1, tiled=True)
    extended = with_halo(signals, (("loop", 1),), halo_width)
    near = near_product(extended, tile_set, near_index, leaf_size)
    local_blocks = signals.reshape(column_count, leaf_count, leaf_size)
    coefficients = jnp.einsum(
        "ckb,rcb->crk", leaf_basis, local_blocks, preferred_element_type=jnp.float32
    ).astype(jnp.bfloat16)
    own_parent = parent - own_index * parent_count
    membership = own_parent[:, None] == jnp.arange(parent_count)[None, :]
    lifted = jnp.einsum("crk,cka->cra", coefficients, transfer, preferred_element_type=jnp.float32)
    parents = jnp.einsum(
        "cp,cra->pra", membership.astype(jnp.float32), lifted, precision=lax.Precision.HIGHEST
    ).astype(jnp.bfloat16)
    flat_leaf = coefficients.reshape(leaf_count, column_count * basis_rank)
    flat_parent = parents.reshape(parent_count, column_count * basis_rank)
    leaf_ids = far_list.reshape(-1)
    parent_ids = parent_far.reshape(-1)
    every_leaf, every_parent = (
        lax.all_gather(flat_leaf, "loop", axis=0, tiled=True),
        lax.all_gather(flat_parent, "loop", axis=0, tiled=True),
    )
    leaf_picked = jnp.take(every_leaf, leaf_ids, axis=0)
    parent_picked = jnp.take(every_parent, parent_ids, axis=0)
    leaf_sources = leaf_picked.reshape(leaf_count, far_count, column_count, basis_rank)
    leaf_mats = coupling.reshape(leaf_count, basis_rank, far_count, basis_rank)
    leaf_far = jnp.einsum(
        "tjrk,tajk->tra", leaf_sources, leaf_mats, preferred_element_type=jnp.float32
    )
    parent_sources = parent_picked.reshape(parent_count, pfar_count, column_count, basis_rank)
    parent_mats = parent_coupling.reshape(parent_count, basis_rank, pfar_count, basis_rank)
    parent_field = jnp.einsum(
        "pjrk,pajk->pra", parent_sources, parent_mats, preferred_element_type=jnp.float32
    ).astype(jnp.bfloat16)
    down_in = jnp.einsum(
        "cp,pra->cra",
        membership.astype(jnp.bfloat16),
        parent_field,
        preferred_element_type=jnp.float32,
    ).astype(jnp.bfloat16)
    descended = jnp.einsum("cra,cka->crk", down_in, transfer, preferred_element_type=jnp.float32)
    combined = (leaf_far + descended).astype(jnp.bfloat16)
    far_out = jnp.einsum("crk,ckb->rcb", combined, leaf_basis, preferred_element_type=jnp.float32)
    far_out = far_out.reshape(column_count, leaf_count * leaf_size)
    return (near + far_out).astype(jnp.bfloat16)


def solution(mesh):
    in_specs = (
        P("rhs", "loop"),
        P("loop", "rhs", None, None),
        P("loop", None),
        P("loop", None, None),
        P("loop", None, None),
        P("loop"),
        P("loop", None, None),
        P("loop", None),
        P("loop", None, None),
        P("loop", None),
    )
    out_specs = P("rhs", "loop")
    return jax.shard_map(shards, mesh=mesh, in_specs=in_specs, out_specs=out_specs, check_vma=False)
```

profile of v0, /device:TPU:1, one launch (start us, length us, event | category | flops | bytes accessed | tf_op | source)
XLA Modules:
  0.0 583.4 jit_solution(11393493400101121685)
XLA Ops:
  6.5 0.0 copy-start
  6.5 0.0 all-gather.9.cloned.1.call-start
  6.5 0.7 broadcast_subtract_fusion
  7.3 0.2 copy-done
  7.5 1.2 convolution_convert_fusion.1
  8.7 0.0 copy-start.5
  8.7 0.0 copy-start.4
  8.7 1.1 fusion.42
  9.8 0.0 copy-start.2
  9.9 0.4 convolution_convert_fusion.2
  10.3 0.7 reshape.150
  11.0 0.0 all-gather.9.cloned.1.call-update
  11.0 0.0 all-gather.5.cloned.1.call-start
  11.0 0.7 all-gather.5.cloned.1.call-update
  11.7 0.0 all-gather.7.cloned.1.call-start
  11.8 0.8 reshape.118
  12.6 0.0 all-gather.7.cloned.1.call-update
  12.6 0.0 copy-done.1
  12.7 2.7 collective-permute-start
  15.3 0.9 collective-permute-start.1
  16.2 0.0 copy-done.6
  16.3 0.1 reshape.126
  16.3 0.0 copy-done.7
  16.3 0.1 reshape.122
  16.4 0.0 copy-done.5
  16.4 0.1 reshape.119
  16.6 0.0 copy-done.4
  16.6 0.3 reshape.123
  16.9 0.0 copy-done.2
  17.0 3.2 reshape.120
  20.1 0.0 collective-permute-done
  20.2 0.2 collective-permute-done.1
  20.5 0.7 gather_fusion
  21.1 206.1 %all-gather.9.cloned.1.call-done = bf16[128,2,4096]{2,1,0:T(2,128)(2,1)} async-done(((bf16[1,2,4096]{2,1,0:T(2,128)(2,1)}), bf16[128,2,4096]{2,1,0:T(2,128)(2,1)}) %all-gather.9.cloned.1.call-update) | async-done | bytes 2097168 | tf_op jit(solution)/shard_map/all_gather | solution.py:76
  227.2 4.1 reshape.151
  231.3 2.8 gather_fusion.2
  234.2 1.3 gather.20
  235.5 1.4 fusion.20
  236.9 0.2 convolution_convert_fusion
  237.1 101.7 %all-gather.5.cloned.1.call-done = bf16[8,8,256,256]{3,2,1,0:T(8,128)(2,1)} async-done(((bf16[8,4,256,256]{3,2,1,0:T(8,128)(2,1)}), bf16[8,8,256,256]{3,2,1,0:T(8,128)(2,1)}) %all-gather.5.cloned.1.call-update) | async-done | bytes 8388624 | tf_op jit(solution)/shard_map/all_gather | solution.py:57
  338.8 6.0 %fusion.9 = f32[8,64,256]{2,1,0:T(8,128)S(1)} fusion(bf16[8,8,256,256]{3,2,1,0:T(8,128)(2,1)} %all-gather.5.cloned.1.call-done, bf16[8,8,64,256]{3,2,1,0:T(8,128)(2,1)S(1)} %bitcast.43, pred[8,8]{1,0:T(8,128)(4,1)S(1)} %get-tuple-element.5), kind=kOutput, calls=%fused_computation.12 | convolution fusion | flops 537919488 | bytes 11010112 | tf_op jit(solution)/shard_map/tjab,rtjb->rta/dot_general | solution.py:27
  344.9 215.1 %all-gather.7.cloned.1.call-done = bf16[1024,4096]{1,0:T(8,128)(2,1)} async-done(((bf16[8,4096]{1,0:T(8,128)(2,1)}), bf16[1024,4096]{1,0:T(8,128)(2,1)}) %all-gather.7.cloned.1.call-update) | async-done | bytes 8388624 | tf_op jit(solution)/shard_map/all_gather | solution.py:75
  560.0 7.5 %gather_fusion.1 = bf16[192,4096]{1,0:T(8,128)(2,1)S(1)} fusion(bf16[1024,4096]{1,0:T(8,128)(2,1)} %all-gather.7.cloned.1.call-done, s32[1024]{0:T(1024)S(1)} %pad_clamp_fusion.1), kind=kCustom, calls=%fused_computation.1 | custom fusion | bytes 3146496 | tf_op jit(solution)/shard_map/jit(_take)/gather | solution.py:78
  567.5 4.4 gather.18
  571.9 3.9 fusion.14
  575.8 0.0 copy-done.3
  575.8 0.3 fusion.13
  576.1 0.7 copy.39
  (16 shorter events, 0.2 us)
Async XLA Ops:
  6.5 1.0 copy-start
  6.5 6.1 %copy-start.1 = (bf16[64,2048]{1,0:T(8,128)(2,1)S(1)}, bf16[64,2048]{1,0:T(8,128)(2,1)}, u32[]{:S(2)}) copy-start(bf16[64,2048]{1,0:T(8,128)(2,1)} %param.10) | copy-start | bytes 786436
  6.5 220.7 %all-gather.9.cloned.1.call-start = ((), (), s32[]{:S(2)}) async-start(), calls=%async_computation.2 | async-start | bytes 2113536 | tf_op jit(solution)/shard_map/all_gather | solution.py:76
  7.5 8.7 %copy-start.6 = (s32[8,8]{1,0:T(8,128)S(1)}, s32[8,8]{1,0:T(8,128)}, u32[]{:S(2)}) copy-start(s32[8,8]{1,0:T(8,128)} %param.12) | copy-start | bytes 772
  7.5 8.8 %copy-start.7 = (s32[2,16]{1,0:T(2,128)S(1)}, s32[2,16]{1,0:T(2,128)}, u32[]{:S(2)}) copy-start(s32[2,16]{1,0:T(2,128)} %param.19) | copy-start | bytes 388
  8.7 7.7 %copy-start.5 = (s32[8,24]{1,0:T(8,128)S(1)}, s32[8,24]{1,0:T(8,128)}, u32[]{:S(2)}) copy-start(s32[8,24]{1,0:T(8,128)} %param.17) | copy-start | bytes 2308
  8.7 7.9 %copy-start.4 = (bf16[2,64,1024]{2,1,0:T(8,128)(2,1)S(1)}, bf16[2,64,1024]{2,1,0:T(8,128)(2,1)}, u32[]{:S(2)}) copy-start(bf16[2,64,1024]{2,1,0:T(8,128)(2,1)} %param.18) | copy-start | bytes 786436
  9.8 7.1 %copy-start.2 = (bf16[8,64,1536]{2,1,0:T(8,128)(2,1)S(1)}, bf16[8,64,1536]{2,1,0:T(8,128)(2,1)}, u32[]{:S(2)}) copy-start(bf16[8,64,1536]{2,1,0:T(8,128)(2,1)} %param.16) | copy-start | bytes 4718596
  11.0 327.8 %all-gather.5.cloned.1.call-start = ((), (), s32[]{:S(2)}) async-start(), calls=%async_computation | async-start | bytes 12582912 | tf_op jit(solution)/shard_map/all_gather | solution.py:57
  11.7 548.2 %all-gather.7.cloned.1.call-start = ((), (), s32[]{:S(2)}) async-start(), calls=%async_computation.1 | async-start | bytes 8454144 | tf_op jit(solution)/shard_map/all_gather | solution.py:75
  12.7 7.5 %collective-permute-start = (bf16[64,1024]{1,0:T(8,128)(2,1)S(1)}, bf16[64,1024]{1,0:T(8,128)(2,1)S(1)}, u32[]{:S(2)}, u32[]{:S(2)}) collective-permute-start(bf16[64,1024]{1,0:T(8,128)(2,1)S(1)} %get-tuple-element.7), channel_id=1, source_target_pairs={{0,2},{2,4},{4,6},{6,8},{8,10},{10,12},{12,14},{14,16},{16,18},{18... | collective-permute-start | bytes 393224 | tf_op jit(solution)/shard_map/ppermute | solution.py:14
  15.3 5.0 collective-permute-start.1
  571.9 3.9 copy-start.3
Sparse Core Ops, SparseCore 0:
  11.1 216.0 all-gather.8
  229.0 109.7 all-gather.4
  340.7 219.2 all-gather.6
where the time goes:
time: 584 us; the launch traced here: 583 us
  waiting for transfers between devices  524 us (90%)
  local copies, waits for them, and re-layouts  27.2 us (5%)
  matrix products  14.6 us (2%)
  between operations  13.3 us (2%)
    all_gather x1, waiting for transfers between devices, shards(): lax.all_gather(flat_leaf, 'loop', axis=0, tiled=True)  215 us
    all_gather x1, waiting for transfers between devices, shards(): lax.all_gather(flat_parent, 'loop', axis=0, tiled=True)  206 us
    all_gather x1, waiting for transfers between devices, shards(): tile_set = lax.all_gather(near_tiles, 'rhs', axis=1, tiled=True)  102 us
    gather x2, local copies, waits for them, and re-layouts, shards(): leaf_picked = jnp.take(every_leaf, leaf_ids, axis=0)  11.9 us
  transfers between devices with their start and end apart: 5, of which 4 were waited for; matrix products, arithmetic and copies ran while one was open for 4% of the time, Pallas kernels for 0%

commit v1 on v0

v1 whole, which is shorter than its diff:
```python
import functools

import jax
import jax.numpy as jnp
from jax import lax
from jax.experimental import pallas as pl
from jax.experimental.pallas import tpu as pltpu
from jax.sharding import PartitionSpec as P

Z, Y, X, C = 8, 4, 2, 2
PLANE = Y * X * C
MIB = 1 << 20
NT = (((1,), (1,)), ((), ()))
NN = (((1,), (0,)), ((), ()))


def loop_moves(target):
    moves = []
    for d in range(Z * PLANE):
        z, y, x, c = d // PLANE, d // (X * C) % Y, d // C % X, d % C
        z, y, x, c = target(z, y, x, c)
        moves.append((d, ((z % Z * Y + y % Y) * X + x) * C + c))
    return moves


def dot(a, b, dims):
    return lax.dot_general(a, b, dims, preferred_element_type=jnp.float32)


def pack(block):
    half = block.shape[0] // 2
    return jnp.concatenate([block[:half], block[half:]], axis=1)


def unpack(block):
    half = block.shape[1] // 2
    return jnp.concatenate([block[:, :half], block[:, half:]], axis=0)


def upward_kernel(place, parent, signals, basis, transfer, ids_col, ids_row, coef_out, pay_out, slot_out):
    leaf_count, rank, leaf_size = basis.shape
    sums = [jnp.zeros((signals.shape[0], rank), jnp.float32) for _ in range(2)]
    for c in range(leaf_count):
        block = signals[:, c * leaf_size : (c + 1) * leaf_size]
        coefs = dot(block, basis[c], NT).astype(jnp.bfloat16)
        coef_out[c] = pack(coefs)
        lifted = dot(coefs, transfer[c], NN)
        member = parent[c] - place[0] * 2
        sums = [s + jnp.where(member == i, lifted, 0.0) for i, s in enumerate(sums)]
    for i, s in enumerate(sums):
        pay_out[i * 32 : (i + 1) * 32] = pack(s.astype(jnp.bfloat16))
    count = ids_col.shape[0]
    owner_col, owner_row = ids_col[...] // leaf_count, ids_row[...] // leaf_count
    same = owner_col == owner_row
    at_col = lax.broadcasted_iota(jnp.int32, (count, count), 0)
    at_row = lax.broadcasted_iota(jnp.int32, (count, count), 1)
    seen_col = jnp.sum(jnp.where(same & (at_row < at_col), 1, 0), axis=1, keepdims=True)
    seen_row = jnp.sum(jnp.where(same & (at_col < at_row), 1, 0), axis=0, keepdims=True)
    hop = (owner_row // PLANE - place[0] // PLANE + Z) % Z
    slot_out[...] = owner_row % PLANE * (2 * Z) + hop * 2 + seen_row
    peers = lax.broadcasted_iota(jnp.int32, (count, Z * PLANE), 1)
    member_col = (ids_col[...] % leaf_count).astype(jnp.float32)
    rows = [
        jnp.sum(jnp.where((owner_col == peers) & (seen_col == i), member_col, 0.0), axis=0, keepdims=True)
        for i in range(2)
    ]
    rows.append(jnp.zeros((14, Z * PLANE), jnp.float32))
    pay_out[64:80] = jnp.concatenate(rows, axis=0).astype(jnp.bfloat16)


def upward(place, parent, signals, basis, transfer, far_list):
    leaf_count = basis.shape[0]
    smem = pl.BlockSpec(memory_space=pltpu.SMEM)
    vmem = pl.BlockSpec(memory_space=pltpu.VMEM)
    return pl.pallas_call(
        upward_kernel,
        out_shape=(
            jax.ShapeDtypeStruct((leaf_count, 32, 128), jnp.bfloat16),
            jax.ShapeDtypeStruct((80, 128), jnp.bfloat16),
            jax.ShapeDtypeStruct((1, far_list.size), jnp.int32),
        ),
        in_specs=[smem, smem, vmem, vmem, vmem, vmem, vmem],
        out_specs=(vmem, vmem, vmem),
        compiler_params=pltpu.CompilerParams(vmem_limit_bytes=16 * MIB),
        name="upward",
    )(place, parent, signals, basis, transfer, far_list.reshape(-1, 1), far_list.reshape(1, -1))


def select_kernel(place, wanted, *refs):
    planes, send = refs[:Z], refs[Z]
    step = pl.program_id(0)
    own = place[0] % PLANE
    first = place[0] // PLANE
    for i in range(send.shape[0]):
        peer = step * send.shape[0] + i
        dy = (peer // (X * C) - own // (X * C) + Y) % Y
        dx = (peer // C % X - own // C % X + X) % X
        dc = (peer % C - own % C + C) % C
        row = ((dc * Y + dy) * X + dx) * 2
        for hop in range(Z):
            lane = (first + hop) % Z * PLANE + own
            for k in range(2):
                send[i, hop * 2 + k] = planes[hop][wanted[row + k, lane]]


def select(place, wanted, planes):
    smem = pl.BlockSpec(memory_space=pltpu.SMEM)
    vmem = pl.BlockSpec(memory_space=pltpu.VMEM)
    per_step = 4
    return pl.pallas_call(
        select_kernel,
        grid=(PLANE // per_step,),
        out_shape=jax.ShapeDtypeStruct((PLANE, 2 * Z, 32, 128), jnp.bfloat16),
        in_specs=[smem, smem] + [vmem] * Z,
        out_specs=pl.BlockSpec((per_step, 2 * Z, 32, 128), lambda s: (s, 0, 0, 0)),
        compiler_params=pltpu.CompilerParams(vmem_limit_bytes=16 * MIB),
        name="select",
    )(place, wanted, *planes)


def near_kernel(place, near_list, both, before, after, tiles, own_out, other_out, extended):
    step = pl.program_id(0)
    rows, width = both.shape
    reach = before.shape[1]

    @pl.when(step == 0)
    def _():
        extended[:, :reach] = before[...]
        extended[:, reach : reach + width] = both[...]
        extended[:, reach + width :] = after[...]

    total = jnp.zeros((rows, tiles.shape[2]), jnp.float32)
    leaves = 8 * Z * PLANE
    for j in range(tiles.shape[1]):
        source = near_list[step, place[1] * tiles.shape[1] + j]
        at = (source - place[0] * 8 + 4 + leaves) % leaves
        block = extended[:, pl.ds(pl.multiple_of(at * 256, 256), 256)]
        total = total + dot(block, tiles[0, j], NT)
    own_out[...] = total[: rows // 2]
    other_out[...] = total[rows // 2 :].astype(jnp.bfloat16)


def near_field(place, near_list, both, before, after, tiles):
    smem = pl.BlockSpec(memory_space=pltpu.SMEM)
    vmem = pl.BlockSpec(memory_space=pltpu.VMEM)
    leaf_count, near_count, leaf_size, _ = tiles.shape
    rows, width = both.shape
    out_spec = pl.BlockSpec((rows // 2, leaf_size), lambda t: (0, t))
    return pl.pallas_call(
        near_kernel,
        grid=(leaf_count,),
        out_shape=(
            jax.ShapeDtypeStruct((rows // 2, width), jnp.float32),
            jax.ShapeDtypeStruct((rows // 2, width), jnp.bfloat16),
        ),
        in_specs=[smem, smem, vmem, vmem, vmem]
        + [pl.BlockSpec((1, near_count, leaf_size, leaf_size), lambda t: (t, 0, 0, 0))],
        out_specs=(out_spec, out_spec),
        scratch_shapes=[pltpu.VMEM((rows, 2 * width), jnp.bfloat16)],
        compiler_params=pltpu.CompilerParams(vmem_limit_bytes=16 * MIB),
        cost_estimate=pl.CostEstimate(flops=600_000_000, bytes_accessed=6_000_000, transcendentals=0),
        name="near_field",
    )(place, near_list, both, before, after, tiles)


def downward_kernel(
    place,
    parent,
    slots,
    parent_far,
    blocks,
    mine,
    theirs,
    parent_coupling,
    coupling,
    transfer,
    basis,
    near_own,
    near_in,
    out,
    fields,
    stacked,
):
    step = pl.program_id(0)
    rank = transfer.shape[1]
    half = blocks.shape[1]
    sources = coupling.shape[2] // rank

    @pl.when(step == 0)
    def _():
        own_plane = place[0] % PLANE
        for p in range(fields.shape[0]):
            total = jnp.zeros((2 * half, rank), jnp.float32)
            for j in range(parent_far.shape[1]):
                source = parent_far[p, j]
                device = source // 2
                dy = (device // (X * C) % Y - own_plane // (X * C) + Y) % Y
                dx = (device // C % X - own_plane // C % X + X) % X
                at = ((device // PLANE * Y + dy) * X + dx) * 2 + source % 2
                block = jnp.where(device % C == own_plane % C, mine[at], theirs[at])
                mat = parent_coupling[p, :, j * rank : (j + 1) * rank]
                total = total + dot(unpack(block), mat, NT)
            fields[p] = total.astype(jnp.bfloat16)

    for j in range(sources):
        block = blocks[slots[step, j]]
        stacked[:half, j * rank : (j + 1) * rank] = block[:, :rank]
        stacked[half:, j * rank : (j + 1) * rank] = block[:, rank:]
    leaf_far = dot(stacked[...], coupling[0], NT)
    field = fields[parent[step] - place[0] * 2]
    combined = (leaf_far + dot(field, transfer[0], NT)).astype(jnp.bfloat16)
    far_out = dot(combined, basis[0], NN)
    out[...] = (near_own[...] + near_in[...].astype(jnp.float32) + far_out).astype(jnp.bfloat16)


def downward(place, parent, slots, parent_far, blocks, mine, theirs, parent_coupling, coupling, transfer, basis, near_own, near_in):
    smem = pl.BlockSpec(memory_space=pltpu.SMEM)
    vmem = pl.BlockSpec(memory_space=pltpu.VMEM)
    leaf_count, rank, leaf_size = basis.shape
    rows = near_own.shape[0]

    def per_leaf(*shape):
        return pl.BlockSpec((1,) + shape, lambda t: (t, 0, 0))

    wide = pl.BlockSpec((rows, leaf_size), lambda t: (0, t))
    return pl.pallas_call(
        downward_kernel,
        grid=(leaf_count,),
        out_shape=jax.ShapeDtypeStruct(near_own.shape, jnp.bfloat16),
        in_specs=[smem] * 4
        + [vmem] * 4
        + [per_leaf(rank, coupling.shape[2]), per_leaf(rank, rank), per_leaf(rank, leaf_size), wide, wide],
        out_specs=wide,
        scratch_shapes=[
            pltpu.VMEM((parent_coupling.shape[0], rows, rank), jnp.bfloat16),
            pltpu.VMEM((rows, coupling.shape[2]), jnp.bfloat16),
        ],
        compiler_params=pltpu.CompilerParams(vmem_limit_bytes=24 * MIB),
        name="downward",
    )(place, parent, slots, parent_far, blocks, mine, theirs, parent_coupling, coupling, transfer, basis, near_own, near_in)


def shards(
    signals,
    near_tiles,
    near_list,
    leaf_basis,
    transfer,
    parent,
    coupling,
    far_list,
    parent_coupling,
    parent_far,
):
    columns, width = signals.shape
    place = jnp.stack([lax.axis_index("loop"), lax.axis_index("rhs")]).astype(jnp.int32)
    along = functools.partial(lax.ppermute, axis_name="loop")
    swap = functools.partial(lax.ppermute, axis_name="rhs", perm=[(0, 1), (1, 0)])
    z_down = loop_moves(lambda z, y, x, c: (z - 1, y, x, c))
    z_up = loop_moves(lambda z, y, x, c: (z + 1, y, x, c))
    x_swap = loop_moves(lambda z, y, x, c: (z, y, 1 - x, c))
    c_swap = loop_moves(lambda z, y, x, c: (z, y, x, 1 - c))
    z_groups = [[z * PLANE + p for z in range(Z)] for p in range(PLANE)]
    planes_of = [[z * PLANE + p for p in range(PLANE)] for z in range(Z)]

    other = swap(signals)
    coefs, payload, slots = upward(place, parent, signals, leaf_basis, transfer, far_list)

    planes = [coefs] + [None] * (Z - 1)
    for h in range(1, Z // 2 + 1):
        planes[h] = along(planes[h - 1], perm=z_down)
        if h < Z // 2:
            planes[Z - h] = along(planes[(Z - h + 1) % Z], perm=z_up)

    pair = jnp.stack([payload, along(payload, perm=x_swap)])
    quads = [pair] + [
        along(pair, perm=loop_moves(lambda z, y, x, c, dy=dy: (z, y - dy, x, c))) for dy in range(1, Y)
    ]
    plane_pay = jnp.stack(quads)
    wanted_mine = plane_pay[:, :, 64:80]
    wanted_theirs = along(wanted_mine, perm=c_swap)
    wanted = jnp.stack([wanted_mine, wanted_theirs])[:, :, :, :2].reshape(-1, Z * PLANE).astype(jnp.int32)
    parents_mine = lax.all_gather(
        plane_pay[:, :, :64].reshape(-1, 128), "loop", axis=0, tiled=True, axis_index_groups=z_groups
    )
    parents_theirs = along(parents_mine, perm=c_swap)
    parents_mine = parents_mine.reshape(-1, 32, 128)
    parents_theirs = parents_theirs.reshape(-1, 32, 128)

    both = jnp.concatenate([signals, other], axis=0)
    reach = width // 2
    count = Z * PLANE
    before = along(both[:, reach:], perm=[(i, (i + 1) % count) for i in range(count)])
    after = along(both[:, :reach], perm=[((i + 1) % count, i) for i in range(count)])
    near_own, near_other = near_field(place, near_list, both, before, after, near_tiles)
    near_in = swap(near_other)

    send = select(place, wanted, planes)
    blocks = lax.all_to_all(send, "loop", 0, 0, tiled=True, axis_index_groups=planes_of)
    return downward(
        place,
        parent,
        slots.reshape(far_list.shape),
        parent_far,
        blocks.reshape(-1, 32, 128),
        parents_mine,
        parents_theirs,
        parent_coupling,
        coupling,
        transfer,
        leaf_basis,
        near_own,
        near_in,
    )


def solution(mesh):
    in_specs = (
        P("rhs", "loop"),
        P("loop", "rhs", None, None),
        P("loop", None),
        P("loop", None, None),
        P("loop", None, None),
        P("loop"),
        P("loop", None, None),
        P("loop", None),
        P("loop", None, None),
        P("loop", None),
    )
    out_specs = P("rhs", "loop")
    return jax.shard_map(shards, mesh=mesh, in_specs=in_specs, out_specs=out_specs, check_vma=False)
```

time: 584 us -> 140 us (0.24)
  waiting for transfers between devices: 524 us -> 51.7 us
  starting transfers between devices: 3.67 us -> 42.1 us
  Pallas kernels: 0 us -> 16.7 us
  local copies, waits for them, and re-layouts: 27.2 us -> 12.2 us
  matrix products: 14.6 us -> 0 us
    all_gather x3 -> x1, waiting for transfers between devices: 523 us -> 0.02 us  [shards(): lax.all_gather(plane_pay[:, :, :64].reshape(-1, 128), 'loop', axis=0, til...]
    ppermute x2 -> x17, waiting for transfers between devices: 0.21 us -> 51.7 us  [the longest x1 26.9 us: shards(): other = swap(signals)]
    ppermute x2 -> x17, starting transfers between devices: 3.59 us -> 33.2 us  [the longest x4 14 us: shards(): planes[h] = along(planes[h - 1], perm=z_down)]
    gather x5 -> x0, local copies, waits for them, and re-layouts: 16.7 us -> none  [the longest x2 11.9 us: shards(): leaf_picked = jnp.take(every_leaf, leaf_ids, axis=0)]
    pallas_call x0 -> x4, Pallas kernels: none -> 16.7 us  [the longest x1 7.27 us: downward(): pl.pallas_call(downward_kernel, grid=(leaf_count,), out_shape=jax.ShapeDt...]
    dot_general x8 -> x0, matrix products: 14.6 us -> none  [the longest x1 6.02 us: near_product(): jnp.einsum('tjab,rtjb->rta', tile_set, picked, preferred_element_type=jnp...]
    all_to_all x0 -> x1, starting transfers between devices: none -> 8.85 us  [shards(): lax.all_to_all(send, 'loop', 0, 0, tiled=True, axis_index_groups=planes_of)]
  transfers between devices with their start and end apart: 5 -> 19, of which waited for: 4 -> 11; matrix products, arithmetic and copies ran while one was open for 4% -> 1% of each run, Pallas kernels for 0% -> 6%
where the time goes in v1:
time: 140 us; the launch traced here: 138 us
  waiting for transfers between devices  51.7 us (37%)
  starting transfers between devices  42.1 us (30%)
  Pallas kernels  16.7 us (12%)
  between operations  13.5 us (10%)
  local copies, waits for them, and re-layouts  12.2 us (9%)
  other arithmetic  1.42 us (1%)
    ppermute x1, waiting for transfers between devices, shards(): other = swap(signals)  26.9 us
    ppermute x4, starting transfers between devices, shards(): planes[h] = along(planes[h - 1], perm=z_down)  14 us
    unnamed x29, local copies, waits for them, and re-layouts  9.95 us
    all_to_all x1, starting transfers between devices, shards(): lax.all_to_all(send, 'loop', 0, 0, tiled=True, axis_index_groups=planes_of)  8.85 us
    pallas_call x1, Pallas kernels, downward(): pl.pallas_call(downward_kernel, grid=(leaf_count,), out_shape=jax.ShapeDt...  7.27 us
    ppermute x1, waiting for transfers between devices, shards(): near_in = swap(near_other)  6.19 us
    ppermute x1, waiting for transfers between devices, shards(): along(both[:, reach:], perm=[(i, (i + 1) % count) for i in range(count)])  6.12 us
    ppermute x1, starting transfers between devices, shards(): wanted_theirs = along(wanted_mine, perm=c_swap)  4.83 us
  transfers between devices with their start and end apart: 19, of which 11 were waited for; matrix products, arithmetic and copies ran while one was open for 1% of the time, Pallas kernels for 6%

profile of v1, /device:TPU:1, one launch (start us, length us, event | category | flops | bytes accessed | tf_op | source)
XLA Modules:
  0.0 137.6 jit_solution(3875487522739190490)
XLA Ops:
  6.5 0.8 reshape.32.ids_col
  7.3 0.8 reshape.25.ids_row
  8.1 0.1 pad_add_fusion.place
  8.2 1.0 copy-done.2
  9.1 0.9 copy-done.4
  10.1 0.9 copy-done.7
  11.0 0.7 copy-done.11
  11.6 1.5 %upward.1 = (bf16[8,32,128]{2,1,0:T(8,128)(2,1)S(1)}, bf16[80,128]{1,0:T(8,128)(2,1)S(1)}, s32[1,192]{1,0:T(1,128)S(1)}) custom-call(s32[2]{0:T(128)S(1)} %pad_add_fusion.place, s32[8]{0:T(128)S(1)} %copy-done.11, bf16[64,2048]{1,0:T(8,128)(2,1)S(1)} %copy-done.4, bf16[8,64,256]{2,1,0:T(8,128)(2,1)S(1)} %copy-done.2, bf16[8,64,64]{2,1,0:T(8,128)(2,1)S(1)} %copy-done.7, ...), custom_call_target="tpu_custom_call" | custom-call | tf_op jit(solution)/shard_map/upward/pallas_call | solution.py:75
  13.1 2.1 %collective-permute-start = (bf16[80,128]{1,0:T(8,128)(2,1)S(1)}, bf16[80,128]{1,0:T(8,128)(2,1)S(1)}, u32[]{:S(2)}, u32[]{:S(2)}) collective-permute-start(bf16[80,128]{1,0:T(8,128)(2,1)S(1)} %get-tuple-element.11), channel_id=1, source_target_pairs={{0,4},{2,6},{4,0},{6,2},{8,12},{10,14},{12,8},{14,10},{16,20},{18,... | collective-permute-start | bytes 61448 | tf_op jit(solution)/shard_map/ppermute | solution.py:275
  15.2 1.2 collective-permute-done
  16.4 3.1 %collective-permute-start.1 = (bf16[2,80,128]{2,1,0:T(8,128)(2,1)S(1)}, bf16[2,80,128]{2,1,0:T(8,128)(2,1)S(1)}, u32[]{:S(2)}, u32[]{:S(2)}) collective-permute-start(bf16[2,80,128]{2,1,0:T(8,128)(2,1)S(1)} %get-tuple-element.18), channel_id=1, source_target_pairs={{0,24},{2,26},{4,28},{6,30},{8,0},{10,2},{12,4},{14,6},{16,8},{18,... | collective-permute-start | bytes 122888 | tf_op jit(solution)/shard_map/ppermute | solution.py:277
  19.5 0.3 collective-permute-start.2
  19.8 0.7 collective-permute-start.3
  20.5 0.1 collective-permute-done.1
  20.6 3.3 %collective-permute-done.2 = bf16[2,80,128]{2,1,0:T(8,128)(2,1)S(1)} collective-permute-done((bf16[2,80,128]{2,1,0:T(8,128)(2,1)S(1)}, bf16[2,80,128]{2,1,0:T(8,128)(2,1)S(1)}, u32[]{:S(2)}, u32[]{:S(2)}) %collective-permute-start.2) | collective-permute-done | bytes 40992 | tf_op jit(solution)/shard_map/ppermute | solution.py:277
  23.9 0.4 collective-permute-done.3
  24.3 0.7 pad_maximum_fusion
  24.9 0.0 all-gather.2.cloned.1.call-update
  25.0 5.7 %collective-permute-start.5 = (bf16[8,32,128]{2,1,0:T(8,128)(2,1)S(1)}, bf16[8,32,128]{2,1,0:T(8,128)(2,1)S(1)}, u32[]{:S(2)}, u32[]{:S(2)}) collective-permute-start(bf16[8,32,128]{2,1,0:T(8,128)(2,1)S(1)} %get-tuple-element.12.refs_0_), channel_id=1, source_target_pairs={{0,224},{2,226},{4,228},{6,230},{8,232},{10,234},{12,236},{14,238}... | collective-permute-start | bytes 196616 | tf_op jit(solution)/shard_map/ppermute | solution.py:271
  30.6 1.3 collective-permute-done.5.refs_1_
  32.0 3.0 %collective-permute-start.6 = (bf16[8,32,128]{2,1,0:T(8,128)(2,1)S(1)}, bf16[8,32,128]{2,1,0:T(8,128)(2,1)S(1)}, u32[]{:S(2)}, u32[]{:S(2)}) collective-permute-start(bf16[8,32,128]{2,1,0:T(8,128)(2,1)S(1)} %collective-permute-done.5.refs_1_), channel_id=1, source_target_pairs={{0,224},{2,226},{4,228},{6,230},{8,232},{10,234},{12,236},{14,238}... | collective-permute-start | bytes 196616 | tf_op jit(solution)/shard_map/ppermute | solution.py:271
  35.0 4.8 %collective-permute-start.4 = (bf16[4,2,16,128]{3,2,1,0:T(8,128)(2,1)S(1)}, bf16[4,2,16,128]{3,2,1,0:T(8,128)(2,1)S(1)}, u32[]{:S(2)}, u32[]{:S(2)}) collective-permute-start(bf16[4,2,16,128]{3,2,1,0:T(8,128)(2,1)S(1)} %pad_maximum_fusion.4), channel_id=1, source_target_pairs={{0,2},{2,0},{4,6},{6,4},{8,10},{10,8},{12,14},{14,12},{16,18},{18,... | collective-permute-start | bytes 98312 | tf_op jit(solution)/shard_map/ppermute | solution.py:281
  39.8 2.7 %collective-permute-start.7 = (bf16[8,32,128]{2,1,0:T(8,128)(2,1)S(1)}, bf16[8,32,128]{2,1,0:T(8,128)(2,1)S(1)}, u32[]{:S(2)}, u32[]{:S(2)}) collective-permute-start(bf16[8,32,128]{2,1,0:T(8,128)(2,1)S(1)} %collective-permute-done.6.refs_2_), channel_id=1, source_target_pairs={{0,224},{2,226},{4,228},{6,230},{8,232},{10,234},{12,236},{14,238}... | collective-permute-start | bytes 196616 | tf_op jit(solution)/shard_map/ppermute | solution.py:271
  42.5 2.9 %collective-permute-done.10.refs_6_ = bf16[8,32,128]{2,1,0:T(8,128)(2,1)S(1)} collective-permute-done((bf16[8,32,128]{2,1,0:T(8,128)(2,1)S(1)}, bf16[8,32,128]{2,1,0:T(8,128)(2,1)S(1)}, u32[]{:S(2)}, u32[]{:S(2)}) %collective-permute-start.10) | collective-permute-done | bytes 65568 | tf_op jit(solution)/shard_map/ppermute | solution.py:273
  45.4 2.7 %collective-permute-start.8 = (bf16[8,32,128]{2,1,0:T(8,128)(2,1)S(1)}, bf16[8,32,128]{2,1,0:T(8,128)(2,1)S(1)}, u32[]{:S(2)}, u32[]{:S(2)}) collective-permute-start(bf16[8,32,128]{2,1,0:T(8,128)(2,1)S(1)} %collective-permute-done.7.refs_3_), channel_id=1, source_target_pairs={{0,224},{2,226},{4,228},{6,230},{8,232},{10,234},{12,236},{14,238}... | collective-permute-start | bytes 196616 | tf_op jit(solution)/shard_map/ppermute | solution.py:271
  48.1 1.8 %collective-permute-done.11.refs_5_ = bf16[8,32,128]{2,1,0:T(8,128)(2,1)S(1)} collective-permute-done((bf16[8,32,128]{2,1,0:T(8,128)(2,1)S(1)}, bf16[8,32,128]{2,1,0:T(8,128)(2,1)S(1)}, u32[]{:S(2)}, u32[]{:S(2)}) %collective-permute-start.11) | collective-permute-done | bytes 65568 | tf_op jit(solution)/shard_map/ppermute | solution.py:273
  49.9 3.2 %select.1 = bf16[16,16,32,128]{3,2,1,0:T(8,128)(2,1)} custom-call(s32[2]{0:T(128)S(1)} %pad_add_fusion.place, s32[32,128]{1,0:T(8,128)S(1)} %convert.1.wanted, bf16[8,32,128]{2,1,0:T(8,128)(2,1)S(1)} %get-tuple-element.12.refs_0_, bf16[8,32,128]{2,1,0:T(8,128)(2,1)S(1)} %collective-permute-done.5.refs_1_, ...), custom_call_target="tpu_custom_call" | custom-call | tf_op jit(solution)/shard_map/select/pallas_call | solution.py:110
  53.1 8.9 %all-to-all-start = ((bf16[16,16,32,128]{3,2,1,0:T(8,128)(2,1)}), bf16[16,16,32,128]{3,2,1,0:T(8,128)(2,1)S(1)}, u32[]{:S(2)}, u32[]{:S(2)}) async-start(bf16[16,16,32,128]{3,2,1,0:T(8,128)(2,1)} %select.1), calls=%async_computation | async-start | bytes 4194304 | tf_op jit(solution)/shard_map/all_to_all | solution.py:299
  62.0 0.0 copy-start.10
  62.0 3.3 %collective-permute-start.13 = (bf16[64,2048]{1,0:T(8,128)(2,1)S(1)}, bf16[64,2048]{1,0:T(8,128)(2,1)S(1)}, u32[]{:S(2)}, u32[]{:S(2)}) collective-permute-start(bf16[64,2048]{1,0:T(8,128)(2,1)S(1)} %copy-done.5), channel_id=1, source_target_pairs={{0,1},{1,0},{2,3},{3,2},{4,5},{5,4},{6,7},{7,6},{8,9},{9,8},{10,11... | collective-permute-start | bytes 786440 | tf_op jit(solution)/shard_map/ppermute | solution.py:266
  65.4 0.0 all-gather.2.cloned.1.call-done
  65.4 3.5 %collective-permute-start.12 = (bf16[4096,128]{1,0:T(8,128)(2,1)}, bf16[4096,128]{1,0:T(8,128)(2,1)}, u32[]{:S(2)}, u32[]{:S(2)}) collective-permute-start(bf16[4096,128]{1,0:T(8,128)(2,1)} %all-gather.2.cloned.1.call-done), channel_id=1, source_target_pairs={{0,2},{2,0},{4,6},{6,4},{8,10},{10,8},{12,14},{14,12},{16,18},{18,... | collective-permute-start | bytes 3145736 | tf_op jit(solution)/shard_map/ppermute | solution.py:286
  68.9 26.9 %collective-permute-done.13 = bf16[64,2048]{1,0:T(8,128)(2,1)S(1)} collective-permute-done((bf16[64,2048]{1,0:T(8,128)(2,1)S(1)}, bf16[64,2048]{1,0:T(8,128)(2,1)S(1)}, u32[]{:S(2)}, u32[]{:S(2)}) %collective-permute-start.13) | collective-permute-done | bytes 262176 | tf_op jit(solution)/shard_map/ppermute | solution.py:266
  95.9 1.3 collective-permute-start.14
  97.2 6.1 %collective-permute-done.14.before = bf16[128,1024]{1,0:T(8,128)(2,1)S(1)} collective-permute-done((bf16[128,1024]{1,0:T(8,128)(2,1)S(1)}, bf16[128,1024]{1,0:T(8,128)(2,1)S(1)}, u32[]{:S(2)}, u32[]{:S(2)}) %collective-permute-start.14) | collective-permute-done | bytes 262176 | tf_op jit(solution)/shard_map/ppermute | solution.py:293
  103.3 1.5 %collective-permute-done.15.after = bf16[128,1024]{1,0:T(8,128)(2,1)S(1)} collective-permute-done((bf16[128,1024]{1,0:T(8,128)(2,1)S(1)}, bf16[128,1024]{1,0:T(8,128)(2,1)S(1)}, u32[]{:S(2)}, u32[]{:S(2)}) %collective-permute-start.15) | collective-permute-done | bytes 262176 | tf_op jit(solution)/shard_map/ppermute | solution.py:294
  104.8 2.2 %copy-done = bf16[8,4,256,256]{3,2,1,0:T(8,128)(2,1)S(1)} copy-done((bf16[8,4,256,256]{3,2,1,0:T(8,128)(2,1)S(1)}, bf16[8,4,256,256]{3,2,1,0:T(8,128)(2,1)}, u32[]{:S(2)}) %copy-start) | copy-done | bytes 4194328
  107.0 4.7 %near_field.1 = (f32[64,2048]{1,0:T(8,128)S(1)}, bf16[64,2048]{1,0:T(8,128)(2,1)}) custom-call(s32[2]{0:T(128)S(1)} %pad_add_fusion.place, s32[8,8]{1,0:T(8,128)S(1)} %copy-done.10, bf16[128,2048]{1,0:T(8,128)(2,1)S(1)} %constant_dynamic-update-slice_fusion.both, bf16[128,1024]{1,0:T(8,128)(2,1)S(1)} %collective-permute-done.14.before, ...), custom_call_target="tpu_custom_call" | custom-call | flops 600000000 | bytes 6000000 | tf_op jit(solution)/shard_map/near_field/pallas_call | solution.py:149
  111.7 0.5 broadcast.3
  112.2 0.7 reduce.3
  112.9 0.1 reshape.26.slots
  113.0 6.2 %collective-permute-done.16.near_in = bf16[64,2048]{1,0:T(8,128)(2,1)S(1)} collective-permute-done((bf16[64,2048]{1,0:T(8,128)(2,1)}, bf16[64,2048]{1,0:T(8,128)(2,1)S(1)}, u32[]{:S(2)}, u32[]{:S(2)}) %collective-permute-start.16) | collective-permute-done | bytes 262176 | tf_op jit(solution)/shard_map/ppermute | solution.py:296
  119.2 0.0 copy-start.1
  119.2 1.4 %copy-done.1 = bf16[8,64,1536]{2,1,0:T(8,128)(2,1)S(1)} copy-done((bf16[8,64,1536]{2,1,0:T(8,128)(2,1)S(1)}, bf16[8,64,1536]{2,1,0:T(8,128)(2,1)}, u32[]{:S(2)}) %copy-start.1) | copy-done | bytes 1572888
  120.6 1.2 copy-done.6
  121.8 0.9 copy-done.9
  122.8 0.7 copy-done.13
  123.5 7.3 %downward.1 = bf16[64,2048]{1,0:T(8,128)(2,1)} custom-call(s32[2]{0:T(128)S(1)} %pad_add_fusion.place, s32[8]{0:T(128)S(1)} %copy-done.12, s32[8,24]{1,0:T(8,128)S(1)} %reshape.26.slots, s32[2,16]{1,0:T(2,128)S(1)} %copy-done.13, bf16[256,32,128]{2,1,0:T(8,128)(2,1)S(1)} %bitcast.18, bf16[128,32,128]{2,1,0:T(8,128)(2,1)S(1)} %bitcast.19, ...), custom_call_target="tpu_custom_call" | custom-call | tf_op jit(solution)/shard_map/downward/pallas_call | solution.py:226
  (38 shorter events, 0.2 us)
Async XLA Ops:
  6.5 58.8 %all-gather.2.cloned.1.call-start = ((), (), s32[]{:S(2)}) async-start(), calls=%async_computation.1 | async-start | bytes 1179648 | tf_op jit(solution)/shard_map/all_gather | solution.py:283
  8.2 1.0 copy-start.2
  9.1 0.9 copy-start.4
  10.1 0.9 copy-start.7
  11.0 0.7 copy-start.11
  13.1 3.3 %collective-permute-start = (bf16[80,128]{1,0:T(8,128)(2,1)S(1)}, bf16[80,128]{1,0:T(8,128)(2,1)S(1)}, u32[]{:S(2)}, u32[]{:S(2)}) collective-permute-start(bf16[80,128]{1,0:T(8,128)(2,1)S(1)} %get-tuple-element.11), channel_id=1, source_target_pairs={{0,4},{2,6},{4,0},{6,2},{8,12},{10,14},{12,8},{14,10},{16,20},{18,... | collective-permute-start | bytes 61448 | tf_op jit(solution)/shard_map/ppermute | solution.py:275
  16.4 4.2 %collective-permute-start.1 = (bf16[2,80,128]{2,1,0:T(8,128)(2,1)S(1)}, bf16[2,80,128]{2,1,0:T(8,128)(2,1)S(1)}, u32[]{:S(2)}, u32[]{:S(2)}) collective-permute-start(bf16[2,80,128]{2,1,0:T(8,128)(2,1)S(1)} %get-tuple-element.18), channel_id=1, source_target_pairs={{0,24},{2,26},{4,28},{6,30},{8,0},{10,2},{12,4},{14,6},{16,8},{18,... | collective-permute-start | bytes 122888 | tf_op jit(solution)/shard_map/ppermute | solution.py:277
  19.5 4.4 %collective-permute-start.2 = (bf16[2,80,128]{2,1,0:T(8,128)(2,1)S(1)}, bf16[2,80,128]{2,1,0:T(8,128)(2,1)S(1)}, u32[]{:S(2)}, u32[]{:S(2)}) collective-permute-start(bf16[2,80,128]{2,1,0:T(8,128)(2,1)S(1)} %get-tuple-element.18), channel_id=1, source_target_pairs={{0,16},{2,18},{4,20},{6,22},{8,24},{10,26},{12,28},{14,30},{16,0},... | collective-permute-start | bytes 122888 | tf_op jit(solution)/shard_map/ppermute | solution.py:277
  19.8 4.4 %collective-permute-start.3 = (bf16[2,80,128]{2,1,0:T(8,128)(2,1)S(1)}, bf16[2,80,128]{2,1,0:T(8,128)(2,1)S(1)}, u32[]{:S(2)}, u32[]{:S(2)}) collective-permute-start(bf16[2,80,128]{2,1,0:T(8,128)(2,1)S(1)} %get-tuple-element.18), channel_id=1, source_target_pairs={{0,8},{2,10},{4,12},{6,14},{8,16},{10,18},{12,20},{14,22},{16,24},... | collective-permute-start | bytes 122888 | tf_op jit(solution)/shard_map/ppermute | solution.py:277
  25.0 7.0 %collective-permute-start.5 = (bf16[8,32,128]{2,1,0:T(8,128)(2,1)S(1)}, bf16[8,32,128]{2,1,0:T(8,128)(2,1)S(1)}, u32[]{:S(2)}, u32[]{:S(2)}) collective-permute-start(bf16[8,32,128]{2,1,0:T(8,128)(2,1)S(1)} %get-tuple-element.12.refs_0_), channel_id=1, source_target_pairs={{0,224},{2,226},{4,228},{6,230},{8,232},{10,234},{12,236},{14,238}... | collective-permute-start | bytes 196616 | tf_op jit(solution)/shard_map/ppermute | solution.py:271
  30.6 9.2 %collective-permute-start.9 = (bf16[8,32,128]{2,1,0:T(8,128)(2,1)S(1)}, bf16[8,32,128]{2,1,0:T(8,128)(2,1)S(1)}, u32[]{:S(2)}, u32[]{:S(2)}) collective-permute-start(bf16[8,32,128]{2,1,0:T(8,128)(2,1)S(1)} %get-tuple-element.12.refs_0_), channel_id=1, source_target_pairs={{0,32},{2,34},{4,36},{6,38},{8,40},{10,42},{12,44},{14,46},{16,48}... | collective-permute-start | bytes 196616 | tf_op jit(solution)/shard_map/ppermute | solution.py:273
  32.0 7.8 %collective-permute-start.6 = (bf16[8,32,128]{2,1,0:T(8,128)(2,1)S(1)}, bf16[8,32,128]{2,1,0:T(8,128)(2,1)S(1)}, u32[]{:S(2)}, u32[]{:S(2)}) collective-permute-start(bf16[8,32,128]{2,1,0:T(8,128)(2,1)S(1)} %collective-permute-done.5.refs_1_), channel_id=1, source_target_pairs={{0,224},{2,226},{4,228},{6,230},{8,232},{10,234},{12,236},{14,238}... | collective-permute-start | bytes 196616 | tf_op jit(solution)/shard_map/ppermute | solution.py:271
  35.0 13.1 %collective-permute-start.4 = (bf16[4,2,16,128]{3,2,1,0:T(8,128)(2,1)S(1)}, bf16[4,2,16,128]{3,2,1,0:T(8,128)(2,1)S(1)}, u32[]{:S(2)}, u32[]{:S(2)}) collective-permute-start(bf16[4,2,16,128]{3,2,1,0:T(8,128)(2,1)S(1)} %pad_maximum_fusion.4), channel_id=1, source_target_pairs={{0,2},{2,0},{4,6},{6,4},{8,10},{10,8},{12,14},{14,12},{16,18},{18,... | collective-permute-start | bytes 98312 | tf_op jit(solution)/shard_map/ppermute | solution.py:281
  39.8 5.6 %collective-permute-start.10 = (bf16[8,32,128]{2,1,0:T(8,128)(2,1)S(1)}, bf16[8,32,128]{2,1,0:T(8,128)(2,1)S(1)}, u32[]{:S(2)}, u32[]{:S(2)}) collective-permute-start(bf16[8,32,128]{2,1,0:T(8,128)(2,1)S(1)} %collective-permute-done.9.refs_7_), channel_id=1, source_target_pairs={{0,32},{2,34},{4,36},{6,38},{8,40},{10,42},{12,44},{14,46},{16,48}... | collective-permute-start | bytes 196616 | tf_op jit(solution)/shard_map/ppermute | solution.py:273
  39.8 5.6 %collective-permute-start.7 = (bf16[8,32,128]{2,1,0:T(8,128)(2,1)S(1)}, bf16[8,32,128]{2,1,0:T(8,128)(2,1)S(1)}, u32[]{:S(2)}, u32[]{:S(2)}) collective-permute-start(bf16[8,32,128]{2,1,0:T(8,128)(2,1)S(1)} %collective-permute-done.6.refs_2_), channel_id=1, source_target_pairs={{0,224},{2,226},{4,228},{6,230},{8,232},{10,234},{12,236},{14,238}... | collective-permute-start | bytes 196616 | tf_op jit(solution)/shard_map/ppermute | solution.py:271
  45.4 4.5 %collective-permute-start.11 = (bf16[8,32,128]{2,1,0:T(8,128)(2,1)S(1)}, bf16[8,32,128]{2,1,0:T(8,128)(2,1)S(1)}, u32[]{:S(2)}, u32[]{:S(2)}) collective-permute-start(bf16[8,32,128]{2,1,0:T(8,128)(2,1)S(1)} %collective-permute-done.10.refs_6_), channel_id=1, source_target_pairs={{0,32},{2,34},{4,36},{6,38},{8,40},{10,42},{12,44},{14,46},{16,48}... | collective-permute-start | bytes 196616 | tf_op jit(solution)/shard_map/ppermute | solution.py:273
  45.4 4.5 %collective-permute-start.8 = (bf16[8,32,128]{2,1,0:T(8,128)(2,1)S(1)}, bf16[8,32,128]{2,1,0:T(8,128)(2,1)S(1)}, u32[]{:S(2)}, u32[]{:S(2)}) collective-permute-start(bf16[8,32,128]{2,1,0:T(8,128)(2,1)S(1)} %collective-permute-done.7.refs_3_), channel_id=1, source_target_pairs={{0,224},{2,226},{4,228},{6,230},{8,232},{10,234},{12,236},{14,238}... | collective-permute-start | bytes 196616 | tf_op jit(solution)/shard_map/ppermute | solution.py:271
  53.1 8.9 %copy-start.5 = (bf16[64,2048]{1,0:T(8,128)(2,1)S(1)}, bf16[64,2048]{1,0:T(8,128)(2,1)}, u32[]{:S(2)}) copy-start(bf16[64,2048]{1,0:T(8,128)(2,1)} %signals.1) | copy-start | bytes 786436
  53.1 66.0 %all-to-all-start = ((bf16[16,16,32,128]{3,2,1,0:T(8,128)(2,1)}), bf16[16,16,32,128]{3,2,1,0:T(8,128)(2,1)S(1)}, u32[]{:S(2)}, u32[]{:S(2)}) async-start(bf16[16,16,32,128]{3,2,1,0:T(8,128)(2,1)} %select.1), calls=%async_computation | async-start | bytes 4194304 | tf_op jit(solution)/shard_map/all_to_all | solution.py:299
  62.0 42.8 %copy-start.10 = (s32[8,8]{1,0:T(8,128)S(1)}, s32[8,8]{1,0:T(8,128)}, u32[]{:S(2)}) copy-start(s32[8,8]{1,0:T(8,128)} %near_list.1) | copy-start | bytes 772
  62.0 33.8 %collective-permute-start.13 = (bf16[64,2048]{1,0:T(8,128)(2,1)S(1)}, bf16[64,2048]{1,0:T(8,128)(2,1)S(1)}, u32[]{:S(2)}, u32[]{:S(2)}) collective-permute-start(bf16[64,2048]{1,0:T(8,128)(2,1)S(1)} %copy-done.5), channel_id=1, source_target_pairs={{0,1},{1,0},{2,3},{3,2},{4,5},{5,4},{6,7},{7,6},{8,9},{9,8},{10,11... | collective-permute-start | bytes 786440 | tf_op jit(solution)/shard_map/ppermute | solution.py:266
  65.4 53.8 %collective-permute-start.12 = (bf16[4096,128]{1,0:T(8,128)(2,1)}, bf16[4096,128]{1,0:T(8,128)(2,1)}, u32[]{:S(2)}, u32[]{:S(2)}) collective-permute-start(bf16[4096,128]{1,0:T(8,128)(2,1)} %all-gather.2.cloned.1.call-done), channel_id=1, source_target_pairs={{0,2},{2,0},{4,6},{6,4},{8,10},{10,8},{12,14},{14,12},{16,18},{18,... | collective-permute-start | bytes 3145736 | tf_op jit(solution)/shard_map/ppermute | solution.py:286
  95.9 7.4 %collective-permute-start.14 = (bf16[128,1024]{1,0:T(8,128)(2,1)S(1)}, bf16[128,1024]{1,0:T(8,128)(2,1)S(1)}, u32[]{:S(2)}, u32[]{:S(2)}) collective-permute-start(bf16[128,1024]{1,0:T(8,128)(2,1)S(1)} %get-tuple-element.16), channel_id=1, source_target_pairs={{0,2},{2,4},{4,6},{6,8},{8,10},{10,12},{12,14},{14,16},{16,18},{18... | collective-permute-start | bytes 786440 | tf_op jit(solution)/shard_map/ppermute | solution.py:293
  97.2 22.0 %copy-start.12 = (s32[8]{0:T(128)S(1)}, s32[8]{0:T(128)}, u32[]{:S(2)}) copy-start(s32[8]{0:T(128)} %parent.3) | copy-start | bytes 100
  97.2 7.6 %collective-permute-start.15 = (bf16[128,1024]{1,0:T(8,128)(2,1)S(1)}, bf16[128,1024]{1,0:T(8,128)(2,1)S(1)}, u32[]{:S(2)}, u32[]{:S(2)}) collective-permute-start(bf16[128,1024]{1,0:T(8,128)(2,1)S(1)} %get-tuple-element.15), channel_id=1, source_target_pairs={{2,0},{4,2},{6,4},{8,6},{10,8},{12,10},{14,12},{16,14},{18,16},{20... | collective-permute-start | bytes 786440 | tf_op jit(solution)/shard_map/ppermute | solution.py:294
  104.8 2.2 %copy-start = (bf16[8,4,256,256]{3,2,1,0:T(8,128)(2,1)S(1)}, bf16[8,4,256,256]{3,2,1,0:T(8,128)(2,1)}, u32[]{:S(2)}) copy-start(bf16[8,4,256,256]{3,2,1,0:T(8,128)(2,1)} %tiles.1) | copy-start | bytes 12582916
  107.0 12.2 %copy-start.3 = (bf16[8,64,256]{2,1,0:T(8,128)(2,1)S(1)}, bf16[8,64,256]{2,1,0:T(8,128)(2,1)}, u32[]{:S(2)}) copy-start(bf16[8,64,256]{2,1,0:T(8,128)(2,1)} %basis.3) | copy-start | bytes 786436
  107.0 12.2 %copy-start.8 = (bf16[8,64,64]{2,1,0:T(8,128)(2,1)S(1)}, bf16[8,64,64]{2,1,0:T(8,128)(2,1)}, u32[]{:S(2)}) copy-start(bf16[8,64,64]{2,1,0:T(8,128)(2,1)} %transfer.3) | copy-start | bytes 196612
  111.7 7.5 %collective-permute-start.16 = (bf16[64,2048]{1,0:T(8,128)(2,1)}, bf16[64,2048]{1,0:T(8,128)(2,1)S(1)}, u32[]{:S(2)}, u32[]{:S(2)}) collective-permute-start(bf16[64,2048]{1,0:T(8,128)(2,1)} %get-tuple-element.14), channel_id=1, source_target_pairs={{0,1},{1,0},{2,3},{3,2},{4,5},{5,4},{6,7},{7,6},{8,9},{9,8},{10,11... | collective-permute-start | bytes 786440 | tf_op jit(solution)/shard_map/ppermute | solution.py:296
  119.2 1.4 %copy-start.1 = (bf16[8,64,1536]{2,1,0:T(8,128)(2,1)S(1)}, bf16[8,64,1536]{2,1,0:T(8,128)(2,1)}, u32[]{:S(2)}) copy-start(bf16[8,64,1536]{2,1,0:T(8,128)(2,1)} %coupling.1) | copy-start | bytes 4718596
  120.6 1.2 copy-start.6
  121.8 0.9 copy-start.9
  122.8 0.7 copy-start.13
Sparse Core Ops, SparseCore 0:
  25.1 38.7 all-gather.1

commit v2 on v0

v2 whole, which is shorter than its diff:
```python
import functools

import jax
import jax.numpy as jnp
from jax import lax
from jax.experimental import pallas as pl
from jax.experimental.pallas import tpu as pltpu
from jax.sharding import PartitionSpec as P

Z, Y, X, C = 8, 4, 2, 2
PLANE = Y * X * C
MIB = 1 << 20
NT = (((1,), (1,)), ((), ()))
TN = (((0,), (0,)), ((), ()))
NN = (((1,), (0,)), ((), ()))


def loop_moves(target):
    moves = []
    for d in range(Z * PLANE):
        z, y, x, c = d // PLANE, d // (X * C) % Y, d // C % X, d % C
        z, y, x, c = target(z, y, x, c)
        moves.append((d, ((z % Z * Y + y % Y) * X + x) * C + c))
    return moves


def dot(a, b, dims):
    return lax.dot_general(a, b, dims, preferred_element_type=jnp.float32)


def pack(block):
    half = block.shape[0] // 2
    return jnp.concatenate([block[:half], block[half:]], axis=1)


def unpack(block):
    half = block.shape[1] // 2
    return [block, jnp.concatenate([block[:, half:], block[:, :half]], axis=1)]


def load(copies, sems):
    pending = [
        pltpu.make_async_copy(source, target, sems.at[i]) for i, (source, target) in enumerate(copies)
    ]
    for copy in pending:
        copy.start()
    return pending


SMEM_SPEC = pl.BlockSpec(memory_space=pltpu.SMEM)
VMEM_SPEC = pl.BlockSpec(memory_space=pltpu.VMEM)
ANY_SPEC = pl.BlockSpec(memory_space=pl.ANY)


def cost(flops, moved):
    return pl.CostEstimate(flops=flops, bytes_accessed=moved, transcendentals=0)


def tables_kernel(lists, own_row, wanted_out, slot_out):
    own = lax.axis_index("loop") % PLANE
    count = 2 * lists.shape[2]
    devices = jnp.concatenate([lists[0], lists[1]], axis=1)
    members = jnp.concatenate([lists[2], lists[3]], axis=1)
    flat = lax.broadcasted_iota(jnp.int32, devices.shape, 1)
    lane = lax.broadcasted_iota(jnp.int32, wanted_out.shape, 1)
    table = jnp.zeros(wanted_out.shape, jnp.int32)
    for z in range(Z):
        place = jnp.where(devices == z * PLANE + own, flat, count)
        lowest = jnp.min(place, axis=1, keepdims=True)
        place_two = jnp.where(place > lowest, place, count)
        second = jnp.min(place_two, axis=1, keepdims=True)
        for k, at in enumerate((lowest, second)):
            member = jnp.sum(jnp.where(flat == at, members, 0), axis=1, keepdims=True)
            table = jnp.where(lane == z * 2 + k, member, table)
    wanted_out[...] = table
    row = own_row[...]
    size = row.shape[1]
    at_col = lax.broadcasted_iota(jnp.int32, (size, size), 0)
    at_row = lax.broadcasted_iota(jnp.int32, (size, size), 1)
    column = jnp.sum(jnp.where(at_col == at_row, row, 0), axis=1, keepdims=True)
    earlier = jnp.where((column == row) & (at_col < at_row), 1, 0)
    seen = jnp.sum(earlier, axis=0, keepdims=True)
    slot_out[...] = row % PLANE * (2 * Z) + row // PLANE * 2 + seen


def tables(lists, own_row):
    return pl.pallas_call(
        tables_kernel,
        out_shape=(
            jax.ShapeDtypeStruct((PLANE, 128), jnp.int32),
            jax.ShapeDtypeStruct(own_row.shape, jnp.int32),
        ),
        in_specs=[VMEM_SPEC] * 2,
        out_specs=(VMEM_SPEC, VMEM_SPEC),
        compiler_params=pltpu.CompilerParams(vmem_limit_bytes=8 * MIB),
        cost_estimate=cost(2_000_000, 20_000),
        name="tables",
    )(lists, own_row)


def upward_kernel(
    parent, far_list, signals_in, basis_in, transfer_in, coef_out, pay_out, row_out, signals, basis, transfer, sems
):
    pending = load([(signals_in, signals), (basis_in, basis), (transfer_in, transfer)], sems)
    ids = far_list[...]
    row = jnp.concatenate([ids[t : t + 1] for t in range(ids.shape[0])], axis=1)
    row = jnp.concatenate([row, jnp.full((1, 256 - row.shape[1]), -8, jnp.int32)], axis=1)
    devices, members = row // ids.shape[0], row % ids.shape[0]
    row_out[...] = devices
    lists = [devices[:, :128], devices[:, 128:], members[:, :128], members[:, 128:], jnp.zeros((12, 128), jnp.int32)]
    pay_out[64:80] = jnp.concatenate(lists, axis=0).astype(jnp.float32).astype(jnp.bfloat16)
    for copy in pending:
        copy.wait()
    leaf_count, rank, leaf_size = basis.shape
    sums = [jnp.zeros((rank, signals.shape[0]), jnp.float32) for _ in range(2)]
    for c in range(leaf_count):
        block = signals[:, c * leaf_size : (c + 1) * leaf_size]
        coefs = dot(basis[c], block, NT).astype(jnp.bfloat16)
        packed = pack(coefs)
        for z in range(Z):
            coef_out[z, c] = packed
        lifted = dot(transfer[c], coefs, TN)
        member = parent[c] - lax.axis_index("loop") * 2
        sums = [s + jnp.where(member == i, lifted, 0.0) for i, s in enumerate(sums)]
    for i, s in enumerate(sums):
        pay_out[i * 32 : (i + 1) * 32] = pack(s.astype(jnp.bfloat16))


def upward(parent, far_list, signals, basis, transfer):
    leaf_count = basis.shape[0]
    return pl.pallas_call(
        upward_kernel,
        out_shape=(
            jax.ShapeDtypeStruct((Z, leaf_count, 32, 128), jnp.bfloat16),
            jax.ShapeDtypeStruct((80, 128), jnp.bfloat16),
            jax.ShapeDtypeStruct((1, 256), jnp.int32),
        ),
        in_specs=[SMEM_SPEC, VMEM_SPEC, ANY_SPEC, ANY_SPEC, ANY_SPEC],
        out_specs=(VMEM_SPEC,) * 3,
        scratch_shapes=[
            pltpu.VMEM(signals.shape, jnp.bfloat16),
            pltpu.VMEM(basis.shape, jnp.bfloat16),
            pltpu.VMEM(transfer.shape, jnp.bfloat16),
            pltpu.SemaphoreType.DMA((3,)),
        ],
        compiler_params=pltpu.CompilerParams(vmem_limit_bytes=56 * MIB),
        cost_estimate=cost(30_000_000, 700_000),
        name="upward",
    )(parent, far_list, signals, basis, transfer)


def select_kernel(wanted, planes, send):
    step = pl.program_id(0)
    own = lax.axis_index("loop") % PLANE
    for i in range(send.shape[0]):
        peer = step * send.shape[0] + i
        dy = jnp.bitwise_and(peer // (X * C) - own // (X * C) + Y, Y - 1)
        row = dy * (X * C) + jnp.bitwise_and(jnp.bitwise_xor(peer, own), X * C - 1)
        for slot in range(2 * Z):
            send[i, slot] = planes[slot // 2, wanted[row, slot]]


def select(wanted, planes):
    per_step = 4
    return pl.pallas_call(
        select_kernel,
        grid=(PLANE // per_step,),
        out_shape=jax.ShapeDtypeStruct((PLANE, 2 * Z, 32, 128), jnp.bfloat16),
        in_specs=[SMEM_SPEC, VMEM_SPEC],
        out_specs=pl.BlockSpec((per_step, 2 * Z, 32, 128), lambda s: (s, 0, 0, 0)),
        compiler_params=pltpu.CompilerParams(vmem_limit_bytes=8 * MIB),
        cost_estimate=cost(1_000_000, 2_500_000),
        name="select",
    )(wanted, planes)


def near_kernel(near_list, signals, other, before, after, tiles, own_out, other_out, extended, sems):
    half, width = signals.shape
    reach = before.shape[1]
    leaf_count, near_count, leaf_size, _ = tiles.shape
    pending = load(
        [
            (before, extended.at[:, :reach]),
            (signals, extended.at[:half, reach : reach + width]),
            (other, extended.at[half:, reach : reach + width]),
            (after, extended.at[:, reach + width :]),
        ],
        sems,
    )
    for copy in pending:
        copy.wait()
    loop, rhs = lax.axis_index("loop"), lax.axis_index("rhs")
    leaves = leaf_count * Z * PLANE
    for t in range(leaf_count):
        total = jnp.zeros((2 * half, leaf_size), jnp.float32)
        for j in range(near_count):
            source = near_list[t, rhs * near_count + j]
            at = (source - loop * leaf_count + leaf_count // 2 + leaves) % leaves
            block = extended[:, pl.ds(pl.multiple_of(at * leaf_size, leaf_size), leaf_size)]
            total = total + dot(block, tiles[t, j], NT)
        own_out[:, t * leaf_size : (t + 1) * leaf_size] = total[:half]
        other_out[:, t * leaf_size : (t + 1) * leaf_size] = total[half:].astype(jnp.bfloat16)


def near_field(near_list, signals, other, before, after, tiles):
    half, width = signals.shape
    return pl.pallas_call(
        near_kernel,
        out_shape=(
            jax.ShapeDtypeStruct((half, width), jnp.float32),
            jax.ShapeDtypeStruct((half, width), jnp.bfloat16),
        ),
        in_specs=[SMEM_SPEC, ANY_SPEC, ANY_SPEC, ANY_SPEC, ANY_SPEC, VMEM_SPEC],
        out_specs=(VMEM_SPEC, VMEM_SPEC),
        scratch_shapes=[
            pltpu.VMEM((2 * half, 2 * width), jnp.bfloat16),
            pltpu.SemaphoreType.DMA((4,)),
        ],
        compiler_params=pltpu.CompilerParams(vmem_limit_bytes=12 * MIB),
        cost_estimate=cost(600_000_000, 10_000_000),
        name="near_field",
    )(near_list, signals, other, before, after, tiles)


def fields_kernel(parent, parent_far, *refs):
    sources = refs[:9]
    coupling_in, transfer_in, out, parents, coupling, transfer, sems = refs[9:]
    copies = [(coupling_in, coupling), (transfer_in, transfer)]
    at = 0
    for ref in sources:
        copies.append((ref, parents.at[at : at + ref.shape[0]]))
        at += ref.shape[0]
    pending = load(copies, sems)
    for copy in pending:
        copy.wait()
    me = lax.axis_index("loop")
    own_plane = me % PLANE
    per = 2 * Y * X
    columns = out.shape[2]
    results = []
    for p in range(parent_far.shape[0]):
        stacked = []
        for j in range(parent_far.shape[1]):
            source = parent_far[p, j]
            device = source // 2
            hop = jnp.bitwise_and(device // PLANE - me // PLANE + Z, Z - 1)
            dy = jnp.bitwise_and(device // (X * C) - own_plane // (X * C) + Y, Y - 1)
            cross = jnp.bitwise_xor(device, own_plane)
            dx = jnp.bitwise_and(cross // C, X - 1)
            member = (dy * X + dx) * 2 + jnp.bitwise_and(source, 1)
            base = jnp.int32(0)
            for place, h in enumerate((0, 1, 7, 2, 3, 6, 5, 4)):
                base = jnp.where(hop == h, place * per, base)
            where = jnp.bitwise_and(cross, C - 1) * (Z * per) + base + member
            stacked += unpack(parents[where])
        field = dot(coupling[p], jnp.concatenate(stacked, axis=0), NN)
        results.append(field[:, :columns].astype(jnp.bfloat16))
    for c in range(transfer.shape[0]):
        field = jnp.where(parent[c] == me * 2, results[0], results[1])
        out[c] = dot(transfer[c], field, NN)


def fields(parent, parent_far, pieces, parent_coupling, transfer):
    return pl.pallas_call(
        fields_kernel,
        out_shape=jax.ShapeDtypeStruct(transfer.shape, jnp.float32),
        in_specs=[SMEM_SPEC] * 2 + [ANY_SPEC] * 11,
        out_specs=VMEM_SPEC,
        scratch_shapes=[
            pltpu.VMEM((2 * Z * Y * X * 2, 32, 128), jnp.bfloat16),
            pltpu.VMEM(parent_coupling.shape, jnp.bfloat16),
            pltpu.VMEM(transfer.shape, jnp.bfloat16),
            pltpu.SemaphoreType.DMA((11,)),
        ],
        compiler_params=pltpu.CompilerParams(vmem_limit_bytes=16 * MIB),
        cost_estimate=cost(50_000_000, 4_000_000),
        name="fields",
    )(parent, parent_far, *pieces, parent_coupling, transfer)


def downward_kernel(
    slots,
    blocks,
    coupling_in,
    descended_in,
    basis_in,
    near_own_in,
    near_in_in,
    out,
    coupling,
    descended,
    basis,
    near_own,
    near_in,
    sems,
):
    leaf_count, rank, leaf_size = basis.shape
    pending = load(
        [(coupling_in.at[c], coupling.at[c]) for c in range(leaf_count)]
        + [(descended_in, descended), (basis_in, basis), (near_own_in, near_own), (near_in_in, near_in)],
        sems,
    )
    sources = coupling.shape[2] // rank
    columns = out.shape[0]
    for c in range(leaf_count):
        stacked = []
        for j in range(sources):
            stacked += unpack(blocks[slots[0, c * sources + j]])
        pending[c].wait()
        if c == 0:
            for copy in pending[leaf_count:]:
                copy.wait()
        leaf_far = dot(coupling[c], jnp.concatenate(stacked, axis=0), NN)[:, :columns]
        combined = (leaf_far + descended[c]).astype(jnp.bfloat16)
        far_out = dot(combined, basis[c], TN)
        at = slice(c * leaf_size, (c + 1) * leaf_size)
        out[:, at] = (near_own[:, at] + near_in[:, at].astype(jnp.float32) + far_out).astype(jnp.bfloat16)


def downward(slots, blocks, coupling, descended, basis, near_own, near_in):
    arrays = (coupling, descended, basis, near_own, near_in)
    return pl.pallas_call(
        downward_kernel,
        out_shape=jax.ShapeDtypeStruct(near_own.shape, jnp.bfloat16),
        in_specs=[SMEM_SPEC, VMEM_SPEC] + [ANY_SPEC] * 5,
        out_specs=VMEM_SPEC,
        scratch_shapes=[pltpu.VMEM(a.shape, a.dtype) for a in arrays]
        + [pltpu.SemaphoreType.DMA((4 + coupling.shape[0],))],
        compiler_params=pltpu.CompilerParams(vmem_limit_bytes=60 * MIB),
        cost_estimate=cost(150_000_000, 6_000_000),
        name="downward",
    )(slots, blocks, *arrays)


def shards(
    signals,
    near_tiles,
    near_list,
    leaf_basis,
    transfer,
    parent,
    coupling,
    far_list,
    parent_coupling,
    parent_far,
):
    width = signals.shape[1]
    leaf_count = leaf_basis.shape[0]
    along = functools.partial(lax.ppermute, axis_name="loop")
    swap = functools.partial(lax.ppermute, axis_name="rhs", perm=[(0, 1), (1, 0)])
    x_swap = loop_moves(lambda z, y, x, c: (z, y, 1 - x, c))
    c_swap = loop_moves(lambda z, y, x, c: (z, y, x, 1 - c))
    columns_of = [[z * PLANE + p for z in range(Z)] for p in range(PLANE)]
    planes_of = [[z * PLANE + p for p in range(PLANE)] for z in range(Z)]

    other = swap(signals)
    coefs, payload, own_row = upward(parent, far_list, signals, leaf_basis, transfer)

    planes = lax.all_to_all(coefs, "loop", 0, 0, tiled=True, axis_index_groups=columns_of)
    pair = jnp.stack([payload, along(payload, perm=x_swap)])
    quads = jnp.stack(
        [pair]
        + [
            along(pair, perm=loop_moves(lambda z, y, x, c, dy=dy: (z, y - dy, x, c)))
            for dy in range(1, Y)
        ]
    )
    core_lists = quads[:, :, 64:68].reshape(Y * X, 4, 128)
    peer_lists = along(core_lists.reshape(-1, 128), perm=c_swap).reshape(Y * X, 4, 128)
    plane_lists = jnp.stack([core_lists, peer_lists], axis=1).reshape(PLANE, 4, 128).transpose(1, 0, 2)
    parents = quads[:, :, :64].reshape(-1, 32, 128)
    one_down = along(parents, perm=loop_moves(lambda z, y, x, c: (z - 1, y, x, c)))
    one_up = along(parents, perm=loop_moves(lambda z, y, x, c: (z + 1, y, x, c)))

    reach = width // 2
    count = Z * PLANE
    before = along(
        jnp.concatenate([signals[:, reach:], other[:, reach:]]), perm=[(i, (i + 1) % count) for i in range(count)]
    )
    after = along(
        jnp.concatenate([signals[:, :reach], other[:, :reach]]), perm=[((i + 1) % count, i) for i in range(count)]
    )
    plane_lists, before, after, one_down, one_up = lax.optimization_barrier(
        (plane_lists, before, after, one_down, one_up)
    )
    wanted, slots = tables(plane_lists.astype(jnp.int32), own_row)
    blocks = lax.all_to_all(
        select(wanted, planes), "loop", 0, 0, tiled=True, axis_index_groups=planes_of
    )

    far_down = along(jnp.concatenate([parents, one_down]), perm=loop_moves(lambda z, y, x, c: (z - 2, y, x, c)))
    far_up = along(jnp.concatenate([parents, one_up]), perm=loop_moves(lambda z, y, x, c: (z + 2, y, x, c)))
    near_own, near_other = near_field(near_list, signals, other, before, after, near_tiles)
    near_other, far_down, far_up = lax.optimization_barrier((near_other, far_down, far_up))
    near_in = swap(near_other)
    half = parents.shape[0] // 2
    last_down = along(far_down[2 * half : 3 * half], perm=loop_moves(lambda z, y, x, c: (z - 1, y, x, c)))
    last_up = along(far_up[3 * half :], perm=loop_moves(lambda z, y, x, c: (z + 1, y, x, c)))
    mine = [parents, one_down, one_up, far_down, far_up, last_down, last_up]
    theirs = [along(jnp.concatenate(part), perm=c_swap) for part in (mine[:5], mine[5:])]
    descended = fields(parent, parent_far, mine + theirs, parent_coupling, transfer)

    return downward(slots, blocks.reshape(-1, 32, 128), coupling, descended, leaf_basis, near_own, near_in)


def solution(mesh):
    in_specs = (
        P("rhs", "loop"),
        P("loop", "rhs", None, None),
        P("loop", None),
        P("loop", None, None),
        P("loop", None, None),
        P("loop"),
        P("loop", None, None),
        P("loop", None),
        P("loop", None, None),
        P("loop", None),
    )
    out_specs = P("rhs", "loop")
    return jax.shard_map(shards, mesh=mesh, in_specs=in_specs, out_specs=out_specs, check_vma=False)
```

time: 584 us -> 88.4 us (0.15)
  waiting for transfers between devices: 524 us -> 11 us
  starting transfers between devices: 3.67 us -> 50.2 us
  local copies, waits for them, and re-layouts: 27.2 us -> 5.35 us
  Pallas kernels: 0 us -> 19.3 us
  matrix products: 14.6 us -> 0 us
  between operations: 13.3 us -> 0.45 us
    all_gather x3 -> x0, waiting for transfers between devices: 523 us -> none  [the longest x1 215 us: shards(): lax.all_gather(flat_leaf, 'loop', axis=0, tiled=True)]
    ppermute x2 -> x17, starting transfers between devices: 3.59 us -> 35.4 us  [the longest x1 7.52 us: shards(): along(far_up[3 * half:], perm=loop_moves(lambda z, y, x, c: (z + 1, y, x,...]
    pallas_call x0 -> x6, Pallas kernels: none -> 19.3 us  [the longest x1 7.32 us: downward(): pl.pallas_call(downward_kernel, out_shape=jax.ShapeDtypeStruct(near_own.s...]
    gather x5 -> x0, local copies, waits for them, and re-layouts: 16.7 us -> none  [the longest x2 11.9 us: shards(): leaf_picked = jnp.take(every_leaf, leaf_ids, axis=0)]
    all_to_all x0 -> x2, starting transfers between devices: none -> 14.8 us  [the longest x1 8.2 us: shards(): lax.all_to_all(coefs, 'loop', 0, 0, tiled=True, axis_index_groups=columns...]
    dot_general x8 -> x0, matrix products: 14.6 us -> none  [the longest x1 6.02 us: near_product(): jnp.einsum('tjab,rtjb->rta', tile_set, picked, preferred_element_type=jnp...]
    ppermute x2 -> x17, waiting for transfers between devices: 0.21 us -> 11 us  [the longest x1 3.27 us: shards(): along(jnp.concatenate([parents, one_up]), perm=loop_moves(lambda z, y, x,...]
  transfers between devices with their start and end apart: 5 -> 19, of which waited for: 4 -> 8; matrix products, arithmetic and copies ran while one was open for 4% -> 2% of each run, Pallas kernels for 0% -> 11%
where the time goes in v2:
time: 88.4 us; the launch traced here: 87.2 us
  starting transfers between devices  50.2 us (57%)
  Pallas kernels  19.3 us (22%)
  waiting for transfers between devices  11 us (12%)
  local copies, waits for them, and re-layouts  5.35 us (6%)
    all_to_all x1, starting transfers between devices, shards(): lax.all_to_all(coefs, 'loop', 0, 0, tiled=True, axis_index_groups=columns...  8.2 us
    ppermute x1, starting transfers between devices, shards(): along(far_up[3 * half:], perm=loop_moves(lambda z, y, x, c: (z + 1, y, x,...  7.52 us
    pallas_call x1, Pallas kernels, downward(): pl.pallas_call(downward_kernel, out_shape=jax.ShapeDtypeStruct(near_own.s...  7.32 us
    all_to_all x1, starting transfers between devices, shards(): lax.all_to_all(select(wanted, planes), 'loop', 0, 0, tiled=True, axis_ind...  6.59 us
    ppermute x1, starting transfers between devices, shards(): along(core_lists.reshape(-1, 128), perm=c_swap).reshape(Y * X, 4, 128)  5.93 us
    ppermute x3, starting transfers between devices, shards(): along(pair, perm=loop_moves(lambda z, y, x, c, dy=dy: (z, y - dy, x, c)))  4.38 us
    unnamed x28, local copies, waits for them, and re-layouts  4.29 us
    ppermute x1, starting transfers between devices, shards(): other = swap(signals)  3.57 us
  transfers between devices with their start and end apart: 19, of which 8 were waited for; matrix products, arithmetic and copies ran while one was open for 2% of the time, Pallas kernels for 11%

profile of v2, /device:TPU:1, one launch (start us, length us, event | category | flops | bytes accessed | tf_op | source)
XLA Modules:
  0.0 87.2 jit_solution(6428971978732738030)
XLA Ops:
  0.0 3.6 %collective-permute-start.5 = (bf16[64,2048]{1,0:T(8,128)(2,1)}, bf16[64,2048]{1,0:T(8,128)(2,1)S(1)}, u32[]{:S(2)}, u32[]{:S(2)}) collective-permute-start(bf16[64,2048]{1,0:T(8,128)(2,1)} %signals.1), channel_id=1, source_target_pairs={{0,1},{1,0},{2,3},{3,2},{4,5},{5,4},{6,7},{7,6},{8,9},{9,8},{10,11... | collective-permute-start | bytes 786440 | tf_op jit(solution)/shard_map/ppermute | solution.py:356
  3.6 3.4 %upward.1 = (bf16[8,8,32,128]{3,2,1,0:T(8,128)(2,1)}, bf16[80,128]{1,0:T(8,128)(2,1)}, s32[1,256]{1,0:T(1,128)}) custom-call(s32[8]{0:T(128)} %parent.3, s32[8,24]{1,0:T(8,128)} %far_list.1, bf16[64,2048]{1,0:T(8,128)(2,1)} %signals.1, bf16[8,64,256]{2,1,0:T(8,128)(2,1)} %basis_in.3, bf16[8,64,64]{2,1,0:T(8,128)(2,1)} %refs_10_.1), custom_call_target="tpu_custom_call" | custom-call | flops 30000000 | bytes 700000 | tf_op jit(solution)/shard_map/upward/pallas_call | solution.py:131
  7.0 8.2 %all-to-all-start = ((bf16[8,8,32,128]{3,2,1,0:T(8,128)(2,1)}), bf16[8,8,32,128]{3,2,1,0:T(8,128)(2,1)S(1)}, u32[]{:S(2)}, u32[]{:S(2)}) async-start(bf16[8,8,32,128]{3,2,1,0:T(8,128)(2,1)} %get-tuple-element.25), calls=%async_computation | async-start | bytes 1048576 | tf_op jit(solution)/shard_map/all_to_all | solution.py:359
  15.2 0.3 collective-permute-start
  15.5 1.0 %fusion.1 = (bf16[64,1024]{1,0:T(8,128)(2,1)S(1)}, bf16[64,1024]{1,0:T(8,128)(2,1)S(1)}) fusion(bf16[64,2048]{1,0:T(8,128)(2,1)} %signals.1), kind=kLoop, calls=%fused_computation.17 | loop fusion | bytes 524288 | tf_op jit(solution)/shard_map/slice | solution.py:381
  16.5 1.5 %collective-permute-done = bf16[80,128]{1,0:T(8,128)(2,1)S(1)} collective-permute-done((bf16[80,128]{1,0:T(8,128)(2,1)}, bf16[80,128]{1,0:T(8,128)(2,1)S(1)}, u32[]{:S(2)}, u32[]{:S(2)}) %collective-permute-start) | collective-permute-done | bytes 20512 | tf_op jit(solution)/shard_map/ppermute | solution.py:360
  18.1 0.7 fusion
  18.8 2.9 %collective-permute-start.2 = (bf16[2,80,128]{2,1,0:T(8,128)(2,1)S(1)}, bf16[2,80,128]{2,1,0:T(8,128)(2,1)S(1)}, u32[]{:S(2)}, u32[]{:S(2)}) collective-permute-start(bf16[2,80,128]{2,1,0:T(8,128)(2,1)S(1)} %get-tuple-element.42), channel_id=1, source_target_pairs={{0,16},{2,18},{4,20},{6,22},{8,24},{10,26},{12,28},{14,30},{16,0},... | collective-permute-start | bytes 122888 | tf_op jit(solution)/shard_map/ppermute | solution.py:364
  21.7 0.8 collective-permute-start.1
  22.5 0.7 collective-permute-start.3
  23.2 0.0 collective-permute-done.5.other
  23.2 3.5 %collective-permute-start.6 = (bf16[128,1024]{1,0:T(8,128)(2,1)S(1)}, bf16[128,1024]{1,0:T(8,128)(2,1)S(1)}, u32[]{:S(2)}, u32[]{:S(2)}) collective-permute-start(bf16[128,1024]{1,0:T(8,128)(2,1)S(1)} %pad_maximum_fusion.2), channel_id=1, source_target_pairs={{0,2},{2,4},{4,6},{6,8},{8,10},{10,12},{12,14},{14,16},{16,18},{18... | collective-permute-start | bytes 786440 | tf_op jit(solution)/shard_map/ppermute | solution.py:377
  26.8 0.1 collective-permute-start.7
  26.9 0.0 collective-permute-done.2
  26.9 0.0 collective-permute-done.3
  26.9 1.8 %collective-permute-start.9 = (bf16[16,32,128]{2,1,0:T(8,128)(2,1)S(1)}, bf16[16,32,128]{2,1,0:T(8,128)(2,1)S(1)}, u32[]{:S(2)}, u32[]{:S(2)}) collective-permute-start(bf16[16,32,128]{2,1,0:T(8,128)(2,1)S(1)} %bitcast.15), channel_id=1, source_target_pairs={{0,32},{2,34},{4,36},{6,38},{8,40},{10,42},{12,44},{14,46},{16,48}... | collective-permute-start | bytes 393224 | tf_op jit(solution)/shard_map/ppermute | solution.py:373
  28.7 1.3 %collective-permute-start.8 = (bf16[16,32,128]{2,1,0:T(8,128)(2,1)S(1)}, bf16[16,32,128]{2,1,0:T(8,128)(2,1)S(1)}, u32[]{:S(2)}, u32[]{:S(2)}) collective-permute-start(bf16[16,32,128]{2,1,0:T(8,128)(2,1)S(1)} %bitcast.16), channel_id=1, source_target_pairs={{0,224},{2,226},{4,228},{6,230},{8,232},{10,234},{12,236},{14,238}... | collective-permute-start | bytes 393224 | tf_op jit(solution)/shard_map/ppermute | solution.py:372
  30.0 5.9 %collective-permute-start.4 = (bf16[32,128]{1,0:T(8,128)(2,1)S(1)}, bf16[32,128]{1,0:T(8,128)(2,1)S(1)}, u32[]{:S(2)}, u32[]{:S(2)}) collective-permute-start(bf16[32,128]{1,0:T(8,128)(2,1)S(1)} %bitcast.27), channel_id=1, source_target_pairs={{0,2},{2,0},{4,6},{6,4},{8,10},{10,8},{12,14},{14,12},{16,18},{18,... | collective-permute-start | bytes 24584 | tf_op jit(solution)/shard_map/ppermute | solution.py:369
  36.0 0.8 collective-permute-done.4
  36.8 0.0 collective-permute-done.8.refs_1_
  36.9 0.0 collective-permute-done.6.before
  36.9 0.5 tables.1
  37.4 0.6 copy-done.10
  38.0 0.0 all-to-all-done.planes
  38.0 2.7 %select.1 = bf16[16,16,32,128]{3,2,1,0:T(8,128)(2,1)} custom-call(s32[16,128]{1,0:T(8,128)S(1)} %get-tuple-element.24.wanted, bf16[8,8,32,128]{3,2,1,0:T(8,128)(2,1)S(1)} %all-to-all-done.planes), custom_call_target="tpu_custom_call" | custom-call | flops 1000000 | bytes 2500000 | tf_op jit(solution)/shard_map/select/pallas_call | solution.py:165
  40.7 6.6 %all-to-all-start.1 = ((bf16[16,16,32,128]{3,2,1,0:T(8,128)(2,1)}), bf16[16,16,32,128]{3,2,1,0:T(8,128)(2,1)}, u32[]{:S(2)}, u32[]{:S(2)}) async-start(bf16[16,16,32,128]{3,2,1,0:T(8,128)(2,1)} %select.1), calls=%async_computation.1 | async-start | bytes 4194304 | tf_op jit(solution)/shard_map/all_to_all | solution.py:387
  47.3 3.3 %collective-permute-start.11 = (bf16[32,32,128]{2,1,0:T(8,128)(2,1)S(1)}, bf16[32,32,128]{2,1,0:T(8,128)(2,1)S(1)}, u32[]{:S(2)}, u32[]{:S(2)}) collective-permute-start(bf16[32,32,128]{2,1,0:T(8,128)(2,1)S(1)} %get-tuple-element.39), channel_id=1, source_target_pairs={{0,64},{2,66},{4,68},{6,70},{8,72},{10,74},{12,76},{14,78},{16,80}... | collective-permute-start | bytes 786440 | tf_op jit(solution)/shard_map/ppermute | solution.py:392
  50.7 0.3 collective-permute-start.10
  51.0 2.2 %copy-done = bf16[8,4,256,256]{3,2,1,0:T(8,128)(2,1)S(1)} copy-done((bf16[8,4,256,256]{3,2,1,0:T(8,128)(2,1)S(1)}, bf16[8,4,256,256]{3,2,1,0:T(8,128)(2,1)}, u32[]{:S(2)}) %copy-start) | copy-done | bytes 4194328
  53.2 2.2 %near_field.1 = (f32[64,2048]{1,0:T(8,128)S(1)}, bf16[64,2048]{1,0:T(8,128)(2,1)S(1)}) custom-call(s32[8,8]{1,0:T(8,128)S(1)} %copy-done.6, bf16[64,2048]{1,0:T(8,128)(2,1)S(1)} %copy-done.1, bf16[64,2048]{1,0:T(8,128)(2,1)S(1)} %collective-permute-done.5.other, bf16[128,1024]{1,0:T(8,128)(2,1)S(1)} %collective-permute-done.6.before, ...), custom_call_target="tpu_custom_call" | custom-call | flops 600000000 | bytes 10000000 | tf_op jit(solution)/shard_map/near_field/pallas_call | solution.py:207
  55.4 0.0 copy-start.3
  55.4 0.0 copy-start.5
  55.4 0.0 copy-start.7
  55.4 0.0 copy-start.8
  55.5 3.3 %collective-permute-done.11.refs_4_ = bf16[32,32,128]{2,1,0:T(8,128)(2,1)S(1)} collective-permute-done((bf16[32,32,128]{2,1,0:T(8,128)(2,1)S(1)}, bf16[32,32,128]{2,1,0:T(8,128)(2,1)S(1)}, u32[]{:S(2)}, u32[]{:S(2)}) %collective-permute-start.11) | collective-permute-done | bytes 262176 | tf_op jit(solution)/shard_map/ppermute | solution.py:392
  58.8 1.1 %collective-permute-done.10.refs_3_ = bf16[32,32,128]{2,1,0:T(8,128)(2,1)S(1)} collective-permute-done((bf16[32,32,128]{2,1,0:T(8,128)(2,1)S(1)}, bf16[32,32,128]{2,1,0:T(8,128)(2,1)S(1)}, u32[]{:S(2)}, u32[]{:S(2)}) %collective-permute-start.10) | collective-permute-done | bytes 262176 | tf_op jit(solution)/shard_map/ppermute | solution.py:391
  60.0 1.4 %collective-permute-start.14 = (bf16[112,32,128]{2,1,0:T(8,128)(2,1)S(1)}, bf16[112,32,128]{2,1,0:T(8,128)(2,1)S(1)}, u32[]{:S(2)}, u32[]{:S(2)}) collective-permute-start(bf16[112,32,128]{2,1,0:T(8,128)(2,1)S(1)} %constant_dynamic-update-slice_fusion), channel_id=1, source_target_pairs={{0,2},{2,0},{4,6},{6,4},{8,10},{10,8},{12,14},{14,12},{16,18},{18,... | collective-permute-start | bytes 2752520 | tf_op jit(solution)/shard_map/ppermute | solution.py:400
  61.4 7.5 %collective-permute-start.13 = (bf16[8,32,128]{2,1,0:T(8,128)(2,1)S(1)}, bf16[8,32,128]{2,1,0:T(8,128)(2,1)S(1)}, u32[]{:S(2)}, u32[]{:S(2)}) collective-permute-start(bf16[8,32,128]{2,1,0:T(8,128)(2,1)S(1)} %slice.31), channel_id=1, source_target_pairs={{0,32},{2,34},{4,36},{6,38},{8,40},{10,42},{12,44},{14,46},{16,48}... | collective-permute-start | bytes 196616 | tf_op jit(solution)/shard_map/ppermute | solution.py:398
  68.9 0.7 collective-permute-start.16
  69.6 1.5 %collective-permute-done.13.refs_6_ = bf16[8,32,128]{2,1,0:T(8,128)(2,1)S(1)} collective-permute-done((bf16[8,32,128]{2,1,0:T(8,128)(2,1)S(1)}, bf16[8,32,128]{2,1,0:T(8,128)(2,1)S(1)}, u32[]{:S(2)}, u32[]{:S(2)}) %collective-permute-start.13) | collective-permute-done | bytes 65568 | tf_op jit(solution)/shard_map/ppermute | solution.py:398
  71.1 1.2 %collective-permute-done.12.refs_5_ = bf16[8,32,128]{2,1,0:T(8,128)(2,1)S(1)} collective-permute-done((bf16[8,32,128]{2,1,0:T(8,128)(2,1)S(1)}, bf16[8,32,128]{2,1,0:T(8,128)(2,1)S(1)}, u32[]{:S(2)}, u32[]{:S(2)}) %collective-permute-start.12) | collective-permute-done | bytes 65568 | tf_op jit(solution)/shard_map/ppermute | solution.py:397
  72.3 1.3 %collective-permute-start.15 = (bf16[16,32,128]{2,1,0:T(8,128)(2,1)S(1)}, bf16[16,32,128]{2,1,0:T(8,128)(2,1)S(1)}, u32[]{:S(2)}, u32[]{:S(2)}) collective-permute-start(bf16[16,32,128]{2,1,0:T(8,128)(2,1)S(1)} %pad_maximum_fusion.7), channel_id=1, source_target_pairs={{0,2},{2,0},{4,6},{6,4},{8,10},{10,8},{12,14},{14,12},{16,18},{18,... | collective-permute-start | bytes 393224 | tf_op jit(solution)/shard_map/ppermute | solution.py:400
  73.6 1.0 %collective-permute-done.15.refs_8_ = bf16[16,32,128]{2,1,0:T(8,128)(2,1)S(1)} collective-permute-done((bf16[16,32,128]{2,1,0:T(8,128)(2,1)S(1)}, bf16[16,32,128]{2,1,0:T(8,128)(2,1)S(1)}, u32[]{:S(2)}, u32[]{:S(2)}) %collective-permute-start.15) | collective-permute-done | bytes 131104 | tf_op jit(solution)/shard_map/ppermute | solution.py:400
  74.6 3.2 %fields.1.descended_in = f32[8,64,64]{2,1,0:T(8,128)S(1)} custom-call(s32[8]{0:T(128)S(1)} %copy-done.7, s32[2,16]{1,0:T(2,128)S(1)} %copy-done.8, bf16[16,32,128]{2,1,0:T(8,128)(2,1)S(1)} %bitcast.19, bf16[16,32,128]{2,1,0:T(8,128)(2,1)S(1)} %collective-permute-done.8.refs_1_, bf16[16,32,128]{2,1,0:T(8,128)(2,1)S(1)} %collective-permute-done.9.refs_2_, ...), custom_call_target="tpu_custom_call" | custom-call | flops 50000000 | bytes 4000000 | tf_op jit(solution)/shard_map/fields/pallas_call | solution.py:264
  77.8 0.7 copy-done.2
  78.5 0.5 collective-permute-done.16.near_in_in
  79.0 0.7 copy-done.11
  79.7 7.3 %downward.1 = bf16[64,2048]{1,0:T(8,128)(2,1)} custom-call(s32[1,256]{1,0:T(1,128)} %copy-done.10, bf16[256,32,128]{2,1,0:T(8,128)(2,1)} %bitcast.12.blocks, bf16[8,64,1536]{2,1,0:T(8,128)(2,1)} %coupling_in.1, f32[8,64,64]{2,1,0:T(8,128)} %copy-done.2, bf16[8,64,256]{2,1,0:T(8,128)(2,1)} %basis_in.3, f32[64,2048]{1,0:T(8,128)} %copy-done.4, ...), custom_call_target="tpu_custom_call" | custom-call | flops 150000000 | bytes 6000000 | tf_op jit(solution)/shard_map/downward/pallas_call | solution.py:322
  (39 shorter events, 0.3 us)
Async XLA Ops:
  0.0 23.2 %collective-permute-start.5 = (bf16[64,2048]{1,0:T(8,128)(2,1)}, bf16[64,2048]{1,0:T(8,128)(2,1)S(1)}, u32[]{:S(2)}, u32[]{:S(2)}) collective-permute-start(bf16[64,2048]{1,0:T(8,128)(2,1)} %signals.1), channel_id=1, source_target_pairs={{0,1},{1,0},{2,3},{3,2},{4,5},{5,4},{6,7},{7,6},{8,9},{9,8},{10,11... | collective-permute-start | bytes 786440 | tf_op jit(solution)/shard_map/ppermute | solution.py:356
  7.0 29.9 %copy-start.9 = (s32[1,256]{1,0:T(1,128)S(1)}, s32[1,256]{1,0:T(1,128)}, u32[]{:S(2)}) copy-start(s32[1,256]{1,0:T(1,128)} %get-tuple-element.22.own_row) | copy-start | bytes 3076
  7.0 30.9 %all-to-all-start = ((bf16[8,8,32,128]{3,2,1,0:T(8,128)(2,1)}), bf16[8,8,32,128]{3,2,1,0:T(8,128)(2,1)S(1)}, u32[]{:S(2)}, u32[]{:S(2)}) async-start(bf16[8,8,32,128]{3,2,1,0:T(8,128)(2,1)} %get-tuple-element.25), calls=%async_computation | async-start | bytes 1048576 | tf_op jit(solution)/shard_map/all_to_all | solution.py:359
  15.2 2.8 %collective-permute-start = (bf16[80,128]{1,0:T(8,128)(2,1)}, bf16[80,128]{1,0:T(8,128)(2,1)S(1)}, u32[]{:S(2)}, u32[]{:S(2)}) collective-permute-start(bf16[80,128]{1,0:T(8,128)(2,1)} %get-tuple-element.20), channel_id=1, source_target_pairs={{0,4},{2,6},{4,0},{6,2},{8,12},{10,14},{12,8},{14,10},{16,20},{18,... | collective-permute-start | bytes 61448 | tf_op jit(solution)/shard_map/ppermute | solution.py:360
  18.8 8.0 %collective-permute-start.2 = (bf16[2,80,128]{2,1,0:T(8,128)(2,1)S(1)}, bf16[2,80,128]{2,1,0:T(8,128)(2,1)S(1)}, u32[]{:S(2)}, u32[]{:S(2)}) collective-permute-start(bf16[2,80,128]{2,1,0:T(8,128)(2,1)S(1)} %get-tuple-element.42), channel_id=1, source_target_pairs={{0,16},{2,18},{4,20},{6,22},{8,24},{10,26},{12,28},{14,30},{16,0},... | collective-permute-start | bytes 122888 | tf_op jit(solution)/shard_map/ppermute | solution.py:364
  21.7 5.1 %collective-permute-start.1 = (bf16[2,80,128]{2,1,0:T(8,128)(2,1)S(1)}, bf16[2,80,128]{2,1,0:T(8,128)(2,1)S(1)}, u32[]{:S(2)}, u32[]{:S(2)}) collective-permute-start(bf16[2,80,128]{2,1,0:T(8,128)(2,1)S(1)} %get-tuple-element.42), channel_id=1, source_target_pairs={{0,24},{2,26},{4,28},{6,30},{8,0},{10,2},{12,4},{14,6},{16,8},{18,... | collective-permute-start | bytes 122888 | tf_op jit(solution)/shard_map/ppermute | solution.py:364
  22.5 4.4 %collective-permute-start.3 = (bf16[2,80,128]{2,1,0:T(8,128)(2,1)S(1)}, bf16[2,80,128]{2,1,0:T(8,128)(2,1)S(1)}, u32[]{:S(2)}, u32[]{:S(2)}) collective-permute-start(bf16[2,80,128]{2,1,0:T(8,128)(2,1)S(1)} %get-tuple-element.42), channel_id=1, source_target_pairs={{0,8},{2,10},{4,12},{6,14},{8,16},{10,18},{12,20},{14,22},{16,24},... | collective-permute-start | bytes 122888 | tf_op jit(solution)/shard_map/ppermute | solution.py:364
  23.2 13.6 %collective-permute-start.6 = (bf16[128,1024]{1,0:T(8,128)(2,1)S(1)}, bf16[128,1024]{1,0:T(8,128)(2,1)S(1)}, u32[]{:S(2)}, u32[]{:S(2)}) collective-permute-start(bf16[128,1024]{1,0:T(8,128)(2,1)S(1)} %pad_maximum_fusion.2), channel_id=1, source_target_pairs={{0,2},{2,4},{4,6},{6,8},{8,10},{10,12},{12,14},{14,16},{16,18},{18... | collective-permute-start | bytes 786440 | tf_op jit(solution)/shard_map/ppermute | solution.py:377
  26.8 10.1 %collective-permute-start.7 = (bf16[128,1024]{1,0:T(8,128)(2,1)S(1)}, bf16[128,1024]{1,0:T(8,128)(2,1)S(1)}, u32[]{:S(2)}, u32[]{:S(2)}) collective-permute-start(bf16[128,1024]{1,0:T(8,128)(2,1)S(1)} %pad_maximum_fusion.3), channel_id=1, source_target_pairs={{2,0},{4,2},{6,4},{8,6},{10,8},{12,10},{14,12},{16,14},{18,16},{20... | collective-permute-start | bytes 786440 | tf_op jit(solution)/shard_map/ppermute | solution.py:380
  26.9 9.9 %collective-permute-start.9 = (bf16[16,32,128]{2,1,0:T(8,128)(2,1)S(1)}, bf16[16,32,128]{2,1,0:T(8,128)(2,1)S(1)}, u32[]{:S(2)}, u32[]{:S(2)}) collective-permute-start(bf16[16,32,128]{2,1,0:T(8,128)(2,1)S(1)} %bitcast.15), channel_id=1, source_target_pairs={{0,32},{2,34},{4,36},{6,38},{8,40},{10,42},{12,44},{14,46},{16,48}... | collective-permute-start | bytes 393224 | tf_op jit(solution)/shard_map/ppermute | solution.py:373
  28.7 8.1 %collective-permute-start.8 = (bf16[16,32,128]{2,1,0:T(8,128)(2,1)S(1)}, bf16[16,32,128]{2,1,0:T(8,128)(2,1)S(1)}, u32[]{:S(2)}, u32[]{:S(2)}) collective-permute-start(bf16[16,32,128]{2,1,0:T(8,128)(2,1)S(1)} %bitcast.16), channel_id=1, source_target_pairs={{0,224},{2,226},{4,228},{6,230},{8,232},{10,234},{12,236},{14,238}... | collective-permute-start | bytes 393224 | tf_op jit(solution)/shard_map/ppermute | solution.py:372
  30.0 6.8 %collective-permute-start.4 = (bf16[32,128]{1,0:T(8,128)(2,1)S(1)}, bf16[32,128]{1,0:T(8,128)(2,1)S(1)}, u32[]{:S(2)}, u32[]{:S(2)}) collective-permute-start(bf16[32,128]{1,0:T(8,128)(2,1)S(1)} %bitcast.27), channel_id=1, source_target_pairs={{0,2},{2,0},{4,6},{6,4},{8,10},{10,8},{12,14},{14,12},{16,18},{18,... | collective-permute-start | bytes 24584 | tf_op jit(solution)/shard_map/ppermute | solution.py:369
  37.4 0.6 copy-start.10
  40.7 10.3 %copy-start.1 = (bf16[64,2048]{1,0:T(8,128)(2,1)S(1)}, bf16[64,2048]{1,0:T(8,128)(2,1)}, u32[]{:S(2)}) copy-start(bf16[64,2048]{1,0:T(8,128)(2,1)} %signals.1) | copy-start | bytes 786436
  40.7 10.3 %copy-start.6 = (s32[8,8]{1,0:T(8,128)S(1)}, s32[8,8]{1,0:T(8,128)}, u32[]{:S(2)}) copy-start(s32[8,8]{1,0:T(8,128)} %near_list.1) | copy-start | bytes 772
  40.7 38.4 %all-to-all-start.1 = ((bf16[16,16,32,128]{3,2,1,0:T(8,128)(2,1)}), bf16[16,16,32,128]{3,2,1,0:T(8,128)(2,1)}, u32[]{:S(2)}, u32[]{:S(2)}) async-start(bf16[16,16,32,128]{3,2,1,0:T(8,128)(2,1)} %select.1), calls=%async_computation.1 | async-start | bytes 4194304 | tf_op jit(solution)/shard_map/all_to_all | solution.py:387
  47.3 11.4 %collective-permute-start.11 = (bf16[32,32,128]{2,1,0:T(8,128)(2,1)S(1)}, bf16[32,32,128]{2,1,0:T(8,128)(2,1)S(1)}, u32[]{:S(2)}, u32[]{:S(2)}) collective-permute-start(bf16[32,32,128]{2,1,0:T(8,128)(2,1)S(1)} %get-tuple-element.39), channel_id=1, source_target_pairs={{0,64},{2,66},{4,68},{6,70},{8,72},{10,74},{12,76},{14,78},{16,80}... | collective-permute-start | bytes 786440 | tf_op jit(solution)/shard_map/ppermute | solution.py:392
  50.7 9.2 %collective-permute-start.10 = (bf16[32,32,128]{2,1,0:T(8,128)(2,1)S(1)}, bf16[32,32,128]{2,1,0:T(8,128)(2,1)S(1)}, u32[]{:S(2)}, u32[]{:S(2)}) collective-permute-start(bf16[32,32,128]{2,1,0:T(8,128)(2,1)S(1)} %get-tuple-element.40), channel_id=1, source_target_pairs={{0,192},{2,194},{4,196},{6,198},{8,200},{10,202},{12,204},{14,206}... | collective-permute-start | bytes 786440 | tf_op jit(solution)/shard_map/ppermute | solution.py:391
  51.0 2.2 %copy-start = (bf16[8,4,256,256]{3,2,1,0:T(8,128)(2,1)S(1)}, bf16[8,4,256,256]{3,2,1,0:T(8,128)(2,1)}, u32[]{:S(2)}) copy-start(bf16[8,4,256,256]{3,2,1,0:T(8,128)(2,1)} %tiles.1) | copy-start | bytes 12582916
  55.4 4.6 %copy-start.4 = (f32[64,2048]{1,0:T(8,128)}, f32[64,2048]{1,0:T(8,128)S(1)}, u32[]{:S(2)}) copy-start(f32[64,2048]{1,0:T(8,128)S(1)} %get-tuple-element.33.near_own_in) | copy-start | bytes 1572868
  55.4 19.2 %copy-start.3 = (bf16[8,64,64]{2,1,0:T(8,128)(2,1)S(1)}, bf16[8,64,64]{2,1,0:T(8,128)(2,1)}, u32[]{:S(2)}) copy-start(bf16[8,64,64]{2,1,0:T(8,128)(2,1)} %refs_10_.1) | copy-start | bytes 196612
  55.4 19.2 %copy-start.5 = (bf16[2,64,1024]{2,1,0:T(8,128)(2,1)S(1)}, bf16[2,64,1024]{2,1,0:T(8,128)(2,1)}, u32[]{:S(2)}) copy-start(bf16[2,64,1024]{2,1,0:T(8,128)(2,1)} %refs_9_.1) | copy-start | bytes 786436
  55.4 19.2 %copy-start.7 = (s32[8]{0:T(128)S(1)}, s32[8]{0:T(128)}, u32[]{:S(2)}) copy-start(s32[8]{0:T(128)} %parent.3) | copy-start | bytes 100
  55.4 19.2 %copy-start.8 = (s32[2,16]{1,0:T(2,128)S(1)}, s32[2,16]{1,0:T(2,128)}, u32[]{:S(2)}) copy-start(s32[2,16]{1,0:T(2,128)} %parent_far.1) | copy-start | bytes 388
  60.0 14.6 %collective-permute-start.14 = (bf16[112,32,128]{2,1,0:T(8,128)(2,1)S(1)}, bf16[112,32,128]{2,1,0:T(8,128)(2,1)S(1)}, u32[]{:S(2)}, u32[]{:S(2)}) collective-permute-start(bf16[112,32,128]{2,1,0:T(8,128)(2,1)S(1)} %constant_dynamic-update-slice_fusion), channel_id=1, source_target_pairs={{0,2},{2,0},{4,6},{6,4},{8,10},{10,8},{12,14},{14,12},{16,18},{18,... | collective-permute-start | bytes 2752520 | tf_op jit(solution)/shard_map/ppermute | solution.py:400
  61.4 9.7 %collective-permute-start.13 = (bf16[8,32,128]{2,1,0:T(8,128)(2,1)S(1)}, bf16[8,32,128]{2,1,0:T(8,128)(2,1)S(1)}, u32[]{:S(2)}, u32[]{:S(2)}) collective-permute-start(bf16[8,32,128]{2,1,0:T(8,128)(2,1)S(1)} %slice.31), channel_id=1, source_target_pairs={{0,32},{2,34},{4,36},{6,38},{8,40},{10,42},{12,44},{14,46},{16,48}... | collective-permute-start | bytes 196616 | tf_op jit(solution)/shard_map/ppermute | solution.py:398
  68.9 3.4 %collective-permute-start.12 = (bf16[8,32,128]{2,1,0:T(8,128)(2,1)S(1)}, bf16[8,32,128]{2,1,0:T(8,128)(2,1)S(1)}, u32[]{:S(2)}, u32[]{:S(2)}) collective-permute-start(bf16[8,32,128]{2,1,0:T(8,128)(2,1)S(1)} %slice.30), channel_id=1, source_target_pairs={{0,224},{2,226},{4,228},{6,230},{8,232},{10,234},{12,236},{14,238}... | collective-permute-start | bytes 196616 | tf_op jit(solution)/shard_map/ppermute | solution.py:397
  68.9 10.1 %collective-permute-start.16 = (bf16[64,2048]{1,0:T(8,128)(2,1)S(1)}, bf16[64,2048]{1,0:T(8,128)(2,1)S(1)}, u32[]{:S(2)}, u32[]{:S(2)}) collective-permute-start(bf16[64,2048]{1,0:T(8,128)(2,1)S(1)} %get-tuple-element.34), channel_id=1, source_target_pairs={{0,1},{1,0},{2,3},{3,2},{4,5},{5,4},{6,7},{7,6},{8,9},{9,8},{10,11... | collective-permute-start | bytes 786440 | tf_op jit(solution)/shard_map/ppermute | solution.py:395
  72.3 2.3 %collective-permute-start.15 = (bf16[16,32,128]{2,1,0:T(8,128)(2,1)S(1)}, bf16[16,32,128]{2,1,0:T(8,128)(2,1)S(1)}, u32[]{:S(2)}, u32[]{:S(2)}) collective-permute-start(bf16[16,32,128]{2,1,0:T(8,128)(2,1)S(1)} %pad_maximum_fusion.7), channel_id=1, source_target_pairs={{0,2},{2,0},{4,6},{6,4},{8,10},{10,8},{12,14},{14,12},{16,18},{18,... | collective-permute-start | bytes 393224 | tf_op jit(solution)/shard_map/ppermute | solution.py:400
  77.8 0.7 copy-start.2
  79.0 0.7 copy-start.11

commit v3 on v2

--- a/solution.py
+++ b/solution.py
@@ -99,15 +99,19 @@
 
 
 def upward_kernel(
-    parent, far_list, signals_in, basis_in, transfer_in, coef_out, pay_out, row_out, signals, basis, transfer, sems
+    parent, own_list, peer_list, signals_in, basis_in, transfer_in, coef_out, pay_out, row_out, signals, basis, transfer, sems
 ):
     pending = load([(signals_in, signals), (basis_in, basis), (transfer_in, transfer)], sems)
-    ids = far_list[...]
-    row = jnp.concatenate([ids[t : t + 1] for t in range(ids.shape[0])], axis=1)
-    row = jnp.concatenate([row, jnp.full((1, 256 - row.shape[1]), -8, jnp.int32)], axis=1)
-    devices, members = row // ids.shape[0], row % ids.shape[0]
-    row_out[...] = devices
-    lists = [devices[:, :128], devices[:, 128:], members[:, :128], members[:, 128:], jnp.zeros((12, 128), jnp.int32)]
+    lists = []
+    for ref in (own_list, peer_list):
+        ids = ref[...]
+        row = jnp.concatenate([ids[t : t + 1] for t in range(ids.shape[0])], axis=1)
+        row = jnp.concatenate([row, jnp.full((1, 256 - row.shape[1]), -8, jnp.int32)], axis=1)
+        devices, members = row // ids.shape[0], row % ids.shape[0]
+        lists += [devices[:, :128], devices[:, 128:], members[:, :128], members[:, 128:]]
+        if ref is own_list:
+            row_out[...] = devices
+    lists.append(jnp.zeros((8, 128), jnp.int32))
     pay_out[64:80] = jnp.concatenate(lists, axis=0).astype(jnp.float32).astype(jnp.bfloat16)
     for copy in pending:
         copy.wait()
@@ -126,7 +130,7 @@
         pay_out[i * 32 : (i + 1) * 32] = pack(s.astype(jnp.bfloat16))
 
 
-def upward(parent, far_list, signals, basis, transfer):
+def upward(parent, own_list, peer_list, signals, basis, transfer):
     leaf_count = basis.shape[0]
     return pl.pallas_call(
         upward_kernel,
@@ -135,7 +139,7 @@
             jax.ShapeDtypeStruct((80, 128), jnp.bfloat16),
             jax.ShapeDtypeStruct((1, 256), jnp.int32),
         ),
-        in_specs=[SMEM_SPEC, VMEM_SPEC, ANY_SPEC, ANY_SPEC, ANY_SPEC],
+        in_specs=[SMEM_SPEC, VMEM_SPEC, VMEM_SPEC, ANY_SPEC, ANY_SPEC, ANY_SPEC],
         out_specs=(VMEM_SPEC,) * 3,
         scratch_shapes=[
             pltpu.VMEM(signals.shape, jnp.bfloat16),
@@ -146,28 +150,31 @@
         compiler_params=pltpu.CompilerParams(vmem_limit_bytes=56 * MIB),
         cost_estimate=cost(30_000_000, 700_000),
         name="upward",
-    )(parent, far_list, signals, basis, transfer)
-
-
-def select_kernel(wanted, planes, send):
-    step = pl.program_id(0)
+    )(parent, own_list, peer_list, signals, basis, transfer)
+
+
+def select_kernel(wanted, planes, send_out, send, sems):
     own = lax.axis_index("loop") % PLANE
-    for i in range(send.shape[0]):
-        peer = step * send.shape[0] + i
+    pending = []
+    for peer in range(PLANE):
         dy = jnp.bitwise_and(peer // (X * C) - own // (X * C) + Y, Y - 1)
         row = dy * (X * C) + jnp.bitwise_and(jnp.bitwise_xor(peer, own), X * C - 1)
         for slot in range(2 * Z):
-            send[i, slot] = planes[slot // 2, wanted[row, slot]]
+            send[peer, slot] = planes[slot // 2, wanted[row, slot]]
+        pending.append(pltpu.make_async_copy(send.at[peer], send_out.at[peer], sems.at[peer]))
+        pending[-1].start()
+    for copy in pending:
+        copy.wait()
 
 
 def select(wanted, planes):
-    per_step = 4
+    shape = (PLANE, 2 * Z, 32, 128)
     return pl.pallas_call(
         select_kernel,
-        grid=(PLANE // per_step,),
-        out_shape=jax.ShapeDtypeStruct((PLANE, 2 * Z, 32, 128), jnp.bfloat16),
+        out_shape=jax.ShapeDtypeStruct(shape, jnp.bfloat16),
         in_specs=[SMEM_SPEC, VMEM_SPEC],
-        out_specs=pl.BlockSpec((per_step, 2 * Z, 32, 128), lambda s: (s, 0, 0, 0)),
+        out_specs=ANY_SPEC,
+        scratch_shapes=[pltpu.VMEM(shape, jnp.bfloat16), pltpu.SemaphoreType.DMA((PLANE,))],
         compiler_params=pltpu.CompilerParams(vmem_limit_bytes=8 * MIB),
         cost_estimate=cost(1_000_000, 2_500_000),
         name="select",
@@ -223,8 +230,8 @@
 
 
 def fields_kernel(parent, parent_far, *refs):
-    sources = refs[:9]
-    coupling_in, transfer_in, out, parents, coupling, transfer, sems = refs[9:]
+    sources = refs[:11]
+    coupling_in, transfer_in, out, parents, coupling, transfer, sems = refs[11:]
     copies = [(coupling_in, coupling), (transfer_in, transfer)]
     at = 0
     for ref in sources:
@@ -249,7 +256,7 @@
             dx = jnp.bitwise_and(cross // C, X - 1)
             member = (dy * X + dx) * 2 + jnp.bitwise_and(source, 1)
             base = jnp.int32(0)
-            for place, h in enumerate((0, 1, 7, 2, 3, 6, 5, 4)):
+            for place, h in enumerate((0, 1, 7, 2, 6, 3, 5, 4)):
                 base = jnp.where(hop == h, place * per, base)
             where = jnp.bitwise_and(cross, C - 1) * (Z * per) + base + member
             stacked += unpack(parents[where])
@@ -264,13 +271,13 @@
     return pl.pallas_call(
         fields_kernel,
         out_shape=jax.ShapeDtypeStruct(transfer.shape, jnp.float32),
-        in_specs=[SMEM_SPEC] * 2 + [ANY_SPEC] * 11,
+        in_specs=[SMEM_SPEC] * 2 + [ANY_SPEC] * 13,
         out_specs=VMEM_SPEC,
         scratch_shapes=[
             pltpu.VMEM((2 * Z * Y * X * 2, 32, 128), jnp.bfloat16),
             pltpu.VMEM(parent_coupling.shape, jnp.bfloat16),
             pltpu.VMEM(transfer.shape, jnp.bfloat16),
-            pltpu.SemaphoreType.DMA((11,)),
+            pltpu.SemaphoreType.DMA((13,)),
         ],
         compiler_params=pltpu.CompilerParams(vmem_limit_bytes=16 * MIB),
         cost_estimate=cost(50_000_000, 4_000_000),
@@ -280,56 +287,74 @@
 
 def downward_kernel(
     slots,
-    blocks,
+    blocks_in,
+    near_in_in,
     coupling_in,
     descended_in,
     basis_in,
     near_own_in,
-    near_in_in,
-    out,
+    out_hbm,
+    blocks,
+    near_in,
     coupling,
     descended,
     basis,
     near_own,
-    near_in,
+    stacked,
+    out,
     sems,
+    out_sems,
 ):
     leaf_count, rank, leaf_size = basis.shape
+    part = blocks.shape[0] // 8
     pending = load(
-        [(coupling_in.at[c], coupling.at[c]) for c in range(leaf_count)]
+        [(blocks_in.at[pl.ds(i * part, part)], blocks.at[pl.ds(i * part, part)]) for i in range(8)]
+        + [(coupling_in.at[c], coupling.at[c]) for c in range(leaf_count)]
         + [(descended_in, descended), (basis_in, basis), (near_own_in, near_own), (near_in_in, near_in)],
         sems,
     )
+    for copy in pending[:8]:
+        copy.wait()
     sources = coupling.shape[2] // rank
     columns = out.shape[0]
     for c in range(leaf_count):
-        stacked = []
         for j in range(sources):
-            stacked += unpack(blocks[slots[0, c * sources + j]])
-        pending[c].wait()
-        if c == 0:
-            for copy in pending[leaf_count:]:
-                copy.wait()
-        leaf_far = dot(coupling[c], jnp.concatenate(stacked, axis=0), NN)[:, :columns]
+            pieces = jnp.concatenate(unpack(blocks[slots[0, c * sources + j]]), axis=0)
+            stacked[c, j * rank : (j + 1) * rank] = pieces
+    for copy in pending[8:]:
+        copy.wait()
+    written = []
+    for c in range(leaf_count):
+        leaf_far = dot(coupling[c], stacked[c], NN)[:, :columns]
         combined = (leaf_far + descended[c]).astype(jnp.bfloat16)
         far_out = dot(combined, basis[c], TN)
-        at = slice(c * leaf_size, (c + 1) * leaf_size)
+        at = pl.ds(c * leaf_size, leaf_size)
         out[:, at] = (near_own[:, at] + near_in[:, at].astype(jnp.float32) + far_out).astype(jnp.bfloat16)
+        written.append(pltpu.make_async_copy(out.at[:, at], out_hbm.at[:, at], out_sems.at[c]))
+        written[-1].start()
+    for copy in written:
+        copy.wait()
 
 
 def downward(slots, blocks, coupling, descended, basis, near_own, near_in):
-    arrays = (coupling, descended, basis, near_own, near_in)
+    arrays = (blocks, near_in, coupling, descended, basis, near_own)
+    leaf_count = basis.shape[0]
     return pl.pallas_call(
         downward_kernel,
         out_shape=jax.ShapeDtypeStruct(near_own.shape, jnp.bfloat16),
-        in_specs=[SMEM_SPEC, VMEM_SPEC] + [ANY_SPEC] * 5,
-        out_specs=VMEM_SPEC,
+        in_specs=[SMEM_SPEC] + [ANY_SPEC] * 6,
+        out_specs=ANY_SPEC,
         scratch_shapes=[pltpu.VMEM(a.shape, a.dtype) for a in arrays]
-        + [pltpu.SemaphoreType.DMA((4 + coupling.shape[0],))],
-        compiler_params=pltpu.CompilerParams(vmem_limit_bytes=60 * MIB),
+        + [
+            pltpu.VMEM((leaf_count, coupling.shape[2], 128), jnp.bfloat16),
+            pltpu.VMEM(near_own.shape, jnp.bfloat16),
+            pltpu.SemaphoreType.DMA((12 + leaf_count,)),
+            pltpu.SemaphoreType.DMA((leaf_count,)),
+        ],
+        compiler_params=pltpu.CompilerParams(vmem_limit_bytes=62 * MIB),
         cost_estimate=cost(150_000_000, 6_000_000),
         name="downward",
-    )(slots, blocks, *arrays)
+    )(slots, *arrays)
 
 
 def shards(
@@ -354,7 +379,8 @@
     planes_of = [[z * PLANE + p for p in range(PLANE)] for z in range(Z)]
 
     other = swap(signals)
-    coefs, payload, own_row = upward(parent, far_list, signals, leaf_basis, transfer)
+    peer_list = along(far_list, perm=c_swap)
+    coefs, payload, own_row = upward(parent, far_list, peer_list, signals, leaf_basis, transfer)
 
     planes = lax.all_to_all(coefs, "loop", 0, 0, tiled=True, axis_index_groups=columns_of)
     pair = jnp.stack([payload, along(payload, perm=x_swap)])
@@ -365,12 +391,11 @@
             for dy in range(1, Y)
         ]
     )
-    core_lists = quads[:, :, 64:68].reshape(Y * X, 4, 128)
-    peer_lists = along(core_lists.reshape(-1, 128), perm=c_swap).reshape(Y * X, 4, 128)
-    plane_lists = jnp.stack([core_lists, peer_lists], axis=1).reshape(PLANE, 4, 128).transpose(1, 0, 2)
+    plane_lists = quads[:, :, 64:72].reshape(PLANE, 4, 128).transpose(1, 0, 2)
     parents = quads[:, :, :64].reshape(-1, 32, 128)
-    one_down = along(parents, perm=loop_moves(lambda z, y, x, c: (z - 1, y, x, c)))
-    one_up = along(parents, perm=loop_moves(lambda z, y, x, c: (z + 1, y, x, c)))
+    down = functools.partial(along, perm=loop_moves(lambda z, y, x, c: (z - 1, y, x, c)))
+    up = functools.partial(along, perm=loop_moves(lambda z, y, x, c: (z + 1, y, x, c)))
+    one_down, one_up = down(parents), up(parents)
 
     reach = width // 2
     count = Z * PLANE
@@ -380,24 +405,21 @@
     after = along(
         jnp.concatenate([signals[:, :reach], other[:, :reach]]), perm=[((i + 1) % count, i) for i in range(count)]
     )
-    plane_lists, before, after, one_down, one_up = lax.optimization_barrier(
-        (plane_lists, before, after, one_down, one_up)
-    )
     wanted, slots = tables(plane_lists.astype(jnp.int32), own_row)
-    blocks = lax.all_to_all(
-        select(wanted, planes), "loop", 0, 0, tiled=True, axis_index_groups=planes_of
-    )
-
-    far_down = along(jnp.concatenate([parents, one_down]), perm=loop_moves(lambda z, y, x, c: (z - 2, y, x, c)))
-    far_up = along(jnp.concatenate([parents, one_up]), perm=loop_moves(lambda z, y, x, c: (z + 2, y, x, c)))
+    send, before, after, one_down, one_up = lax.optimization_barrier(
+        (select(wanted, planes), before, after, one_down, one_up)
+    )
+    blocks = lax.all_to_all(send, "loop", 0, 0, tiled=True, axis_index_groups=planes_of)
+
+    two_down, two_up = down(one_down), up(one_up)
     near_own, near_other = near_field(near_list, signals, other, before, after, near_tiles)
-    near_other, far_down, far_up = lax.optimization_barrier((near_other, far_down, far_up))
     near_in = swap(near_other)
+    _, two_down, two_up = lax.optimization_barrier((near_other, two_down, two_up))
+    three_down, three_up = down(two_down), up(two_up)
     half = parents.shape[0] // 2
-    last_down = along(far_down[2 * half : 3 * half], perm=loop_moves(lambda z, y, x, c: (z - 1, y, x, c)))
-    last_up = along(far_up[3 * half :], perm=loop_moves(lambda z, y, x, c: (z + 1, y, x, c)))
-    mine = [parents, one_down, one_up, far_down, far_up, last_down, last_up]
-    theirs = [along(jnp.concatenate(part), perm=c_swap) for part in (mine[:5], mine[5:])]
+    four_down, four_up = down(three_down[:half]), up(three_up[half:])
+    mine = [parents, one_down, one_up, two_down, two_up, three_down, three_up, four_down, four_up]
+    theirs = [along(jnp.concatenate(part), perm=c_swap) for part in (mine[:7], mine[7:])]
     descended = fields(parent, parent_far, mine + theirs, parent_coupling, transfer)
 
     return downward(slots, blocks.reshape(-1, 32, 128), coupling, descended, leaf_basis, near_own, near_in)

time: 88.4 us -> 82.6 us (0.934)
  starting transfers between devices: 50.2 us -> 37.8 us
  waiting for transfers between devices: 11 us -> 19.2 us
  Pallas kernels: 19.3 us -> 18.1 us
    ppermute x7 -> x9, starting transfers between devices: 20.2 us -> 11.1 us  [the longest x1 3.24 us: shards(): peer_list = along(far_list, perm=c_swap)]
    all_to_all x1, waiting for transfers between devices: 0.01 us -> 4.58 us  [shards(): lax.all_to_all(coefs, 'loop', 0, 0, tiled=True, axis_index_groups=columns...]
    ppermute x1, waiting for transfers between devices: 0.55 us -> 3.26 us  [shards(): near_in = swap(near_other)]
    ppermute x1, starting transfers between devices: 3.57 us -> 1.01 us  [shards(): other = swap(signals)]
    ppermute x1, waiting for transfers between devices: 1.54 us -> 0.01 us  [shards(): pair = jnp.stack([payload, along(payload, perm=x_swap)])]
    pallas_call x1, Pallas kernels: 7.32 us -> 5.93 us  [downward(): pl.pallas_call(downward_kernel, out_shape=jax.ShapeDtypeStruct(near_own.s...]
    ppermute x7 -> x9, waiting for transfers between devices: 7.94 us -> 9.25 us  [the longest x2 5.37 us: shards(): three_down, three_up = (down(two_down), up(two_up))]
    ppermute x3, waiting for transfers between devices: 0.01 us -> 1.08 us  [shards(): along(pair, perm=loop_moves(lambda z, y, x, c, dy=dy: (z, y - dy, x, c)))]
  transfers between devices with their start and end apart: 19 -> 21, of which waited for: 8 -> 10; matrix products, arithmetic and copies ran while one was open for 2% -> 2% of each run, Pallas kernels for 11% -> 15%
where the time goes in v3:
time: 82.6 us; the launch traced here: 82.2 us
  starting transfers between devices  37.8 us (46%)
  waiting for transfers between devices  19.2 us (23%)
  Pallas kernels  18.1 us (22%)
  local copies, waits for them, and re-layouts  5.89 us (7%)
    all_to_all x1, starting transfers between devices, shards(): lax.all_to_all(coefs, 'loop', 0, 0, tiled=True, axis_index_groups=columns...  8.19 us
    all_to_all x1, starting transfers between devices, shards(): lax.all_to_all(send, 'loop', 0, 0, tiled=True, axis_index_groups=planes_of)  6.65 us
    pallas_call x1, Pallas kernels, downward(): pl.pallas_call(downward_kernel, out_shape=jax.ShapeDtypeStruct(near_own.s...  5.93 us
    ppermute x2, waiting for transfers between devices, shards(): three_down, three_up = (down(two_down), up(two_up))  5.37 us
    unnamed x32, local copies, waits for them, and re-layouts  4.86 us
    all_to_all x1, waiting for transfers between devices, shards(): lax.all_to_all(coefs, 'loop', 0, 0, tiled=True, axis_index_groups=columns...  4.58 us
    pallas_call x1, Pallas kernels, fields(): pl.pallas_call(fields_kernel, out_shape=jax.ShapeDtypeStruct(transfer.sha...  3.82 us
    ppermute x3, starting transfers between devices, shards(): along(pair, perm=loop_moves(lambda z, y, x, c, dy=dy: (z, y - dy, x, c)))  3.77 us
  transfers between devices with their start and end apart: 21, of which 10 were waited for; matrix products, arithmetic and copies ran while one was open for 2% of the time, Pallas kernels for 15%

profile of v3, /device:TPU:1, one launch (start us, length us, event | category | flops | bytes accessed | tf_op | source)
XLA Modules:
  0.0 82.2 jit_solution(5864237609019302283)
XLA Ops:
  0.0 3.2 %collective-permute-start = (s32[8,24]{1,0:T(8,128)}, s32[8,24]{1,0:T(8,128)S(1)}, u32[]{:S(2)}, u32[]{:S(2)}) collective-permute-start(s32[8,24]{1,0:T(8,128)} %own_list.1), channel_id=1, source_target_pairs={{0,2},{2,0},{4,6},{6,4},{8,10},{10,8},{12,14},{14,12},{16,18},{18,... | collective-permute-start | bytes 2312 | tf_op jit(solution)/shard_map/ppermute | solution.py:382
  3.2 1.0 %collective-permute-start.5 = (bf16[64,2048]{1,0:T(8,128)(2,1)}, bf16[64,2048]{1,0:T(8,128)(2,1)S(1)}, u32[]{:S(2)}, u32[]{:S(2)}) collective-permute-start(bf16[64,2048]{1,0:T(8,128)(2,1)} %signals.1), channel_id=1, source_target_pairs={{0,1},{1,0},{2,3},{3,2},{4,5},{5,4},{6,7},{7,6},{8,9},{9,8},{10,11... | collective-permute-start | bytes 786440 | tf_op jit(solution)/shard_map/ppermute | solution.py:381
  4.2 0.0 collective-permute-done.peer_list
  4.3 0.6 copy-done.12
  4.9 3.4 %upward.1 = (bf16[8,8,32,128]{3,2,1,0:T(8,128)(2,1)}, bf16[80,128]{1,0:T(8,128)(2,1)}, s32[1,256]{1,0:T(1,128)}) custom-call(s32[8]{0:T(128)} %parent.3, s32[8,24]{1,0:T(8,128)} %own_list.1, s32[8,24]{1,0:T(8,128)} %copy-done.12, bf16[64,2048]{1,0:T(8,128)(2,1)} %signals.1, bf16[8,64,256]{2,1,0:T(8,128)(2,1)} %basis_in.3, bf16[8,64,64]{2,1,0:T(8,128)(2,1)} %refs_12_.1), custom_call_target="tpu_custom_call" | custom-call | flops 30000000 | bytes 700000 | tf_op jit(solution)/shard_map/upward/pallas_call | solution.py:135
  8.3 0.4 collective-permute-start.1
  8.7 8.2 %all-to-all-start = ((bf16[8,8,32,128]{3,2,1,0:T(8,128)(2,1)}), bf16[8,8,32,128]{3,2,1,0:T(8,128)(2,1)S(1)}, u32[]{:S(2)}, u32[]{:S(2)}) async-start(bf16[8,8,32,128]{3,2,1,0:T(8,128)(2,1)} %get-tuple-element.23), calls=%async_computation | async-start | bytes 1048576 | tf_op jit(solution)/shard_map/all_to_all | solution.py:385
  16.9 1.0 %fusion.1 = (bf16[64,1024]{1,0:T(8,128)(2,1)S(1)}, bf16[64,1024]{1,0:T(8,128)(2,1)S(1)}) fusion(bf16[64,2048]{1,0:T(8,128)(2,1)} %signals.1), kind=kLoop, calls=%fused_computation.17 | loop fusion | bytes 524288 | tf_op jit(solution)/shard_map/slice | solution.py:406
  17.9 0.0 collective-permute-done.1
  17.9 0.7 fusion
  18.6 2.7 %collective-permute-start.2 = (bf16[2,80,128]{2,1,0:T(8,128)(2,1)S(1)}, bf16[2,80,128]{2,1,0:T(8,128)(2,1)S(1)}, u32[]{:S(2)}, u32[]{:S(2)}) collective-permute-start(bf16[2,80,128]{2,1,0:T(8,128)(2,1)S(1)} %get-tuple-element.38), channel_id=1, source_target_pairs={{0,24},{2,26},{4,28},{6,30},{8,0},{10,2},{12,4},{14,6},{16,8},{18,... | collective-permute-start | bytes 122888 | tf_op jit(solution)/shard_map/ppermute | solution.py:390
  21.4 0.3 collective-permute-start.3
  21.7 0.7 collective-permute-start.4
  22.4 0.0 collective-permute-done.5.other
  22.4 2.8 %collective-permute-start.6 = (bf16[128,1024]{1,0:T(8,128)(2,1)S(1)}, bf16[128,1024]{1,0:T(8,128)(2,1)S(1)}, u32[]{:S(2)}, u32[]{:S(2)}) collective-permute-start(bf16[128,1024]{1,0:T(8,128)(2,1)S(1)} %pad_maximum_fusion), channel_id=1, source_target_pairs={{0,2},{2,4},{4,6},{6,8},{8,10},{10,12},{12,14},{14,16},{16,18},{18... | collective-permute-start | bytes 786440 | tf_op jit(solution)/shard_map/ppermute | solution.py:402
  25.3 0.1 collective-permute-start.7
  25.4 0.6 collective-permute-done.3
  26.0 0.4 collective-permute-done.4
  26.5 2.8 %collective-permute-start.8 = (bf16[16,32,128]{2,1,0:T(8,128)(2,1)S(1)}, bf16[16,32,128]{2,1,0:T(8,128)(2,1)S(1)}, u32[]{:S(2)}, u32[]{:S(2)}) collective-permute-start(bf16[16,32,128]{2,1,0:T(8,128)(2,1)S(1)} %bitcast.15), channel_id=1, source_target_pairs={{0,224},{2,226},{4,228},{6,230},{8,232},{10,234},{12,236},{14,238}... | collective-permute-start | bytes 393224 | tf_op jit(solution)/shard_map/ppermute | solution.py:398
  29.2 0.5 tables.1
  29.7 0.5 copy-done.10
  30.3 4.6 %all-to-all-done.planes = bf16[8,8,32,128]{3,2,1,0:T(8,128)(2,1)S(1)} async-done(((bf16[8,8,32,128]{3,2,1,0:T(8,128)(2,1)}), bf16[8,8,32,128]{3,2,1,0:T(8,128)(2,1)S(1)}, u32[]{:S(2)}, u32[]{:S(2)}) %all-to-all-start) | async-done | bytes 524320 | tf_op jit(solution)/shard_map/all_to_all | solution.py:385
  34.8 2.2 %select.1 = bf16[16,16,32,128]{3,2,1,0:T(8,128)(2,1)} custom-call(s32[16,128]{1,0:T(8,128)S(1)} %get-tuple-element.22.wanted, bf16[8,8,32,128]{3,2,1,0:T(8,128)(2,1)S(1)} %all-to-all-done.planes), custom_call_target="tpu_custom_call" | custom-call | flops 1000000 | bytes 2500000 | tf_op jit(solution)/shard_map/select/pallas_call | solution.py:172
  37.0 0.0 copy-start.1
  37.1 0.0 copy-start.6
  37.1 0.0 collective-permute-done.9.refs_2_
  37.1 6.6 %all-to-all-start.1 = ((bf16[16,16,32,128]{3,2,1,0:T(8,128)(2,1)}), bf16[16,16,32,128]{3,2,1,0:T(8,128)(2,1)}, u32[]{:S(2)}, u32[]{:S(2)}) async-start(bf16[16,16,32,128]{3,2,1,0:T(8,128)(2,1)} %select.1), calls=%async_computation.1 | async-start | bytes 4194304 | tf_op jit(solution)/shard_map/all_to_all | solution.py:412
  43.8 1.9 %collective-permute-start.11 = (bf16[16,32,128]{2,1,0:T(8,128)(2,1)S(1)}, bf16[16,32,128]{2,1,0:T(8,128)(2,1)S(1)}, u32[]{:S(2)}, u32[]{:S(2)}) collective-permute-start(bf16[16,32,128]{2,1,0:T(8,128)(2,1)S(1)} %collective-permute-done.8.refs_1_), channel_id=1, source_target_pairs={{0,224},{2,226},{4,228},{6,230},{8,232},{10,234},{12,236},{14,238}... | collective-permute-start | bytes 393224 | tf_op jit(solution)/shard_map/ppermute | solution.py:414
  45.7 0.0 copy-start
  45.7 2.2 %copy-done = bf16[8,4,256,256]{3,2,1,0:T(8,128)(2,1)S(1)} copy-done((bf16[8,4,256,256]{3,2,1,0:T(8,128)(2,1)S(1)}, bf16[8,4,256,256]{3,2,1,0:T(8,128)(2,1)}, u32[]{:S(2)}) %copy-start) | copy-done | bytes 4194328
  47.9 2.2 %near_field.1 = (f32[64,2048]{1,0:T(8,128)S(1)}, bf16[64,2048]{1,0:T(8,128)(2,1)S(1)}) custom-call(s32[8,8]{1,0:T(8,128)S(1)} %copy-done.6, bf16[64,2048]{1,0:T(8,128)(2,1)S(1)} %copy-done.1, bf16[64,2048]{1,0:T(8,128)(2,1)S(1)} %collective-permute-done.5.other, bf16[128,1024]{1,0:T(8,128)(2,1)S(1)} %collective-permute-done.6.before, ...), custom_call_target="tpu_custom_call" | custom-call | flops 600000000 | bytes 10000000 | tf_op jit(solution)/shard_map/near_field/pallas_call | solution.py:214
  50.2 1.3 %collective-permute-done.12.refs_4_ = bf16[16,32,128]{2,1,0:T(8,128)(2,1)S(1)} collective-permute-done((bf16[16,32,128]{2,1,0:T(8,128)(2,1)S(1)}, bf16[16,32,128]{2,1,0:T(8,128)(2,1)S(1)}, u32[]{:S(2)}, u32[]{:S(2)}) %collective-permute-start.12) | collective-permute-done | bytes 131104 | tf_op jit(solution)/shard_map/ppermute | solution.py:414
  51.5 1.5 %collective-permute-start.13 = (bf16[16,32,128]{2,1,0:T(8,128)(2,1)S(1)}, bf16[16,32,128]{2,1,0:T(8,128)(2,1)S(1)}, u32[]{:S(2)}, u32[]{:S(2)}) collective-permute-start(bf16[16,32,128]{2,1,0:T(8,128)(2,1)S(1)} %collective-permute-done.11.refs_3_), channel_id=1, source_target_pairs={{0,224},{2,226},{4,228},{6,230},{8,232},{10,234},{12,236},{14,238}... | collective-permute-start | bytes 393224 | tf_op jit(solution)/shard_map/ppermute | solution.py:418
  52.9 0.3 collective-permute-start.14
  53.2 2.4 %collective-permute-done.13.refs_5_ = bf16[16,32,128]{2,1,0:T(8,128)(2,1)S(1)} collective-permute-done((bf16[16,32,128]{2,1,0:T(8,128)(2,1)S(1)}, bf16[16,32,128]{2,1,0:T(8,128)(2,1)S(1)}, u32[]{:S(2)}, u32[]{:S(2)}) %collective-permute-start.13) | collective-permute-done | bytes 131104 | tf_op jit(solution)/shard_map/ppermute | solution.py:418
  55.7 2.9 %collective-permute-done.14.refs_6_ = bf16[16,32,128]{2,1,0:T(8,128)(2,1)S(1)} collective-permute-done((bf16[16,32,128]{2,1,0:T(8,128)(2,1)S(1)}, bf16[16,32,128]{2,1,0:T(8,128)(2,1)S(1)}, u32[]{:S(2)}, u32[]{:S(2)}) %collective-permute-start.14) | collective-permute-done | bytes 131104 | tf_op jit(solution)/shard_map/ppermute | solution.py:418
  58.7 2.0 %collective-permute-start.17 = (bf16[112,32,128]{2,1,0:T(8,128)(2,1)S(1)}, bf16[112,32,128]{2,1,0:T(8,128)(2,1)S(1)}, u32[]{:S(2)}, u32[]{:S(2)}) collective-permute-start(bf16[112,32,128]{2,1,0:T(8,128)(2,1)S(1)} %constant_dynamic-update-slice_fusion), channel_id=1, source_target_pairs={{0,2},{2,0},{4,6},{6,4},{8,10},{10,8},{12,14},{14,12},{16,18},{18,... | collective-permute-start | bytes 2752520 | tf_op jit(solution)/shard_map/ppermute | solution.py:422
  60.6 1.5 %collective-permute-start.16 = (bf16[8,32,128]{2,1,0:T(8,128)(2,1)S(1)}, bf16[8,32,128]{2,1,0:T(8,128)(2,1)S(1)}, u32[]{:S(2)}, u32[]{:S(2)}) collective-permute-start(bf16[8,32,128]{2,1,0:T(8,128)(2,1)S(1)} %slice.35), channel_id=1, source_target_pairs={{0,32},{2,34},{4,36},{6,38},{8,40},{10,42},{12,44},{14,46},{16,48}... | collective-permute-start | bytes 196616 | tf_op jit(solution)/shard_map/ppermute | solution.py:420
  62.1 1.0 %collective-permute-start.10 = (bf16[64,2048]{1,0:T(8,128)(2,1)S(1)}, bf16[64,2048]{1,0:T(8,128)(2,1)S(1)}, u32[]{:S(2)}, u32[]{:S(2)}) collective-permute-start(bf16[64,2048]{1,0:T(8,128)(2,1)S(1)} %get-tuple-element.27), channel_id=1, source_target_pairs={{0,1},{1,0},{2,3},{3,2},{4,5},{5,4},{6,7},{7,6},{8,9},{9,8},{10,11... | collective-permute-start | bytes 786440 | tf_op jit(solution)/shard_map/ppermute | solution.py:416
  63.1 1.2 %collective-permute-done.15.refs_7_ = bf16[8,32,128]{2,1,0:T(8,128)(2,1)S(1)} collective-permute-done((bf16[8,32,128]{2,1,0:T(8,128)(2,1)S(1)}, bf16[8,32,128]{2,1,0:T(8,128)(2,1)S(1)}, u32[]{:S(2)}, u32[]{:S(2)}) %collective-permute-start.15) | collective-permute-done | bytes 65568 | tf_op jit(solution)/shard_map/ppermute | solution.py:420
  64.4 1.3 %collective-permute-done.16.refs_8_ = bf16[8,32,128]{2,1,0:T(8,128)(2,1)S(1)} collective-permute-done((bf16[8,32,128]{2,1,0:T(8,128)(2,1)S(1)}, bf16[8,32,128]{2,1,0:T(8,128)(2,1)S(1)}, u32[]{:S(2)}, u32[]{:S(2)}) %collective-permute-start.16) | collective-permute-done | bytes 65568 | tf_op jit(solution)/shard_map/ppermute | solution.py:420
  65.7 0.9 %collective-permute-start.18 = (bf16[16,32,128]{2,1,0:T(8,128)(2,1)S(1)}, bf16[16,32,128]{2,1,0:T(8,128)(2,1)S(1)}, u32[]{:S(2)}, u32[]{:S(2)}) collective-permute-start(bf16[16,32,128]{2,1,0:T(8,128)(2,1)S(1)} %pad_maximum_fusion.5), channel_id=1, source_target_pairs={{0,2},{2,0},{4,6},{6,4},{8,10},{10,8},{12,14},{14,12},{16,18},{18,... | collective-permute-start | bytes 393224 | tf_op jit(solution)/shard_map/ppermute | solution.py:422
  66.6 1.0 %collective-permute-done.18.refs_10_ = bf16[16,32,128]{2,1,0:T(8,128)(2,1)S(1)} collective-permute-done((bf16[16,32,128]{2,1,0:T(8,128)(2,1)S(1)}, bf16[16,32,128]{2,1,0:T(8,128)(2,1)S(1)}, u32[]{:S(2)}, u32[]{:S(2)}) %collective-permute-start.18) | collective-permute-done | bytes 131104 | tf_op jit(solution)/shard_map/ppermute | solution.py:422
  67.6 3.8 %fields.1.descended_in = f32[8,64,64]{2,1,0:T(8,128)S(1)} custom-call(s32[8]{0:T(128)S(1)} %copy-done.7, s32[2,16]{1,0:T(2,128)S(1)} %copy-done.8, bf16[16,32,128]{2,1,0:T(8,128)(2,1)S(1)} %bitcast.18, bf16[16,32,128]{2,1,0:T(8,128)(2,1)S(1)} %collective-permute-done.8.refs_1_, bf16[16,32,128]{2,1,0:T(8,128)(2,1)S(1)} %collective-permute-done.9.refs_2_, ...), custom_call_target="tpu_custom_call" | custom-call | flops 50000000 | bytes 4000000 | tf_op jit(solution)/shard_map/fields/pallas_call | solution.py:271
  71.4 0.7 copy-done.2
  72.1 3.3 %collective-permute-done.10.near_in_in = bf16[64,2048]{1,0:T(8,128)(2,1)S(1)} collective-permute-done((bf16[64,2048]{1,0:T(8,128)(2,1)S(1)}, bf16[64,2048]{1,0:T(8,128)(2,1)S(1)}, u32[]{:S(2)}, u32[]{:S(2)}) %collective-permute-start.10) | collective-permute-done | bytes 262176 | tf_op jit(solution)/shard_map/ppermute | solution.py:416
  75.4 0.7 copy-done.11
  76.1 5.9 %downward.1 = bf16[64,2048]{1,0:T(8,128)(2,1)} custom-call(s32[1,256]{1,0:T(1,128)} %copy-done.10, bf16[256,32,128]{2,1,0:T(8,128)(2,1)} %bitcast.9.blocks_in, bf16[64,2048]{1,0:T(8,128)(2,1)} %copy-done.11, bf16[8,64,1536]{2,1,0:T(8,128)(2,1)} %coupling_in.1, f32[8,64,64]{2,1,0:T(8,128)} %copy-done.2, bf16[8,64,256]{2,1,0:T(8,128)(2,1)} %basis_in.3, ...), custom_call_target="tpu_custom_call" | custom-call | flops 150000000 | bytes 6000000 | tf_op jit(solution)/shard_map/downward/pallas_call | solution.py:342
  (44 shorter events, 0.3 us)
Async XLA Ops:
  0.0 4.3 %collective-permute-start = (s32[8,24]{1,0:T(8,128)}, s32[8,24]{1,0:T(8,128)S(1)}, u32[]{:S(2)}, u32[]{:S(2)}) collective-permute-start(s32[8,24]{1,0:T(8,128)} %own_list.1), channel_id=1, source_target_pairs={{0,2},{2,0},{4,6},{6,4},{8,10},{10,8},{12,14},{14,12},{16,18},{18,... | collective-permute-start | bytes 2312 | tf_op jit(solution)/shard_map/ppermute | solution.py:382
  3.2 19.2 %collective-permute-start.5 = (bf16[64,2048]{1,0:T(8,128)(2,1)}, bf16[64,2048]{1,0:T(8,128)(2,1)S(1)}, u32[]{:S(2)}, u32[]{:S(2)}) collective-permute-start(bf16[64,2048]{1,0:T(8,128)(2,1)} %signals.1), channel_id=1, source_target_pairs={{0,1},{1,0},{2,3},{3,2},{4,5},{5,4},{6,7},{7,6},{8,9},{9,8},{10,11... | collective-permute-start | bytes 786440 | tf_op jit(solution)/shard_map/ppermute | solution.py:381
  4.3 0.6 copy-start.12
  8.3 20.9 %copy-start.9 = (s32[1,256]{1,0:T(1,128)S(1)}, s32[1,256]{1,0:T(1,128)}, u32[]{:S(2)}) copy-start(s32[1,256]{1,0:T(1,128)} %get-tuple-element.20.own_row) | copy-start | bytes 3076
  8.3 9.6 %collective-permute-start.1 = (bf16[80,128]{1,0:T(8,128)(2,1)}, bf16[80,128]{1,0:T(8,128)(2,1)S(1)}, u32[]{:S(2)}, u32[]{:S(2)}) collective-permute-start(bf16[80,128]{1,0:T(8,128)(2,1)} %get-tuple-element.19), channel_id=1, source_target_pairs={{0,4},{2,6},{4,0},{6,2},{8,12},{10,14},{12,8},{14,10},{16,20},{18,... | collective-permute-start | bytes 61448 | tf_op jit(solution)/shard_map/ppermute | solution.py:386
  8.7 26.1 %all-to-all-start = ((bf16[8,8,32,128]{3,2,1,0:T(8,128)(2,1)}), bf16[8,8,32,128]{3,2,1,0:T(8,128)(2,1)S(1)}, u32[]{:S(2)}, u32[]{:S(2)}) async-start(bf16[8,8,32,128]{3,2,1,0:T(8,128)(2,1)} %get-tuple-element.23), calls=%async_computation | async-start | bytes 1048576 | tf_op jit(solution)/shard_map/all_to_all | solution.py:385
  18.6 6.7 %collective-permute-start.2 = (bf16[2,80,128]{2,1,0:T(8,128)(2,1)S(1)}, bf16[2,80,128]{2,1,0:T(8,128)(2,1)S(1)}, u32[]{:S(2)}, u32[]{:S(2)}) collective-permute-start(bf16[2,80,128]{2,1,0:T(8,128)(2,1)S(1)} %get-tuple-element.38), channel_id=1, source_target_pairs={{0,24},{2,26},{4,28},{6,30},{8,0},{10,2},{12,4},{14,6},{16,8},{18,... | collective-permute-start | bytes 122888 | tf_op jit(solution)/shard_map/ppermute | solution.py:390
  21.4 4.7 %collective-permute-start.3 = (bf16[2,80,128]{2,1,0:T(8,128)(2,1)S(1)}, bf16[2,80,128]{2,1,0:T(8,128)(2,1)S(1)}, u32[]{:S(2)}, u32[]{:S(2)}) collective-permute-start(bf16[2,80,128]{2,1,0:T(8,128)(2,1)S(1)} %get-tuple-element.38), channel_id=1, source_target_pairs={{0,16},{2,18},{4,20},{6,22},{8,24},{10,26},{12,28},{14,30},{16,0},... | collective-permute-start | bytes 122888 | tf_op jit(solution)/shard_map/ppermute | solution.py:390
  21.7 4.7 %collective-permute-start.4 = (bf16[2,80,128]{2,1,0:T(8,128)(2,1)S(1)}, bf16[2,80,128]{2,1,0:T(8,128)(2,1)S(1)}, u32[]{:S(2)}, u32[]{:S(2)}) collective-permute-start(bf16[2,80,128]{2,1,0:T(8,128)(2,1)S(1)} %get-tuple-element.38), channel_id=1, source_target_pairs={{0,8},{2,10},{4,12},{6,14},{8,16},{10,18},{12,20},{14,22},{16,24},... | collective-permute-start | bytes 122888 | tf_op jit(solution)/shard_map/ppermute | solution.py:390
  22.4 14.6 %collective-permute-start.6 = (bf16[128,1024]{1,0:T(8,128)(2,1)S(1)}, bf16[128,1024]{1,0:T(8,128)(2,1)S(1)}, u32[]{:S(2)}, u32[]{:S(2)}) collective-permute-start(bf16[128,1024]{1,0:T(8,128)(2,1)S(1)} %pad_maximum_fusion), channel_id=1, source_target_pairs={{0,2},{2,4},{4,6},{6,8},{8,10},{10,12},{12,14},{14,16},{16,18},{18... | collective-permute-start | bytes 786440 | tf_op jit(solution)/shard_map/ppermute | solution.py:402
  25.3 11.8 %collective-permute-start.7 = (bf16[128,1024]{1,0:T(8,128)(2,1)S(1)}, bf16[128,1024]{1,0:T(8,128)(2,1)S(1)}, u32[]{:S(2)}, u32[]{:S(2)}) collective-permute-start(bf16[128,1024]{1,0:T(8,128)(2,1)S(1)} %pad_maximum_fusion.1), channel_id=1, source_target_pairs={{2,0},{4,2},{6,4},{8,6},{10,8},{12,10},{14,12},{16,14},{18,16},{20... | collective-permute-start | bytes 786440 | tf_op jit(solution)/shard_map/ppermute | solution.py:405
  26.5 10.6 %collective-permute-start.8 = (bf16[16,32,128]{2,1,0:T(8,128)(2,1)S(1)}, bf16[16,32,128]{2,1,0:T(8,128)(2,1)S(1)}, u32[]{:S(2)}, u32[]{:S(2)}) collective-permute-start(bf16[16,32,128]{2,1,0:T(8,128)(2,1)S(1)} %bitcast.15), channel_id=1, source_target_pairs={{0,224},{2,226},{4,228},{6,230},{8,232},{10,234},{12,236},{14,238}... | collective-permute-start | bytes 393224 | tf_op jit(solution)/shard_map/ppermute | solution.py:398
  29.2 7.9 %collective-permute-start.9 = (bf16[16,32,128]{2,1,0:T(8,128)(2,1)S(1)}, bf16[16,32,128]{2,1,0:T(8,128)(2,1)S(1)}, u32[]{:S(2)}, u32[]{:S(2)}) collective-permute-start(bf16[16,32,128]{2,1,0:T(8,128)(2,1)S(1)} %bitcast.16), channel_id=1, source_target_pairs={{0,32},{2,34},{4,36},{6,38},{8,40},{10,42},{12,44},{14,46},{16,48}... | collective-permute-start | bytes 393224 | tf_op jit(solution)/shard_map/ppermute | solution.py:398
  29.7 0.5 copy-start.10
  37.0 8.6 %copy-start.1 = (bf16[64,2048]{1,0:T(8,128)(2,1)S(1)}, bf16[64,2048]{1,0:T(8,128)(2,1)}, u32[]{:S(2)}) copy-start(bf16[64,2048]{1,0:T(8,128)(2,1)} %signals.1) | copy-start | bytes 786436
  37.1 8.6 %copy-start.6 = (s32[8,8]{1,0:T(8,128)S(1)}, s32[8,8]{1,0:T(8,128)}, u32[]{:S(2)}) copy-start(s32[8,8]{1,0:T(8,128)} %near_list.1) | copy-start | bytes 772
  37.1 38.3 %all-to-all-start.1 = ((bf16[16,16,32,128]{3,2,1,0:T(8,128)(2,1)}), bf16[16,16,32,128]{3,2,1,0:T(8,128)(2,1)}, u32[]{:S(2)}, u32[]{:S(2)}) async-start(bf16[16,16,32,128]{3,2,1,0:T(8,128)(2,1)} %select.1), calls=%async_computation.1 | async-start | bytes 4194304 | tf_op jit(solution)/shard_map/all_to_all | solution.py:412
  43.8 6.4 %collective-permute-start.11 = (bf16[16,32,128]{2,1,0:T(8,128)(2,1)S(1)}, bf16[16,32,128]{2,1,0:T(8,128)(2,1)S(1)}, u32[]{:S(2)}, u32[]{:S(2)}) collective-permute-start(bf16[16,32,128]{2,1,0:T(8,128)(2,1)S(1)} %collective-permute-done.8.refs_1_), channel_id=1, source_target_pairs={{0,224},{2,226},{4,228},{6,230},{8,232},{10,234},{12,236},{14,238}... | collective-permute-start | bytes 393224 | tf_op jit(solution)/shard_map/ppermute | solution.py:414
  45.6 5.8 %collective-permute-start.12 = (bf16[16,32,128]{2,1,0:T(8,128)(2,1)S(1)}, bf16[16,32,128]{2,1,0:T(8,128)(2,1)S(1)}, u32[]{:S(2)}, u32[]{:S(2)}) collective-permute-start(bf16[16,32,128]{2,1,0:T(8,128)(2,1)S(1)} %collective-permute-done.9.refs_2_), channel_id=1, source_target_pairs={{0,32},{2,34},{4,36},{6,38},{8,40},{10,42},{12,44},{14,46},{16,48}... | collective-permute-start | bytes 393224 | tf_op jit(solution)/shard_map/ppermute | solution.py:414
  45.7 2.2 %copy-start = (bf16[8,4,256,256]{3,2,1,0:T(8,128)(2,1)S(1)}, bf16[8,4,256,256]{3,2,1,0:T(8,128)(2,1)}, u32[]{:S(2)}) copy-start(bf16[8,4,256,256]{3,2,1,0:T(8,128)(2,1)} %tiles.1) | copy-start | bytes 12582916
  47.9 19.7 %copy-start.3 = (bf16[8,64,64]{2,1,0:T(8,128)(2,1)S(1)}, bf16[8,64,64]{2,1,0:T(8,128)(2,1)}, u32[]{:S(2)}) copy-start(bf16[8,64,64]{2,1,0:T(8,128)(2,1)} %refs_12_.1) | copy-start | bytes 196612
  47.9 19.7 %copy-start.5 = (bf16[2,64,1024]{2,1,0:T(8,128)(2,1)S(1)}, bf16[2,64,1024]{2,1,0:T(8,128)(2,1)}, u32[]{:S(2)}) copy-start(bf16[2,64,1024]{2,1,0:T(8,128)(2,1)} %refs_11_.1) | copy-start | bytes 786436
  47.9 19.7 %copy-start.7 = (s32[8]{0:T(128)S(1)}, s32[8]{0:T(128)}, u32[]{:S(2)}) copy-start(s32[8]{0:T(128)} %parent.3) | copy-start | bytes 100
  47.9 19.7 %copy-start.8 = (s32[2,16]{1,0:T(2,128)S(1)}, s32[2,16]{1,0:T(2,128)}, u32[]{:S(2)}) copy-start(s32[2,16]{1,0:T(2,128)} %parent_far.1) | copy-start | bytes 388
  50.1 17.4 %copy-start.4 = (f32[64,2048]{1,0:T(8,128)}, f32[64,2048]{1,0:T(8,128)S(1)}, u32[]{:S(2)}) copy-start(f32[64,2048]{1,0:T(8,128)S(1)} %get-tuple-element.32.near_own_in) | copy-start | bytes 1572868
  51.5 4.2 %collective-permute-start.13 = (bf16[16,32,128]{2,1,0:T(8,128)(2,1)S(1)}, bf16[16,32,128]{2,1,0:T(8,128)(2,1)S(1)}, u32[]{:S(2)}, u32[]{:S(2)}) collective-permute-start(bf16[16,32,128]{2,1,0:T(8,128)(2,1)S(1)} %collective-permute-done.11.refs_3_), channel_id=1, source_target_pairs={{0,224},{2,226},{4,228},{6,230},{8,232},{10,234},{12,236},{14,238}... | collective-permute-start | bytes 393224 | tf_op jit(solution)/shard_map/ppermute | solution.py:418
  52.9 5.7 %collective-permute-start.14 = (bf16[16,32,128]{2,1,0:T(8,128)(2,1)S(1)}, bf16[16,32,128]{2,1,0:T(8,128)(2,1)S(1)}, u32[]{:S(2)}, u32[]{:S(2)}) collective-permute-start(bf16[16,32,128]{2,1,0:T(8,128)(2,1)S(1)} %collective-permute-done.12.refs_4_), channel_id=1, source_target_pairs={{0,32},{2,34},{4,36},{6,38},{8,40},{10,42},{12,44},{14,46},{16,48}... | collective-permute-start | bytes 393224 | tf_op jit(solution)/shard_map/ppermute | solution.py:418
  58.7 8.9 %collective-permute-start.17 = (bf16[112,32,128]{2,1,0:T(8,128)(2,1)S(1)}, bf16[112,32,128]{2,1,0:T(8,128)(2,1)S(1)}, u32[]{:S(2)}, u32[]{:S(2)}) collective-permute-start(bf16[112,32,128]{2,1,0:T(8,128)(2,1)S(1)} %constant_dynamic-update-slice_fusion), channel_id=1, source_target_pairs={{0,2},{2,0},{4,6},{6,4},{8,10},{10,8},{12,14},{14,12},{16,18},{18,... | collective-permute-start | bytes 2752520 | tf_op jit(solution)/shard_map/ppermute | solution.py:422
  60.6 3.8 %collective-permute-start.15 = (bf16[8,32,128]{2,1,0:T(8,128)(2,1)S(1)}, bf16[8,32,128]{2,1,0:T(8,128)(2,1)S(1)}, u32[]{:S(2)}, u32[]{:S(2)}) collective-permute-start(bf16[8,32,128]{2,1,0:T(8,128)(2,1)S(1)} %slice.34), channel_id=1, source_target_pairs={{0,224},{2,226},{4,228},{6,230},{8,232},{10,234},{12,236},{14,238}... | collective-permute-start | bytes 196616 | tf_op jit(solution)/shard_map/ppermute | solution.py:420
  60.6 5.1 %collective-permute-start.16 = (bf16[8,32,128]{2,1,0:T(8,128)(2,1)S(1)}, bf16[8,32,128]{2,1,0:T(8,128)(2,1)S(1)}, u32[]{:S(2)}, u32[]{:S(2)}) collective-permute-start(bf16[8,32,128]{2,1,0:T(8,128)(2,1)S(1)} %slice.35), channel_id=1, source_target_pairs={{0,32},{2,34},{4,36},{6,38},{8,40},{10,42},{12,44},{14,46},{16,48}... | collective-permute-start | bytes 196616 | tf_op jit(solution)/shard_map/ppermute | solution.py:420
  62.1 13.3 %collective-permute-start.10 = (bf16[64,2048]{1,0:T(8,128)(2,1)S(1)}, bf16[64,2048]{1,0:T(8,128)(2,1)S(1)}, u32[]{:S(2)}, u32[]{:S(2)}) collective-permute-start(bf16[64,2048]{1,0:T(8,128)(2,1)S(1)} %get-tuple-element.27), channel_id=1, source_target_pairs={{0,1},{1,0},{2,3},{3,2},{4,5},{5,4},{6,7},{7,6},{8,9},{9,8},{10,11... | collective-permute-start | bytes 786440 | tf_op jit(solution)/shard_map/ppermute | solution.py:416
  65.7 1.8 %collective-permute-start.18 = (bf16[16,32,128]{2,1,0:T(8,128)(2,1)S(1)}, bf16[16,32,128]{2,1,0:T(8,128)(2,1)S(1)}, u32[]{:S(2)}, u32[]{:S(2)}) collective-permute-start(bf16[16,32,128]{2,1,0:T(8,128)(2,1)S(1)} %pad_maximum_fusion.5), channel_id=1, source_target_pairs={{0,2},{2,0},{4,6},{6,4},{8,10},{10,8},{12,14},{14,12},{16,18},{18,... | collective-permute-start | bytes 393224 | tf_op jit(solution)/shard_map/ppermute | solution.py:422
  71.4 0.7 copy-start.2
  75.4 0.7 copy-start.11

commit v4 on v3

--- a/solution.py
+++ b/solution.py
@@ -56,7 +56,7 @@
     return pl.CostEstimate(flops=flops, bytes_accessed=moved, transcendentals=0)
 
 
-def tables_kernel(lists, own_row, wanted_out, slot_out):
+def tables_kernel(lists, wanted_out):
     own = lax.axis_index("loop") % PLANE
     count = 2 * lists.shape[2]
     devices = jnp.concatenate([lists[0], lists[1]], axis=1)
@@ -73,29 +73,18 @@
             member = jnp.sum(jnp.where(flat == at, members, 0), axis=1, keepdims=True)
             table = jnp.where(lane == z * 2 + k, member, table)
     wanted_out[...] = table
-    row = own_row[...]
-    size = row.shape[1]
-    at_col = lax.broadcasted_iota(jnp.int32, (size, size), 0)
-    at_row = lax.broadcasted_iota(jnp.int32, (size, size), 1)
-    column = jnp.sum(jnp.where(at_col == at_row, row, 0), axis=1, keepdims=True)
-    earlier = jnp.where((column == row) & (at_col < at_row), 1, 0)
-    seen = jnp.sum(earlier, axis=0, keepdims=True)
-    slot_out[...] = row % PLANE * (2 * Z) + row // PLANE * 2 + seen
-
-
-def tables(lists, own_row):
+
+
+def tables(lists):
     return pl.pallas_call(
         tables_kernel,
-        out_shape=(
-            jax.ShapeDtypeStruct((PLANE, 128), jnp.int32),
-            jax.ShapeDtypeStruct(own_row.shape, jnp.int32),
-        ),
-        in_specs=[VMEM_SPEC] * 2,
-        out_specs=(VMEM_SPEC, VMEM_SPEC),
+        out_shape=jax.ShapeDtypeStruct((PLANE, 128), jnp.int32),
+        in_specs=[VMEM_SPEC],
+        out_specs=VMEM_SPEC,
         compiler_params=pltpu.CompilerParams(vmem_limit_bytes=8 * MIB),
         cost_estimate=cost(2_000_000, 20_000),
         name="tables",
-    )(lists, own_row)
+    )(lists)
 
 
 def upward_kernel(
@@ -181,7 +170,9 @@
     )(wanted, planes)
 
 
-def near_kernel(near_list, signals, other, before, after, tiles, own_out, other_out, extended, sems):
+def near_kernel(
+    near_list, own_row, signals, other, before, after, tiles, own_out, other_out, slot_out, extended, sems
+):
     half, width = signals.shape
     reach = before.shape[1]
     leaf_count, near_count, leaf_size, _ = tiles.shape
@@ -196,6 +187,14 @@
     )
     for copy in pending:
         copy.wait()
+    row = own_row[...]
+    size = row.shape[1]
+    at_col = lax.broadcasted_iota(jnp.int32, (size, size), 0)
+    at_row = lax.broadcasted_iota(jnp.int32, (size, size), 1)
+    column = jnp.sum(jnp.where(at_col == at_row, row, 0), axis=1, keepdims=True)
+    earlier = jnp.where((column == row) & (at_col < at_row), 1, 0)
+    seen = jnp.sum(earlier, axis=0, keepdims=True)
+    slot_out[...] = row % PLANE * (2 * Z) + row // PLANE * 2 + seen
     loop, rhs = lax.axis_index("loop"), lax.axis_index("rhs")
     leaves = leaf_count * Z * PLANE
     for t in range(leaf_count):
@@ -209,16 +208,17 @@
         other_out[:, t * leaf_size : (t + 1) * leaf_size] = total[half:].astype(jnp.bfloat16)
 
 
-def near_field(near_list, signals, other, before, after, tiles):
+def near_field(near_list, own_row, signals, other, before, after, tiles):
     half, width = signals.shape
     return pl.pallas_call(
         near_kernel,
         out_shape=(
             jax.ShapeDtypeStruct((half, width), jnp.float32),
             jax.ShapeDtypeStruct((half, width), jnp.bfloat16),
+            jax.ShapeDtypeStruct(own_row.shape, jnp.int32),
         ),
-        in_specs=[SMEM_SPEC, ANY_SPEC, ANY_SPEC, ANY_SPEC, ANY_SPEC, VMEM_SPEC],
-        out_specs=(VMEM_SPEC, VMEM_SPEC),
+        in_specs=[SMEM_SPEC, VMEM_SPEC, ANY_SPEC, ANY_SPEC, ANY_SPEC, ANY_SPEC, VMEM_SPEC],
+        out_specs=(VMEM_SPEC,) * 3,
         scratch_shapes=[
             pltpu.VMEM((2 * half, 2 * width), jnp.bfloat16),
             pltpu.SemaphoreType.DMA((4,)),
@@ -226,20 +226,16 @@
         compiler_params=pltpu.CompilerParams(vmem_limit_bytes=12 * MIB),
         cost_estimate=cost(600_000_000, 10_000_000),
         name="near_field",
-    )(near_list, signals, other, before, after, tiles)
+    )(near_list, own_row, signals, other, before, after, tiles)
 
 
 def fields_kernel(parent, parent_far, *refs):
     sources = refs[:11]
-    coupling_in, transfer_in, out, parents, coupling, transfer, sems = refs[11:]
-    copies = [(coupling_in, coupling), (transfer_in, transfer)]
+    coupling, transfer, out, parents = refs[11:]
     at = 0
     for ref in sources:
-        copies.append((ref, parents.at[at : at + ref.shape[0]]))
+        parents[at : at + ref.shape[0]] = ref[...]
         at += ref.shape[0]
-    pending = load(copies, sems)
-    for copy in pending:
-        copy.wait()
     me = lax.axis_index("loop")
     own_plane = me % PLANE
     per = 2 * Y * X
@@ -271,14 +267,9 @@
     return pl.pallas_call(
         fields_kernel,
         out_shape=jax.ShapeDtypeStruct(transfer.shape, jnp.float32),
-        in_specs=[SMEM_SPEC] * 2 + [ANY_SPEC] * 13,
+        in_specs=[SMEM_SPEC] * 2 + [VMEM_SPEC] * 13,
         out_specs=VMEM_SPEC,
-        scratch_shapes=[
-            pltpu.VMEM((2 * Z * Y * X * 2, 32, 128), jnp.bfloat16),
-            pltpu.VMEM(parent_coupling.shape, jnp.bfloat16),
-            pltpu.VMEM(transfer.shape, jnp.bfloat16),
-            pltpu.SemaphoreType.DMA((13,)),
-        ],
+        scratch_shapes=[pltpu.VMEM((2 * Z * Y * X * 2, 32, 128), jnp.bfloat16)],
         compiler_params=pltpu.CompilerParams(vmem_limit_bytes=16 * MIB),
         cost_estimate=cost(50_000_000, 4_000_000),
         name="fields",
@@ -288,14 +279,12 @@
 def downward_kernel(
     slots,
     blocks_in,
-    near_in_in,
     coupling_in,
     descended_in,
     basis_in,
     near_own_in,
     out_hbm,
     blocks,
-    near_in,
     coupling,
     descended,
     basis,
@@ -310,7 +299,7 @@
     pending = load(
         [(blocks_in.at[pl.ds(i * part, part)], blocks.at[pl.ds(i * part, part)]) for i in range(8)]
         + [(coupling_in.at[c], coupling.at[c]) for c in range(leaf_count)]
-        + [(descended_in, descended), (basis_in, basis), (near_own_in, near_own), (near_in_in, near_in)],
+        + [(descended_in, descended), (basis_in, basis), (near_own_in, near_own)],
         sems,
     )
     for copy in pending[:8]:
@@ -329,26 +318,26 @@
         combined = (leaf_far + descended[c]).astype(jnp.bfloat16)
         far_out = dot(combined, basis[c], TN)
         at = pl.ds(c * leaf_size, leaf_size)
-        out[:, at] = (near_own[:, at] + near_in[:, at].astype(jnp.float32) + far_out).astype(jnp.bfloat16)
+        out[:, at] = near_own[:, at] + far_out
         written.append(pltpu.make_async_copy(out.at[:, at], out_hbm.at[:, at], out_sems.at[c]))
         written[-1].start()
     for copy in written:
         copy.wait()
 
 
-def downward(slots, blocks, coupling, descended, basis, near_own, near_in):
-    arrays = (blocks, near_in, coupling, descended, basis, near_own)
+def downward(slots, blocks, coupling, descended, basis, near_own):
+    arrays = (blocks, coupling, descended, basis, near_own)
     leaf_count = basis.shape[0]
     return pl.pallas_call(
         downward_kernel,
-        out_shape=jax.ShapeDtypeStruct(near_own.shape, jnp.bfloat16),
-        in_specs=[SMEM_SPEC] + [ANY_SPEC] * 6,
+        out_shape=jax.ShapeDtypeStruct(near_own.shape, jnp.float32),
+        in_specs=[SMEM_SPEC] + [ANY_SPEC] * 5,
         out_specs=ANY_SPEC,
         scratch_shapes=[pltpu.VMEM(a.shape, a.dtype) for a in arrays]
         + [
             pltpu.VMEM((leaf_count, coupling.shape[2], 128), jnp.bfloat16),
-            pltpu.VMEM(near_own.shape, jnp.bfloat16),
-            pltpu.SemaphoreType.DMA((12 + leaf_count,)),
+            pltpu.VMEM(near_own.shape, jnp.float32),
+            pltpu.SemaphoreType.DMA((11 + leaf_count,)),
             pltpu.SemaphoreType.DMA((leaf_count,)),
         ],
         compiler_params=pltpu.CompilerParams(vmem_limit_bytes=62 * MIB),
@@ -405,14 +394,14 @@
     after = along(
         jnp.concatenate([signals[:, :reach], other[:, :reach]]), perm=[((i + 1) % count, i) for i in range(count)]
     )
-    wanted, slots = tables(plane_lists.astype(jnp.int32), own_row)
+    wanted = tables(plane_lists.astype(jnp.int32))
     send, before, after, one_down, one_up = lax.optimization_barrier(
         (select(wanted, planes), before, after, one_down, one_up)
     )
     blocks = lax.all_to_all(send, "loop", 0, 0, tiled=True, axis_index_groups=planes_of)
 
     two_down, two_up = down(one_down), up(one_up)
-    near_own, near_other = near_field(near_list, signals, other, before, after, near_tiles)
+    near_own, near_other, slots = near_field(near_list, own_row, signals, other, before, after, near_tiles)
     near_in = swap(near_other)
     _, two_down, two_up = lax.optimization_barrier((near_other, two_down, two_up))
     three_down, three_up = down(two_down), up(two_up)
@@ -422,7 +411,8 @@
     theirs = [along(jnp.concatenate(part), perm=c_swap) for part in (mine[:7], mine[7:])]
     descended = fields(parent, parent_far, mine + theirs, parent_coupling, transfer)
 
-    return downward(slots, blocks.reshape(-1, 32, 128), coupling, descended, leaf_basis, near_own, near_in)
+    partial = downward(slots, blocks.reshape(-1, 32, 128), coupling, descended, leaf_basis, near_own)
+    return (partial + near_in.astype(jnp.float32)).astype(jnp.bfloat16)
 
 
 def solution(mesh):

time: 82.6 us -> 79.2 us (0.959)
  Pallas kernels: 18.1 us -> 16 us
  other arithmetic: 0.8 us -> 2.61 us
  waiting for transfers between devices: 19.2 us -> 17.4 us
  local copies, waits for them, and re-layouts: 5.89 us -> 4.65 us
    ppermute x1, waiting for transfers between devices: 3.26 us -> 0.01 us  [shards(): near_in = swap(near_other)]
    pallas_call x1, Pallas kernels: 3.82 us -> 1.81 us  [fields(): pl.pallas_call(fields_kernel, out_shape=jax.ShapeDtypeStruct(transfer.sha...]
    convert_element_type x1 -> x2, other arithmetic: 0.01 us -> 1.81 us  [the longest x1 1.8 us: shards(): return (partial + near_in.astype(jnp.float32)).astype(jnp.bfloat16)]
    unnamed x32 -> x30, local copies, waits for them, and re-layouts: 4.86 us -> 3.61 us
    all_to_all x1, waiting for transfers between devices: 0.01 us -> 0.92 us  [shards(): lax.all_to_all(send, 'loop', 0, 0, tiled=True, axis_index_groups=planes_of)]
  transfers between devices with their start and end apart: 21 -> 21, of which waited for: 10 -> 10; matrix products, arithmetic and copies ran while one was open for 2% -> 2% of each run, Pallas kernels for 15% -> 20%
where the time goes in v4:
time: 79.2 us; the launch traced here: 78.8 us
  starting transfers between devices  37.8 us (48%)
  waiting for transfers between devices  17.4 us (22%)
  Pallas kernels  16 us (20%)
  local copies, waits for them, and re-layouts  4.65 us (6%)
  other arithmetic  2.61 us (3%)
    all_to_all x1, starting transfers between devices, shards(): lax.all_to_all(coefs, 'loop', 0, 0, tiled=True, axis_index_groups=columns...  8.19 us
    all_to_all x1, starting transfers between devices, shards(): lax.all_to_all(send, 'loop', 0, 0, tiled=True, axis_index_groups=planes_of)  6.64 us
    pallas_call x1, Pallas kernels, downward(): pl.pallas_call(downward_kernel, out_shape=jax.ShapeDtypeStruct(near_own.s...  5.88 us
    ppermute x2, waiting for transfers between devices, shards(): three_down, three_up = (down(two_down), up(two_up))  5.37 us
    all_to_all x1, waiting for transfers between devices, shards(): lax.all_to_all(coefs, 'loop', 0, 0, tiled=True, axis_index_groups=columns...  5.16 us
    ppermute x3, starting transfers between devices, shards(): along(pair, perm=loop_moves(lambda z, y, x, c, dy=dy: (z, y - dy, x, c)))  3.77 us
    unnamed x30, local copies, waits for them, and re-layouts  3.61 us
    pallas_call x1, Pallas kernels, upward(): pl.pallas_call(upward_kernel, out_shape=(jax.ShapeDtypeStruct((Z, leaf_co...  3.45 us
  transfers between devices with their start and end apart: 21, of which 10 were waited for; matrix products, arithmetic and copies ran while one was open for 2% of the time, Pallas kernels for 20%

profile of v4, /device:TPU:1, one launch (start us, length us, event | category | flops | bytes accessed | tf_op | source)
XLA Modules:
  0.0 78.8 jit_solution(16379242270407512178)
XLA Ops:
  0.0 3.2 %collective-permute-start = (s32[8,24]{1,0:T(8,128)}, s32[8,24]{1,0:T(8,128)S(1)}, u32[]{:S(2)}, u32[]{:S(2)}) collective-permute-start(s32[8,24]{1,0:T(8,128)} %own_list.1), channel_id=1, source_target_pairs={{0,2},{2,0},{4,6},{6,4},{8,10},{10,8},{12,14},{14,12},{16,18},{18,... | collective-permute-start | bytes 2312 | tf_op jit(solution)/shard_map/ppermute | solution.py:371
  3.2 1.0 %collective-permute-start.1 = (bf16[64,2048]{1,0:T(8,128)(2,1)}, bf16[64,2048]{1,0:T(8,128)(2,1)S(1)}, u32[]{:S(2)}, u32[]{:S(2)}) collective-permute-start(bf16[64,2048]{1,0:T(8,128)(2,1)} %signals.1), channel_id=1, source_target_pairs={{0,1},{1,0},{2,3},{3,2},{4,5},{5,4},{6,7},{7,6},{8,9},{9,8},{10,11... | collective-permute-start | bytes 786440 | tf_op jit(solution)/shard_map/ppermute | solution.py:370
  4.2 0.0 collective-permute-done.peer_list
  4.3 0.6 copy-done.11
  4.9 3.4 %upward.1 = (bf16[8,8,32,128]{3,2,1,0:T(8,128)(2,1)}, bf16[80,128]{1,0:T(8,128)(2,1)}, s32[1,256]{1,0:T(1,128)}) custom-call(s32[8]{0:T(128)} %parent.3, s32[8,24]{1,0:T(8,128)} %own_list.1, s32[8,24]{1,0:T(8,128)} %copy-done.11, bf16[64,2048]{1,0:T(8,128)(2,1)} %signals.1, bf16[8,64,256]{2,1,0:T(8,128)(2,1)} %basis_in.3, bf16[8,64,64]{2,1,0:T(8,128)(2,1)} %refs_12_.1), custom_call_target="tpu_custom_call" | custom-call | flops 30000000 | bytes 700000 | tf_op jit(solution)/shard_map/upward/pallas_call | solution.py:124
  8.3 0.4 collective-permute-start.2
  8.7 8.2 %all-to-all-start = ((bf16[8,8,32,128]{3,2,1,0:T(8,128)(2,1)}), bf16[8,8,32,128]{3,2,1,0:T(8,128)(2,1)S(1)}, u32[]{:S(2)}, u32[]{:S(2)}) async-start(bf16[8,8,32,128]{3,2,1,0:T(8,128)(2,1)} %get-tuple-element.20), calls=%async_computation | async-start | bytes 1048576 | tf_op jit(solution)/shard_map/all_to_all | solution.py:374
  16.9 1.0 %fusion.1 = (bf16[64,1024]{1,0:T(8,128)(2,1)S(1)}, bf16[64,1024]{1,0:T(8,128)(2,1)S(1)}) fusion(bf16[64,2048]{1,0:T(8,128)(2,1)} %signals.1), kind=kLoop, calls=%fused_computation.18 | loop fusion | bytes 524288 | tf_op jit(solution)/shard_map/slice | solution.py:395
  17.9 0.0 collective-permute-done.2
  17.9 0.7 fusion
  18.6 2.7 %collective-permute-start.3 = (bf16[2,80,128]{2,1,0:T(8,128)(2,1)S(1)}, bf16[2,80,128]{2,1,0:T(8,128)(2,1)S(1)}, u32[]{:S(2)}, u32[]{:S(2)}) collective-permute-start(bf16[2,80,128]{2,1,0:T(8,128)(2,1)S(1)} %get-tuple-element.36), channel_id=1, source_target_pairs={{0,24},{2,26},{4,28},{6,30},{8,0},{10,2},{12,4},{14,6},{16,8},{18,... | collective-permute-start | bytes 122888 | tf_op jit(solution)/shard_map/ppermute | solution.py:379
  21.4 0.3 collective-permute-start.4
  21.7 0.7 collective-permute-start.5
  22.4 0.0 collective-permute-done.1.other
  22.5 2.8 %collective-permute-start.6 = (bf16[128,1024]{1,0:T(8,128)(2,1)S(1)}, bf16[128,1024]{1,0:T(8,128)(2,1)S(1)}, u32[]{:S(2)}, u32[]{:S(2)}) collective-permute-start(bf16[128,1024]{1,0:T(8,128)(2,1)S(1)} %pad_maximum_fusion), channel_id=1, source_target_pairs={{0,2},{2,4},{4,6},{6,8},{8,10},{10,12},{12,14},{14,16},{16,18},{18... | collective-permute-start | bytes 786440 | tf_op jit(solution)/shard_map/ppermute | solution.py:391
  25.3 0.1 collective-permute-start.7
  25.4 0.6 collective-permute-done.4
  26.0 0.4 collective-permute-done.5
  26.5 2.8 %collective-permute-start.8 = (bf16[16,32,128]{2,1,0:T(8,128)(2,1)S(1)}, bf16[16,32,128]{2,1,0:T(8,128)(2,1)S(1)}, u32[]{:S(2)}, u32[]{:S(2)}) collective-permute-start(bf16[16,32,128]{2,1,0:T(8,128)(2,1)S(1)} %bitcast.15), channel_id=1, source_target_pairs={{0,224},{2,226},{4,228},{6,230},{8,232},{10,234},{12,236},{14,238}... | collective-permute-start | bytes 393224 | tf_op jit(solution)/shard_map/ppermute | solution.py:387
  29.2 0.4 tables.1.wanted
  29.7 5.2 %all-to-all-done.planes = bf16[8,8,32,128]{3,2,1,0:T(8,128)(2,1)S(1)} async-done(((bf16[8,8,32,128]{3,2,1,0:T(8,128)(2,1)}), bf16[8,8,32,128]{3,2,1,0:T(8,128)(2,1)S(1)}, u32[]{:S(2)}, u32[]{:S(2)}) %all-to-all-start) | async-done | bytes 524320 | tf_op jit(solution)/shard_map/all_to_all | solution.py:374
  34.8 2.2 %select.1 = bf16[16,16,32,128]{3,2,1,0:T(8,128)(2,1)} custom-call(s32[16,128]{1,0:T(8,128)S(1)} %tables.1.wanted, bf16[8,8,32,128]{3,2,1,0:T(8,128)(2,1)S(1)} %all-to-all-done.planes), custom_call_target="tpu_custom_call" | custom-call | flops 1000000 | bytes 2500000 | tf_op jit(solution)/shard_map/select/pallas_call | solution.py:161
  37.0 0.0 copy-start.1
  37.0 0.0 copy-start.6
  37.1 0.0 collective-permute-done.8.refs_1_
  37.1 6.6 %all-to-all-start.1 = ((bf16[16,16,32,128]{3,2,1,0:T(8,128)(2,1)}), bf16[16,16,32,128]{3,2,1,0:T(8,128)(2,1)}, u32[]{:S(2)}, u32[]{:S(2)}) async-start(bf16[16,16,32,128]{3,2,1,0:T(8,128)(2,1)} %select.1), calls=%async_computation.1 | async-start | bytes 4194304 | tf_op jit(solution)/shard_map/all_to_all | solution.py:401
  43.8 1.9 %collective-permute-start.10 = (bf16[16,32,128]{2,1,0:T(8,128)(2,1)S(1)}, bf16[16,32,128]{2,1,0:T(8,128)(2,1)S(1)}, u32[]{:S(2)}, u32[]{:S(2)}) collective-permute-start(bf16[16,32,128]{2,1,0:T(8,128)(2,1)S(1)} %collective-permute-done.8.refs_1_), channel_id=1, source_target_pairs={{0,224},{2,226},{4,228},{6,230},{8,232},{10,234},{12,236},{14,238}... | collective-permute-start | bytes 393224 | tf_op jit(solution)/shard_map/ppermute | solution.py:403
  45.7 0.0 copy-start
  45.7 2.2 %copy-done = bf16[8,4,256,256]{3,2,1,0:T(8,128)(2,1)S(1)} copy-done((bf16[8,4,256,256]{3,2,1,0:T(8,128)(2,1)S(1)}, bf16[8,4,256,256]{3,2,1,0:T(8,128)(2,1)}, u32[]{:S(2)}) %copy-start) | copy-done | bytes 4194328
  47.9 2.2 %near_field.1 = (f32[64,2048]{1,0:T(8,128)S(1)}, bf16[64,2048]{1,0:T(8,128)(2,1)S(1)}, s32[1,256]{1,0:T(1,128)S(1)}) custom-call(s32[8,8]{1,0:T(8,128)S(1)} %copy-done.6, s32[1,256]{1,0:T(1,128)S(1)} %copy-done.9, bf16[64,2048]{1,0:T(8,128)(2,1)S(1)} %copy-done.1, bf16[64,2048]{1,0:T(8,128)(2,1)S(1)} %collective-permute-done.1.other, ...), custom_call_target="tpu_custom_call" | custom-call | flops 600000000 | bytes 10000000 | tf_op jit(solution)/shard_map/near_field/pallas_call | solution.py:213
  50.2 1.3 %collective-permute-done.11.refs_4_ = bf16[16,32,128]{2,1,0:T(8,128)(2,1)S(1)} collective-permute-done((bf16[16,32,128]{2,1,0:T(8,128)(2,1)S(1)}, bf16[16,32,128]{2,1,0:T(8,128)(2,1)S(1)}, u32[]{:S(2)}, u32[]{:S(2)}) %collective-permute-start.11) | collective-permute-done | bytes 131104 | tf_op jit(solution)/shard_map/ppermute | solution.py:403
  51.4 1.5 %collective-permute-start.12 = (bf16[16,32,128]{2,1,0:T(8,128)(2,1)S(1)}, bf16[16,32,128]{2,1,0:T(8,128)(2,1)S(1)}, u32[]{:S(2)}, u32[]{:S(2)}) collective-permute-start(bf16[16,32,128]{2,1,0:T(8,128)(2,1)S(1)} %collective-permute-done.10.refs_3_), channel_id=1, source_target_pairs={{0,224},{2,226},{4,228},{6,230},{8,232},{10,234},{12,236},{14,238}... | collective-permute-start | bytes 393224 | tf_op jit(solution)/shard_map/ppermute | solution.py:407
  53.0 0.3 collective-permute-start.13
  53.3 2.4 %collective-permute-done.12.refs_5_ = bf16[16,32,128]{2,1,0:T(8,128)(2,1)S(1)} collective-permute-done((bf16[16,32,128]{2,1,0:T(8,128)(2,1)S(1)}, bf16[16,32,128]{2,1,0:T(8,128)(2,1)S(1)}, u32[]{:S(2)}, u32[]{:S(2)}) %collective-permute-start.12) | collective-permute-done | bytes 131104 | tf_op jit(solution)/shard_map/ppermute | solution.py:407
  55.7 3.0 %collective-permute-done.13.refs_6_ = bf16[16,32,128]{2,1,0:T(8,128)(2,1)S(1)} collective-permute-done((bf16[16,32,128]{2,1,0:T(8,128)(2,1)S(1)}, bf16[16,32,128]{2,1,0:T(8,128)(2,1)S(1)}, u32[]{:S(2)}, u32[]{:S(2)}) %collective-permute-start.13) | collective-permute-done | bytes 131104 | tf_op jit(solution)/shard_map/ppermute | solution.py:407
  58.7 2.0 %collective-permute-start.16 = (bf16[112,32,128]{2,1,0:T(8,128)(2,1)S(1)}, bf16[112,32,128]{2,1,0:T(8,128)(2,1)S(1)}, u32[]{:S(2)}, u32[]{:S(2)}) collective-permute-start(bf16[112,32,128]{2,1,0:T(8,128)(2,1)S(1)} %constant_dynamic-update-slice_fusion), channel_id=1, source_target_pairs={{0,2},{2,0},{4,6},{6,4},{8,10},{10,8},{12,14},{14,12},{16,18},{18,... | collective-permute-start | bytes 2752520 | tf_op jit(solution)/shard_map/ppermute | solution.py:411
  60.7 1.5 %collective-permute-start.15 = (bf16[8,32,128]{2,1,0:T(8,128)(2,1)S(1)}, bf16[8,32,128]{2,1,0:T(8,128)(2,1)S(1)}, u32[]{:S(2)}, u32[]{:S(2)}) collective-permute-start(bf16[8,32,128]{2,1,0:T(8,128)(2,1)S(1)} %slice.35), channel_id=1, source_target_pairs={{0,32},{2,34},{4,36},{6,38},{8,40},{10,42},{12,44},{14,46},{16,48}... | collective-permute-start | bytes 196616 | tf_op jit(solution)/shard_map/ppermute | solution.py:409
  62.1 1.0 %collective-permute-start.18 = (bf16[64,2048]{1,0:T(8,128)(2,1)S(1)}, bf16[64,2048]{1,0:T(8,128)(2,1)S(1)}, u32[]{:S(2)}, u32[]{:S(2)}) collective-permute-start(bf16[64,2048]{1,0:T(8,128)(2,1)S(1)} %get-tuple-element.27), channel_id=1, source_target_pairs={{0,1},{1,0},{2,3},{3,2},{4,5},{5,4},{6,7},{7,6},{8,9},{9,8},{10,11... | collective-permute-start | bytes 786440 | tf_op jit(solution)/shard_map/ppermute | solution.py:405
  63.2 1.2 %collective-permute-done.14.refs_7_ = bf16[8,32,128]{2,1,0:T(8,128)(2,1)S(1)} collective-permute-done((bf16[8,32,128]{2,1,0:T(8,128)(2,1)S(1)}, bf16[8,32,128]{2,1,0:T(8,128)(2,1)S(1)}, u32[]{:S(2)}, u32[]{:S(2)}) %collective-permute-start.14) | collective-permute-done | bytes 65568 | tf_op jit(solution)/shard_map/ppermute | solution.py:409
  64.4 1.3 %collective-permute-done.15.refs_8_ = bf16[8,32,128]{2,1,0:T(8,128)(2,1)S(1)} collective-permute-done((bf16[8,32,128]{2,1,0:T(8,128)(2,1)S(1)}, bf16[8,32,128]{2,1,0:T(8,128)(2,1)S(1)}, u32[]{:S(2)}, u32[]{:S(2)}) %collective-permute-start.15) | collective-permute-done | bytes 65568 | tf_op jit(solution)/shard_map/ppermute | solution.py:409
  65.7 0.9 %collective-permute-start.17 = (bf16[16,32,128]{2,1,0:T(8,128)(2,1)S(1)}, bf16[16,32,128]{2,1,0:T(8,128)(2,1)S(1)}, u32[]{:S(2)}, u32[]{:S(2)}) collective-permute-start(bf16[16,32,128]{2,1,0:T(8,128)(2,1)S(1)} %pad_maximum_fusion.5), channel_id=1, source_target_pairs={{0,2},{2,0},{4,6},{6,4},{8,10},{10,8},{12,14},{14,12},{16,18},{18,... | collective-permute-start | bytes 393224 | tf_op jit(solution)/shard_map/ppermute | solution.py:411
  66.6 1.0 %collective-permute-done.17.refs_10_ = bf16[16,32,128]{2,1,0:T(8,128)(2,1)S(1)} collective-permute-done((bf16[16,32,128]{2,1,0:T(8,128)(2,1)S(1)}, bf16[16,32,128]{2,1,0:T(8,128)(2,1)S(1)}, u32[]{:S(2)}, u32[]{:S(2)}) %collective-permute-start.17) | collective-permute-done | bytes 131104 | tf_op jit(solution)/shard_map/ppermute | solution.py:411
  67.6 1.8 %fields.1.descended_in = f32[8,64,64]{2,1,0:T(8,128)S(1)} custom-call(s32[8]{0:T(128)S(1)} %copy-done.7, s32[2,16]{1,0:T(2,128)S(1)} %copy-done.8, bf16[16,32,128]{2,1,0:T(8,128)(2,1)S(1)} %bitcast.18, bf16[16,32,128]{2,1,0:T(8,128)(2,1)S(1)} %collective-permute-done.8.refs_1_, bf16[16,32,128]{2,1,0:T(8,128)(2,1)S(1)} %collective-permute-done.9.refs_2_, ...), custom_call_target="tpu_custom_call" | custom-call | flops 50000000 | bytes 4000000 | tf_op jit(solution)/shard_map/fields/pallas_call | solution.py:267
  69.4 0.0 copy-start.2
  69.4 0.7 copy-done.2
  70.1 0.9 %all-to-all-done.1 = bf16[16,16,32,128]{3,2,1,0:T(8,128)(2,1)} async-done(((bf16[16,16,32,128]{3,2,1,0:T(8,128)(2,1)}), bf16[16,16,32,128]{3,2,1,0:T(8,128)(2,1)}, u32[]{:S(2)}, u32[]{:S(2)}) %all-to-all-start.1) | async-done | bytes 2097184 | tf_op jit(solution)/shard_map/all_to_all | solution.py:401
  71.1 5.9 %downward.1 = f32[64,2048]{1,0:T(8,128)} custom-call(s32[1,256]{1,0:T(1,128)} %copy-done.10, bf16[256,32,128]{2,1,0:T(8,128)(2,1)} %bitcast.9.blocks_in, bf16[8,64,1536]{2,1,0:T(8,128)(2,1)} %coupling_in.1, f32[8,64,64]{2,1,0:T(8,128)} %copy-done.2, bf16[8,64,256]{2,1,0:T(8,128)(2,1)} %basis_in.3, f32[64,2048]{1,0:T(8,128)} %copy-done.4), custom_call_target="tpu_custom_call" | custom-call | flops 150000000 | bytes 6000000 | tf_op jit(solution)/shard_map/downward/pallas_call | solution.py:331
  77.0 1.8 %add_convert_fusion = bf16[64,2048]{1,0:T(8,128)(2,1)} fusion(f32[64,2048]{1,0:T(8,128)} %downward.1, bf16[64,2048]{1,0:T(8,128)(2,1)S(1)} %collective-permute-done.18), kind=kLoop, calls=%fused_computation | loop fusion | flops 393216 | bytes 1048576 | tf_op jit(solution)/shard_map/convert_element_type | solution.py:415
  (43 shorter events, 0.3 us)
Async XLA Ops:
  0.0 4.3 %collective-permute-start = (s32[8,24]{1,0:T(8,128)}, s32[8,24]{1,0:T(8,128)S(1)}, u32[]{:S(2)}, u32[]{:S(2)}) collective-permute-start(s32[8,24]{1,0:T(8,128)} %own_list.1), channel_id=1, source_target_pairs={{0,2},{2,0},{4,6},{6,4},{8,10},{10,8},{12,14},{14,12},{16,18},{18,... | collective-permute-start | bytes 2312 | tf_op jit(solution)/shard_map/ppermute | solution.py:371
  3.2 19.2 %collective-permute-start.1 = (bf16[64,2048]{1,0:T(8,128)(2,1)}, bf16[64,2048]{1,0:T(8,128)(2,1)S(1)}, u32[]{:S(2)}, u32[]{:S(2)}) collective-permute-start(bf16[64,2048]{1,0:T(8,128)(2,1)} %signals.1), channel_id=1, source_target_pairs={{0,1},{1,0},{2,3},{3,2},{4,5},{5,4},{6,7},{7,6},{8,9},{9,8},{10,11... | collective-permute-start | bytes 786440 | tf_op jit(solution)/shard_map/ppermute | solution.py:370
  4.3 0.6 copy-start.11
  8.3 9.6 %collective-permute-start.2 = (bf16[80,128]{1,0:T(8,128)(2,1)}, bf16[80,128]{1,0:T(8,128)(2,1)S(1)}, u32[]{:S(2)}, u32[]{:S(2)}) collective-permute-start(bf16[80,128]{1,0:T(8,128)(2,1)} %get-tuple-element.19), channel_id=1, source_target_pairs={{0,4},{2,6},{4,0},{6,2},{8,12},{10,14},{12,8},{14,10},{16,20},{18,... | collective-permute-start | bytes 61448 | tf_op jit(solution)/shard_map/ppermute | solution.py:375
  8.7 26.1 %all-to-all-start = ((bf16[8,8,32,128]{3,2,1,0:T(8,128)(2,1)}), bf16[8,8,32,128]{3,2,1,0:T(8,128)(2,1)S(1)}, u32[]{:S(2)}, u32[]{:S(2)}) async-start(bf16[8,8,32,128]{3,2,1,0:T(8,128)(2,1)} %get-tuple-element.20), calls=%async_computation | async-start | bytes 1048576 | tf_op jit(solution)/shard_map/all_to_all | solution.py:374
  18.6 6.7 %collective-permute-start.3 = (bf16[2,80,128]{2,1,0:T(8,128)(2,1)S(1)}, bf16[2,80,128]{2,1,0:T(8,128)(2,1)S(1)}, u32[]{:S(2)}, u32[]{:S(2)}) collective-permute-start(bf16[2,80,128]{2,1,0:T(8,128)(2,1)S(1)} %get-tuple-element.36), channel_id=1, source_target_pairs={{0,24},{2,26},{4,28},{6,30},{8,0},{10,2},{12,4},{14,6},{16,8},{18,... | collective-permute-start | bytes 122888 | tf_op jit(solution)/shard_map/ppermute | solution.py:379
  21.4 4.7 %collective-permute-start.4 = (bf16[2,80,128]{2,1,0:T(8,128)(2,1)S(1)}, bf16[2,80,128]{2,1,0:T(8,128)(2,1)S(1)}, u32[]{:S(2)}, u32[]{:S(2)}) collective-permute-start(bf16[2,80,128]{2,1,0:T(8,128)(2,1)S(1)} %get-tuple-element.36), channel_id=1, source_target_pairs={{0,16},{2,18},{4,20},{6,22},{8,24},{10,26},{12,28},{14,30},{16,0},... | collective-permute-start | bytes 122888 | tf_op jit(solution)/shard_map/ppermute | solution.py:379
  21.7 4.7 %collective-permute-start.5 = (bf16[2,80,128]{2,1,0:T(8,128)(2,1)S(1)}, bf16[2,80,128]{2,1,0:T(8,128)(2,1)S(1)}, u32[]{:S(2)}, u32[]{:S(2)}) collective-permute-start(bf16[2,80,128]{2,1,0:T(8,128)(2,1)S(1)} %get-tuple-element.36), channel_id=1, source_target_pairs={{0,8},{2,10},{4,12},{6,14},{8,16},{10,18},{12,20},{14,22},{16,24},... | collective-permute-start | bytes 122888 | tf_op jit(solution)/shard_map/ppermute | solution.py:379
  22.5 14.6 %collective-permute-start.6 = (bf16[128,1024]{1,0:T(8,128)(2,1)S(1)}, bf16[128,1024]{1,0:T(8,128)(2,1)S(1)}, u32[]{:S(2)}, u32[]{:S(2)}) collective-permute-start(bf16[128,1024]{1,0:T(8,128)(2,1)S(1)} %pad_maximum_fusion), channel_id=1, source_target_pairs={{0,2},{2,4},{4,6},{6,8},{8,10},{10,12},{12,14},{14,16},{16,18},{18... | collective-permute-start | bytes 786440 | tf_op jit(solution)/shard_map/ppermute | solution.py:391
  25.3 11.8 %collective-permute-start.7 = (bf16[128,1024]{1,0:T(8,128)(2,1)S(1)}, bf16[128,1024]{1,0:T(8,128)(2,1)S(1)}, u32[]{:S(2)}, u32[]{:S(2)}) collective-permute-start(bf16[128,1024]{1,0:T(8,128)(2,1)S(1)} %pad_maximum_fusion.1), channel_id=1, source_target_pairs={{2,0},{4,2},{6,4},{8,6},{10,8},{12,10},{14,12},{16,14},{18,16},{20... | collective-permute-start | bytes 786440 | tf_op jit(solution)/shard_map/ppermute | solution.py:394
  26.5 10.6 %collective-permute-start.8 = (bf16[16,32,128]{2,1,0:T(8,128)(2,1)S(1)}, bf16[16,32,128]{2,1,0:T(8,128)(2,1)S(1)}, u32[]{:S(2)}, u32[]{:S(2)}) collective-permute-start(bf16[16,32,128]{2,1,0:T(8,128)(2,1)S(1)} %bitcast.15), channel_id=1, source_target_pairs={{0,224},{2,226},{4,228},{6,230},{8,232},{10,234},{12,236},{14,238}... | collective-permute-start | bytes 393224 | tf_op jit(solution)/shard_map/ppermute | solution.py:387
  29.2 7.9 %collective-permute-start.9 = (bf16[16,32,128]{2,1,0:T(8,128)(2,1)S(1)}, bf16[16,32,128]{2,1,0:T(8,128)(2,1)S(1)}, u32[]{:S(2)}, u32[]{:S(2)}) collective-permute-start(bf16[16,32,128]{2,1,0:T(8,128)(2,1)S(1)} %bitcast.16), channel_id=1, source_target_pairs={{0,32},{2,34},{4,36},{6,38},{8,40},{10,42},{12,44},{14,46},{16,48}... | collective-permute-start | bytes 393224 | tf_op jit(solution)/shard_map/ppermute | solution.py:387
  37.0 8.6 %copy-start.1 = (bf16[64,2048]{1,0:T(8,128)(2,1)S(1)}, bf16[64,2048]{1,0:T(8,128)(2,1)}, u32[]{:S(2)}) copy-start(bf16[64,2048]{1,0:T(8,128)(2,1)} %signals.1) | copy-start | bytes 786436
  37.0 8.6 %copy-start.6 = (s32[8,8]{1,0:T(8,128)S(1)}, s32[8,8]{1,0:T(8,128)}, u32[]{:S(2)}) copy-start(s32[8,8]{1,0:T(8,128)} %near_list.1) | copy-start | bytes 772
  37.1 8.6 %copy-start.9 = (s32[1,256]{1,0:T(1,128)S(1)}, s32[1,256]{1,0:T(1,128)}, u32[]{:S(2)}) copy-start(s32[1,256]{1,0:T(1,128)} %get-tuple-element.18.own_row) | copy-start | bytes 3076
  37.1 34.0 %all-to-all-start.1 = ((bf16[16,16,32,128]{3,2,1,0:T(8,128)(2,1)}), bf16[16,16,32,128]{3,2,1,0:T(8,128)(2,1)}, u32[]{:S(2)}, u32[]{:S(2)}) async-start(bf16[16,16,32,128]{3,2,1,0:T(8,128)(2,1)} %select.1), calls=%async_computation.1 | async-start | bytes 4194304 | tf_op jit(solution)/shard_map/all_to_all | solution.py:401
  43.8 6.4 %collective-permute-start.10 = (bf16[16,32,128]{2,1,0:T(8,128)(2,1)S(1)}, bf16[16,32,128]{2,1,0:T(8,128)(2,1)S(1)}, u32[]{:S(2)}, u32[]{:S(2)}) collective-permute-start(bf16[16,32,128]{2,1,0:T(8,128)(2,1)S(1)} %collective-permute-done.8.refs_1_), channel_id=1, source_target_pairs={{0,224},{2,226},{4,228},{6,230},{8,232},{10,234},{12,236},{14,238}... | collective-permute-start | bytes 393224 | tf_op jit(solution)/shard_map/ppermute | solution.py:403
  45.6 5.8 %collective-permute-start.11 = (bf16[16,32,128]{2,1,0:T(8,128)(2,1)S(1)}, bf16[16,32,128]{2,1,0:T(8,128)(2,1)S(1)}, u32[]{:S(2)}, u32[]{:S(2)}) collective-permute-start(bf16[16,32,128]{2,1,0:T(8,128)(2,1)S(1)} %collective-permute-done.9.refs_2_), channel_id=1, source_target_pairs={{0,32},{2,34},{4,36},{6,38},{8,40},{10,42},{12,44},{14,46},{16,48}... | collective-permute-start | bytes 393224 | tf_op jit(solution)/shard_map/ppermute | solution.py:403
  45.7 2.2 %copy-start = (bf16[8,4,256,256]{3,2,1,0:T(8,128)(2,1)S(1)}, bf16[8,4,256,256]{3,2,1,0:T(8,128)(2,1)}, u32[]{:S(2)}) copy-start(bf16[8,4,256,256]{3,2,1,0:T(8,128)(2,1)} %tiles.1) | copy-start | bytes 12582916
  47.9 19.7 %copy-start.3 = (bf16[8,64,64]{2,1,0:T(8,128)(2,1)S(1)}, bf16[8,64,64]{2,1,0:T(8,128)(2,1)}, u32[]{:S(2)}) copy-start(bf16[8,64,64]{2,1,0:T(8,128)(2,1)} %refs_12_.1) | copy-start | bytes 196612
  47.9 19.7 %copy-start.5 = (bf16[2,64,1024]{2,1,0:T(8,128)(2,1)S(1)}, bf16[2,64,1024]{2,1,0:T(8,128)(2,1)}, u32[]{:S(2)}) copy-start(bf16[2,64,1024]{2,1,0:T(8,128)(2,1)} %refs_11_.1) | copy-start | bytes 786436
  47.9 19.7 %copy-start.7 = (s32[8]{0:T(128)S(1)}, s32[8]{0:T(128)}, u32[]{:S(2)}) copy-start(s32[8]{0:T(128)} %parent.3) | copy-start | bytes 100
  47.9 19.7 %copy-start.8 = (s32[2,16]{1,0:T(2,128)S(1)}, s32[2,16]{1,0:T(2,128)}, u32[]{:S(2)}) copy-start(s32[2,16]{1,0:T(2,128)} %parent_far.1) | copy-start | bytes 388
  50.1 17.5 %copy-start.4 = (f32[64,2048]{1,0:T(8,128)}, f32[64,2048]{1,0:T(8,128)S(1)}, u32[]{:S(2)}) copy-start(f32[64,2048]{1,0:T(8,128)S(1)} %get-tuple-element.30.near_own_in) | copy-start | bytes 1572868
  50.1 17.4 %copy-start.10 = (s32[1,256]{1,0:T(1,128)}, s32[1,256]{1,0:T(1,128)S(1)}, u32[]{:S(2)}) copy-start(s32[1,256]{1,0:T(1,128)S(1)} %get-tuple-element.23.slots) | copy-start | bytes 3076
  51.4 4.2 %collective-permute-start.12 = (bf16[16,32,128]{2,1,0:T(8,128)(2,1)S(1)}, bf16[16,32,128]{2,1,0:T(8,128)(2,1)S(1)}, u32[]{:S(2)}, u32[]{:S(2)}) collective-permute-start(bf16[16,32,128]{2,1,0:T(8,128)(2,1)S(1)} %collective-permute-done.10.refs_3_), channel_id=1, source_target_pairs={{0,224},{2,226},{4,228},{6,230},{8,232},{10,234},{12,236},{14,238}... | collective-permute-start | bytes 393224 | tf_op jit(solution)/shard_map/ppermute | solution.py:407
  53.0 5.7 %collective-permute-start.13 = (bf16[16,32,128]{2,1,0:T(8,128)(2,1)S(1)}, bf16[16,32,128]{2,1,0:T(8,128)(2,1)S(1)}, u32[]{:S(2)}, u32[]{:S(2)}) collective-permute-start(bf16[16,32,128]{2,1,0:T(8,128)(2,1)S(1)} %collective-permute-done.11.refs_4_), channel_id=1, source_target_pairs={{0,32},{2,34},{4,36},{6,38},{8,40},{10,42},{12,44},{14,46},{16,48}... | collective-permute-start | bytes 393224 | tf_op jit(solution)/shard_map/ppermute | solution.py:407
  58.7 8.9 %collective-permute-start.16 = (bf16[112,32,128]{2,1,0:T(8,128)(2,1)S(1)}, bf16[112,32,128]{2,1,0:T(8,128)(2,1)S(1)}, u32[]{:S(2)}, u32[]{:S(2)}) collective-permute-start(bf16[112,32,128]{2,1,0:T(8,128)(2,1)S(1)} %constant_dynamic-update-slice_fusion), channel_id=1, source_target_pairs={{0,2},{2,0},{4,6},{6,4},{8,10},{10,8},{12,14},{14,12},{16,18},{18,... | collective-permute-start | bytes 2752520 | tf_op jit(solution)/shard_map/ppermute | solution.py:411
  60.6 3.8 %collective-permute-start.14 = (bf16[8,32,128]{2,1,0:T(8,128)(2,1)S(1)}, bf16[8,32,128]{2,1,0:T(8,128)(2,1)S(1)}, u32[]{:S(2)}, u32[]{:S(2)}) collective-permute-start(bf16[8,32,128]{2,1,0:T(8,128)(2,1)S(1)} %slice.34), channel_id=1, source_target_pairs={{0,224},{2,226},{4,228},{6,230},{8,232},{10,234},{12,236},{14,238}... | collective-permute-start | bytes 196616 | tf_op jit(solution)/shard_map/ppermute | solution.py:409
  60.7 5.1 %collective-permute-start.15 = (bf16[8,32,128]{2,1,0:T(8,128)(2,1)S(1)}, bf16[8,32,128]{2,1,0:T(8,128)(2,1)S(1)}, u32[]{:S(2)}, u32[]{:S(2)}) collective-permute-start(bf16[8,32,128]{2,1,0:T(8,128)(2,1)S(1)} %slice.35), channel_id=1, source_target_pairs={{0,32},{2,34},{4,36},{6,38},{8,40},{10,42},{12,44},{14,46},{16,48}... | collective-permute-start | bytes 196616 | tf_op jit(solution)/shard_map/ppermute | solution.py:409
  62.1 14.8 %collective-permute-start.18 = (bf16[64,2048]{1,0:T(8,128)(2,1)S(1)}, bf16[64,2048]{1,0:T(8,128)(2,1)S(1)}, u32[]{:S(2)}, u32[]{:S(2)}) collective-permute-start(bf16[64,2048]{1,0:T(8,128)(2,1)S(1)} %get-tuple-element.27), channel_id=1, source_target_pairs={{0,1},{1,0},{2,3},{3,2},{4,5},{5,4},{6,7},{7,6},{8,9},{9,8},{10,11... | collective-permute-start | bytes 786440 | tf_op jit(solution)/shard_map/ppermute | solution.py:405
  65.7 1.8 %collective-permute-start.17 = (bf16[16,32,128]{2,1,0:T(8,128)(2,1)S(1)}, bf16[16,32,128]{2,1,0:T(8,128)(2,1)S(1)}, u32[]{:S(2)}, u32[]{:S(2)}) collective-permute-start(bf16[16,32,128]{2,1,0:T(8,128)(2,1)S(1)} %pad_maximum_fusion.5), channel_id=1, source_target_pairs={{0,2},{2,0},{4,6},{6,4},{8,10},{10,8},{12,14},{14,12},{16,18},{18,... | collective-permute-start | bytes 393224 | tf_op jit(solution)/shard_map/ppermute | solution.py:411
  69.4 0.7 copy-start.2

commit v5 on v4

--- a/solution.py
+++ b/solution.py
@@ -88,7 +88,7 @@
 
 
 def upward_kernel(
-    parent, own_list, peer_list, signals_in, basis_in, transfer_in, coef_out, pay_out, row_out, signals, basis, transfer, sems
+    parent, own_list, peer_list, signals_in, basis_in, transfer_in, coef_out, pay_out, row_out, signals, basis, transfer, packed, sems, out_sems
 ):
     pending = load([(signals_in, signals), (basis_in, basis), (transfer_in, transfer)], sems)
     lists = []
@@ -105,18 +105,22 @@
     for copy in pending:
         copy.wait()
     leaf_count, rank, leaf_size = basis.shape
+    coefs = []
+    for c in range(leaf_count):
+        block = signals[:, c * leaf_size : (c + 1) * leaf_size]
+        coefs.append(dot(basis[c], block, NT).astype(jnp.bfloat16))
+    for c in range(leaf_count):
+        packed[c] = pack(coefs[c])
+    written = load([(packed, coef_out.at[z]) for z in range(Z)], out_sems)
+    lifted = [dot(transfer[c], coefs[c], TN) for c in range(leaf_count)]
     sums = [jnp.zeros((rank, signals.shape[0]), jnp.float32) for _ in range(2)]
     for c in range(leaf_count):
-        block = signals[:, c * leaf_size : (c + 1) * leaf_size]
-        coefs = dot(basis[c], block, NT).astype(jnp.bfloat16)
-        packed = pack(coefs)
-        for z in range(Z):
-            coef_out[z, c] = packed
-        lifted = dot(transfer[c], coefs, TN)
         member = parent[c] - lax.axis_index("loop") * 2
-        sums = [s + jnp.where(member == i, lifted, 0.0) for i, s in enumerate(sums)]
+        sums = [s + jnp.where(member == i, lifted[c], 0.0) for i, s in enumerate(sums)]
     for i, s in enumerate(sums):
         pay_out[i * 32 : (i + 1) * 32] = pack(s.astype(jnp.bfloat16))
+    for copy in written:
+        copy.wait()
 
 
 def upward(parent, own_list, peer_list, signals, basis, transfer):
@@ -129,12 +133,14 @@
             jax.ShapeDtypeStruct((1, 256), jnp.int32),
         ),
         in_specs=[SMEM_SPEC, VMEM_SPEC, VMEM_SPEC, ANY_SPEC, ANY_SPEC, ANY_SPEC],
-        out_specs=(VMEM_SPEC,) * 3,
+        out_specs=(ANY_SPEC, VMEM_SPEC, VMEM_SPEC),
         scratch_shapes=[
             pltpu.VMEM(signals.shape, jnp.bfloat16),
             pltpu.VMEM(basis.shape, jnp.bfloat16),
             pltpu.VMEM(transfer.shape, jnp.bfloat16),
+            pltpu.VMEM((leaf_count, 32, 128), jnp.bfloat16),
             pltpu.SemaphoreType.DMA((3,)),
+            pltpu.SemaphoreType.DMA((Z,)),
         ],
         compiler_params=pltpu.CompilerParams(vmem_limit_bytes=56 * MIB),
         cost_estimate=cost(30_000_000, 700_000),
@@ -230,8 +236,8 @@
 
 
 def fields_kernel(parent, parent_far, *refs):
-    sources = refs[:11]
-    coupling, transfer, out, parents = refs[11:]
+    sources = refs[:10]
+    coupling, transfer, out, parents = refs[10:]
     at = 0
     for ref in sources:
         parents[at : at + ref.shape[0]] = ref[...]
@@ -267,7 +273,7 @@
     return pl.pallas_call(
         fields_kernel,
         out_shape=jax.ShapeDtypeStruct(transfer.shape, jnp.float32),
-        in_specs=[SMEM_SPEC] * 2 + [VMEM_SPEC] * 13,
+        in_specs=[SMEM_SPEC] * 2 + [VMEM_SPEC] * 12,
         out_specs=VMEM_SPEC,
         scratch_shapes=[pltpu.VMEM((2 * Z * Y * X * 2, 32, 128), jnp.bfloat16)],
         compiler_params=pltpu.CompilerParams(vmem_limit_bytes=16 * MIB),
@@ -312,13 +318,12 @@
             stacked[c, j * rank : (j + 1) * rank] = pieces
     for copy in pending[8:]:
         copy.wait()
+    far = [dot(coupling[c], stacked[c], NN)[:, :columns] for c in range(leaf_count)]
+    combined = [(far[c] + descended[c]).astype(jnp.bfloat16) for c in range(leaf_count)]
     written = []
     for c in range(leaf_count):
-        leaf_far = dot(coupling[c], stacked[c], NN)[:, :columns]
-        combined = (leaf_far + descended[c]).astype(jnp.bfloat16)
-        far_out = dot(combined, basis[c], TN)
         at = pl.ds(c * leaf_size, leaf_size)
-        out[:, at] = near_own[:, at] + far_out
+        out[:, at] = near_own[:, at] + dot(combined[c], basis[c], TN)
         written.append(pltpu.make_async_copy(out.at[:, at], out_hbm.at[:, at], out_sems.at[c]))
         written[-1].start()
     for copy in written:
@@ -395,9 +400,8 @@
         jnp.concatenate([signals[:, :reach], other[:, :reach]]), perm=[((i + 1) % count, i) for i in range(count)]
     )
     wanted = tables(plane_lists.astype(jnp.int32))
-    send, before, after, one_down, one_up = lax.optimization_barrier(
-        (select(wanted, planes), before, after, one_down, one_up)
-    )
+    send = select(wanted, planes)
+    _, one_down, one_up, before, after = lax.optimization_barrier((send, one_down, one_up, before, after))
     blocks = lax.all_to_all(send, "loop", 0, 0, tiled=True, axis_index_groups=planes_of)
 
     two_down, two_up = down(one_down), up(one_up)
@@ -406,9 +410,10 @@
     _, two_down, two_up = lax.optimization_barrier((near_other, two_down, two_up))
     three_down, three_up = down(two_down), up(two_up)
     half = parents.shape[0] // 2
-    four_down, four_up = down(three_down[:half]), up(three_up[half:])
+    four_down = along(two_down[:half], perm=loop_moves(lambda z, y, x, c: (z - 2, y, x, c)))
+    four_up = along(two_up[half:], perm=loop_moves(lambda z, y, x, c: (z + 2, y, x, c)))
     mine = [parents, one_down, one_up, two_down, two_up, three_down, three_up, four_down, four_up]
-    theirs = [along(jnp.concatenate(part), perm=c_swap) for part in (mine[:7], mine[7:])]
+    theirs = [along(jnp.concatenate(mine), perm=c_swap)]
     descended = fields(parent, parent_far, mine + theirs, parent_coupling, transfer)
 
     partial = downward(slots, blocks.reshape(-1, 32, 128), coupling, descended, leaf_basis, near_own)

time: 79.2 us -> 78.3 us (0.989)
  Pallas kernels: 16 us -> 15 us
  starting transfers between devices: 37.8 us -> 38.6 us
    all_to_all x1, waiting for transfers between devices: 0.92 us -> 4.33 us  [shards(): lax.all_to_all(send, 'loop', 0, 0, tiled=True, axis_index_groups=planes_of)]
    ppermute x2, waiting for transfers between devices: 5.37 us -> 2.65 us  [shards(): three_down, three_up = (down(two_down), up(two_up))]
    ppermute x4 -> x3, starting transfers between devices: 4.28 us -> 5.7 us  [the longest x1 3.25 us: shards(): theirs = [along(jnp.concatenate(mine), perm=c_swap)]]
    pallas_call x1, Pallas kernels: 5.88 us -> 4.78 us  [downward(): pl.pallas_call(downward_kernel, out_shape=jax.ShapeDtypeStruct(near_own.s...]
    ppermute x4 -> x3, waiting for transfers between devices: 3.53 us -> 2.57 us  [the longest x1 1.23 us: shards(): theirs = [along(jnp.concatenate(mine), perm=c_swap)]]
    ppermute x2, waiting for transfers between devices: 1.27 us -> 0.33 us  [shards(): two_down, two_up = (down(one_down), up(one_up))]
    unnamed x30 -> x32, local copies, waits for them, and re-layouts: 3.61 us -> 3.65 us
  transfers between devices with their start and end apart: 21 -> 20, of which waited for: 10 -> 9; matrix products, arithmetic and copies ran while one was open for 2% -> 3% of each run, Pallas kernels for 20% -> 19%
where the time goes in v5:
time: 78.3 us; the launch traced here: 77.9 us
  starting transfers between devices  38.6 us (49%)
  waiting for transfers between devices  16.7 us (21%)
  Pallas kernels  15 us (19%)
  local copies, waits for them, and re-layouts  4.68 us (6%)
  other arithmetic  2.58 us (3%)
    all_to_all x1, starting transfers between devices, shards(): lax.all_to_all(coefs, 'loop', 0, 0, tiled=True, axis_index_groups=columns...  8.2 us
    all_to_all x1, starting transfers between devices, shards(): lax.all_to_all(send, 'loop', 0, 0, tiled=True, axis_index_groups=planes_of)  6.28 us
    all_to_all x1, waiting for transfers between devices, shards(): lax.all_to_all(coefs, 'loop', 0, 0, tiled=True, axis_index_groups=columns...  5.72 us
    pallas_call x1, Pallas kernels, downward(): pl.pallas_call(downward_kernel, out_shape=jax.ShapeDtypeStruct(near_own.s...  4.78 us
    all_to_all x1, waiting for transfers between devices, shards(): lax.all_to_all(send, 'loop', 0, 0, tiled=True, axis_index_groups=planes_of)  4.33 us
    ppermute x3, starting transfers between devices, shards(): along(pair, perm=loop_moves(lambda z, y, x, c, dy=dy: (z, y - dy, x, c)))  3.78 us
    unnamed x32, local copies, waits for them, and re-layouts  3.65 us
    pallas_call x1, Pallas kernels, upward(): pl.pallas_call(upward_kernel, out_shape=(jax.ShapeDtypeStruct((Z, leaf_co...  3.57 us
  transfers between devices with their start and end apart: 20, of which 9 were waited for; matrix products, arithmetic and copies ran while one was open for 3% of the time, Pallas kernels for 19%

profile of v5, /device:TPU:1, one launch (start us, length us, event | category | flops | bytes accessed | tf_op | source)
XLA Modules:
  0.0 77.9 jit_solution(12119019270641128506)
XLA Ops:
  0.0 3.2 %collective-permute-start = (s32[8,24]{1,0:T(8,128)}, s32[8,24]{1,0:T(8,128)S(1)}, u32[]{:S(2)}, u32[]{:S(2)}) collective-permute-start(s32[8,24]{1,0:T(8,128)} %own_list.1), channel_id=1, source_target_pairs={{0,2},{2,0},{4,6},{6,4},{8,10},{10,8},{12,14},{14,12},{16,18},{18,... | collective-permute-start | bytes 2312 | tf_op jit(solution)/shard_map/ppermute | solution.py:376
  3.2 1.0 %collective-permute-start.1 = (bf16[64,2048]{1,0:T(8,128)(2,1)}, bf16[64,2048]{1,0:T(8,128)(2,1)S(1)}, u32[]{:S(2)}, u32[]{:S(2)}) collective-permute-start(bf16[64,2048]{1,0:T(8,128)(2,1)} %signals.1), channel_id=1, source_target_pairs={{0,1},{1,0},{2,3},{3,2},{4,5},{5,4},{6,7},{7,6},{8,9},{9,8},{10,11... | collective-permute-start | bytes 786440 | tf_op jit(solution)/shard_map/ppermute | solution.py:375
  4.2 0.0 collective-permute-done.peer_list
  4.3 0.6 copy-done.11
  4.9 3.6 %upward.1 = (bf16[8,8,32,128]{3,2,1,0:T(8,128)(2,1)}, bf16[80,128]{1,0:T(8,128)(2,1)}, s32[1,256]{1,0:T(1,128)}) custom-call(s32[8]{0:T(128)} %parent.3, s32[8,24]{1,0:T(8,128)} %own_list.1, s32[8,24]{1,0:T(8,128)} %copy-done.11, bf16[64,2048]{1,0:T(8,128)(2,1)} %signals.1, bf16[8,64,256]{2,1,0:T(8,128)(2,1)} %basis_in.3, bf16[8,64,64]{2,1,0:T(8,128)(2,1)} %refs_11_.1), custom_call_target="tpu_custom_call" | custom-call | flops 30000000 | bytes 700000 | tf_op jit(solution)/shard_map/upward/pallas_call | solution.py:128
  8.4 0.4 collective-permute-start.2
  8.8 1.0 %fusion.1 = (bf16[64,1024]{1,0:T(8,128)(2,1)S(1)}, bf16[64,1024]{1,0:T(8,128)(2,1)S(1)}) fusion(bf16[64,2048]{1,0:T(8,128)(2,1)} %signals.1), kind=kLoop, calls=%fused_computation.19 | loop fusion | bytes 524288 | tf_op jit(solution)/shard_map/slice | solution.py:400
  9.8 8.2 %all-to-all-start = ((bf16[8,8,32,128]{3,2,1,0:T(8,128)(2,1)}), bf16[8,8,32,128]{3,2,1,0:T(8,128)(2,1)S(1)}, u32[]{:S(2)}, u32[]{:S(2)}) async-start(bf16[8,8,32,128]{3,2,1,0:T(8,128)(2,1)} %get-tuple-element.19), calls=%async_computation | async-start | bytes 1048576 | tf_op jit(solution)/shard_map/all_to_all | solution.py:379
  18.0 0.7 fusion
  18.8 2.7 %collective-permute-start.3 = (bf16[2,80,128]{2,1,0:T(8,128)(2,1)S(1)}, bf16[2,80,128]{2,1,0:T(8,128)(2,1)S(1)}, u32[]{:S(2)}, u32[]{:S(2)}) collective-permute-start(bf16[2,80,128]{2,1,0:T(8,128)(2,1)S(1)} %get-tuple-element.34), channel_id=1, source_target_pairs={{0,24},{2,26},{4,28},{6,30},{8,0},{10,2},{12,4},{14,6},{16,8},{18,... | collective-permute-start | bytes 122888 | tf_op jit(solution)/shard_map/ppermute | solution.py:384
  21.5 0.3 collective-permute-start.4
  21.8 0.7 collective-permute-start.5
  22.6 2.8 %collective-permute-start.8 = (bf16[128,1024]{1,0:T(8,128)(2,1)S(1)}, bf16[128,1024]{1,0:T(8,128)(2,1)S(1)}, u32[]{:S(2)}, u32[]{:S(2)}) collective-permute-start(bf16[128,1024]{1,0:T(8,128)(2,1)S(1)} %pad_maximum_fusion), channel_id=1, source_target_pairs={{0,2},{2,4},{4,6},{6,8},{8,10},{10,12},{12,14},{14,16},{16,18},{18... | collective-permute-start | bytes 786440 | tf_op jit(solution)/shard_map/ppermute | solution.py:396
  25.4 0.1 collective-permute-start.9
  25.5 0.0 collective-permute-done.3
  25.5 0.6 collective-permute-done.4
  26.1 0.4 collective-permute-done.5
  26.6 2.7 %collective-permute-start.6 = (bf16[16,32,128]{2,1,0:T(8,128)(2,1)S(1)}, bf16[16,32,128]{2,1,0:T(8,128)(2,1)S(1)}, u32[]{:S(2)}, u32[]{:S(2)}) collective-permute-start(bf16[16,32,128]{2,1,0:T(8,128)(2,1)S(1)} %bitcast.15), channel_id=1, source_target_pairs={{0,224},{2,226},{4,228},{6,230},{8,232},{10,234},{12,236},{14,238}... | collective-permute-start | bytes 393224 | tf_op jit(solution)/shard_map/ppermute | solution.py:392
  29.3 0.0 collective-permute-start.7
  29.4 0.4 tables.1.wanted
  29.8 5.7 %all-to-all-done.planes = bf16[8,8,32,128]{3,2,1,0:T(8,128)(2,1)S(1)} async-done(((bf16[8,8,32,128]{3,2,1,0:T(8,128)(2,1)}), bf16[8,8,32,128]{3,2,1,0:T(8,128)(2,1)S(1)}, u32[]{:S(2)}, u32[]{:S(2)}) %all-to-all-start) | async-done | bytes 524320 | tf_op jit(solution)/shard_map/all_to_all | solution.py:379
  35.5 2.2 %select.1 = bf16[16,16,32,128]{3,2,1,0:T(8,128)(2,1)} custom-call(s32[16,128]{1,0:T(8,128)S(1)} %tables.1.wanted, bf16[8,8,32,128]{3,2,1,0:T(8,128)(2,1)S(1)} %all-to-all-done.planes), custom_call_target="tpu_custom_call" | custom-call | flops 1000000 | bytes 2500000 | tf_op jit(solution)/shard_map/select/pallas_call | solution.py:167
  37.7 0.0 copy-start.1
  37.8 0.0 copy-start.6
  37.8 6.3 %all-to-all-start.1 = ((bf16[16,16,32,128]{3,2,1,0:T(8,128)(2,1)}), bf16[16,16,32,128]{3,2,1,0:T(8,128)(2,1)}, u32[]{:S(2)}, u32[]{:S(2)}) async-start(bf16[16,16,32,128]{3,2,1,0:T(8,128)(2,1)} %select.1), calls=%async_computation.1 | async-start | bytes 4194304 | tf_op jit(solution)/shard_map/all_to_all | solution.py:405
  44.1 0.0 collective-permute-done.7.refs_2_
  44.1 0.1 collective-permute-start.10
  44.2 1.5 %collective-permute-start.11 = (bf16[16,32,128]{2,1,0:T(8,128)(2,1)S(1)}, bf16[16,32,128]{2,1,0:T(8,128)(2,1)S(1)}, u32[]{:S(2)}, u32[]{:S(2)}) collective-permute-start(bf16[16,32,128]{2,1,0:T(8,128)(2,1)S(1)} %collective-permute-done.7.refs_2_), channel_id=1, source_target_pairs={{0,32},{2,34},{4,36},{6,38},{8,40},{10,42},{12,44},{14,46},{16,48}... | collective-permute-start | bytes 393224 | tf_op jit(solution)/shard_map/ppermute | solution.py:407
  45.8 2.2 %copy-done = bf16[8,4,256,256]{3,2,1,0:T(8,128)(2,1)S(1)} copy-done((bf16[8,4,256,256]{3,2,1,0:T(8,128)(2,1)S(1)}, bf16[8,4,256,256]{3,2,1,0:T(8,128)(2,1)}, u32[]{:S(2)}) %copy-start) | copy-done | bytes 4194328
  47.9 2.2 %near_field.1 = (f32[64,2048]{1,0:T(8,128)S(1)}, bf16[64,2048]{1,0:T(8,128)(2,1)S(1)}, s32[1,256]{1,0:T(1,128)S(1)}) custom-call(s32[8,8]{1,0:T(8,128)S(1)} %copy-done.6, s32[1,256]{1,0:T(1,128)S(1)} %copy-done.9, bf16[64,2048]{1,0:T(8,128)(2,1)S(1)} %copy-done.1, bf16[64,2048]{1,0:T(8,128)(2,1)S(1)} %collective-permute-done.1.other, ...), custom_call_target="tpu_custom_call" | custom-call | flops 600000000 | bytes 10000000 | tf_op jit(solution)/shard_map/near_field/pallas_call | solution.py:219
  50.2 0.3 collective-permute-done.11.refs_4_
  50.6 1.0 %collective-permute-start.12 = (bf16[16,32,128]{2,1,0:T(8,128)(2,1)S(1)}, bf16[16,32,128]{2,1,0:T(8,128)(2,1)S(1)}, u32[]{:S(2)}, u32[]{:S(2)}) collective-permute-start(bf16[16,32,128]{2,1,0:T(8,128)(2,1)S(1)} %collective-permute-done.10.refs_3_), channel_id=1, source_target_pairs={{0,224},{2,226},{4,228},{6,230},{8,232},{10,234},{12,236},{14,238}... | collective-permute-start | bytes 393224 | tf_op jit(solution)/shard_map/ppermute | solution.py:411
  51.6 0.7 collective-permute-start.13
  52.4 0.8 %collective-permute-start.14 = (bf16[8,32,128]{2,1,0:T(8,128)(2,1)S(1)}, bf16[8,32,128]{2,1,0:T(8,128)(2,1)S(1)}, u32[]{:S(2)}, u32[]{:S(2)}) collective-permute-start(bf16[8,32,128]{2,1,0:T(8,128)(2,1)S(1)} %slice.30), channel_id=1, source_target_pairs={{0,192},{2,194},{4,196},{6,198},{8,200},{10,202},{12,204},{14,206}... | collective-permute-start | bytes 196616 | tf_op jit(solution)/shard_map/ppermute | solution.py:413
  53.2 1.6 %collective-permute-start.15 = (bf16[8,32,128]{2,1,0:T(8,128)(2,1)S(1)}, bf16[8,32,128]{2,1,0:T(8,128)(2,1)S(1)}, u32[]{:S(2)}, u32[]{:S(2)}) collective-permute-start(bf16[8,32,128]{2,1,0:T(8,128)(2,1)S(1)} %slice.31), channel_id=1, source_target_pairs={{0,64},{2,66},{4,68},{6,70},{8,72},{10,74},{12,76},{14,78},{16,80}... | collective-permute-start | bytes 196616 | tf_op jit(solution)/shard_map/ppermute | solution.py:414
  54.8 0.0 collective-permute-done.12.refs_5_
  54.8 2.6 %collective-permute-done.13.refs_6_ = bf16[16,32,128]{2,1,0:T(8,128)(2,1)S(1)} collective-permute-done((bf16[16,32,128]{2,1,0:T(8,128)(2,1)S(1)}, bf16[16,32,128]{2,1,0:T(8,128)(2,1)S(1)}, u32[]{:S(2)}, u32[]{:S(2)}) %collective-permute-start.13) | collective-permute-done | bytes 131104 | tf_op jit(solution)/shard_map/ppermute | solution.py:411
  57.5 0.7 collective-permute-done.14.refs_7_
  58.2 0.6 collective-permute-done.15.refs_8_
  58.9 3.3 %collective-permute-start.16 = (bf16[128,32,128]{2,1,0:T(8,128)(2,1)S(1)}, bf16[128,32,128]{2,1,0:T(8,128)(2,1)S(1)}, u32[]{:S(2)}, u32[]{:S(2)}) collective-permute-start(bf16[128,32,128]{2,1,0:T(8,128)(2,1)S(1)} %constant_dynamic-update-slice_fusion), channel_id=1, source_target_pairs={{0,2},{2,0},{4,6},{6,4},{8,10},{10,8},{12,14},{14,12},{16,18},{18,... | collective-permute-start | bytes 3145736 | tf_op jit(solution)/shard_map/ppermute | solution.py:416
  62.1 1.1 %collective-permute-start.17 = (bf16[64,2048]{1,0:T(8,128)(2,1)S(1)}, bf16[64,2048]{1,0:T(8,128)(2,1)S(1)}, u32[]{:S(2)}, u32[]{:S(2)}) collective-permute-start(bf16[64,2048]{1,0:T(8,128)(2,1)S(1)} %get-tuple-element.25), channel_id=1, source_target_pairs={{0,1},{1,0},{2,3},{3,2},{4,5},{5,4},{6,7},{7,6},{8,9},{9,8},{10,11... | collective-permute-start | bytes 786440 | tf_op jit(solution)/shard_map/ppermute | solution.py:409
  63.2 1.2 %collective-permute-done.16.refs_9_ = bf16[128,32,128]{2,1,0:T(8,128)(2,1)S(1)} collective-permute-done((bf16[128,32,128]{2,1,0:T(8,128)(2,1)S(1)}, bf16[128,32,128]{2,1,0:T(8,128)(2,1)S(1)}, u32[]{:S(2)}, u32[]{:S(2)}) %collective-permute-start.16) | collective-permute-done | bytes 1048608 | tf_op jit(solution)/shard_map/ppermute | solution.py:416
  64.4 1.8 %fields.1.descended_in = f32[8,64,64]{2,1,0:T(8,128)S(1)} custom-call(s32[8]{0:T(128)S(1)} %copy-done.7, s32[2,16]{1,0:T(2,128)S(1)} %copy-done.8, bf16[16,32,128]{2,1,0:T(8,128)(2,1)S(1)} %bitcast.18, bf16[16,32,128]{2,1,0:T(8,128)(2,1)S(1)} %collective-permute-done.6.refs_1_, bf16[16,32,128]{2,1,0:T(8,128)(2,1)S(1)} %collective-permute-done.7.refs_2_, ...), custom_call_target="tpu_custom_call" | custom-call | flops 50000000 | bytes 4000000 | tf_op jit(solution)/shard_map/fields/pallas_call | solution.py:273
  66.2 0.0 copy-start.2
  66.3 0.7 copy-done.2
  67.0 4.3 %all-to-all-done.1 = bf16[16,16,32,128]{3,2,1,0:T(8,128)(2,1)} async-done(((bf16[16,16,32,128]{3,2,1,0:T(8,128)(2,1)}), bf16[16,16,32,128]{3,2,1,0:T(8,128)(2,1)}, u32[]{:S(2)}, u32[]{:S(2)}) %all-to-all-start.1) | async-done | bytes 2097184 | tf_op jit(solution)/shard_map/all_to_all | solution.py:405
  71.3 4.8 %downward.1 = f32[64,2048]{1,0:T(8,128)} custom-call(s32[1,256]{1,0:T(1,128)} %copy-done.10, bf16[256,32,128]{2,1,0:T(8,128)(2,1)} %bitcast.9.blocks_in, bf16[8,64,1536]{2,1,0:T(8,128)(2,1)} %coupling_in.1, f32[8,64,64]{2,1,0:T(8,128)} %copy-done.2, bf16[8,64,256]{2,1,0:T(8,128)(2,1)} %basis_in.3, f32[64,2048]{1,0:T(8,128)} %copy-done.4), custom_call_target="tpu_custom_call" | custom-call | flops 150000000 | bytes 6000000 | tf_op jit(solution)/shard_map/downward/pallas_call | solution.py:336
  76.1 1.8 %add_convert_fusion = bf16[64,2048]{1,0:T(8,128)(2,1)} fusion(f32[64,2048]{1,0:T(8,128)} %downward.1, bf16[64,2048]{1,0:T(8,128)(2,1)S(1)} %collective-permute-done.17), kind=kLoop, calls=%fused_computation | loop fusion | flops 393216 | bytes 1048576 | tf_op jit(solution)/shard_map/convert_element_type | solution.py:420
  (42 shorter events, 0.3 us)
Async XLA Ops:
  0.0 4.3 %collective-permute-start = (s32[8,24]{1,0:T(8,128)}, s32[8,24]{1,0:T(8,128)S(1)}, u32[]{:S(2)}, u32[]{:S(2)}) collective-permute-start(s32[8,24]{1,0:T(8,128)} %own_list.1), channel_id=1, source_target_pairs={{0,2},{2,0},{4,6},{6,4},{8,10},{10,8},{12,14},{14,12},{16,18},{18,... | collective-permute-start | bytes 2312 | tf_op jit(solution)/shard_map/ppermute | solution.py:376
  3.2 19.3 %collective-permute-start.1 = (bf16[64,2048]{1,0:T(8,128)(2,1)}, bf16[64,2048]{1,0:T(8,128)(2,1)S(1)}, u32[]{:S(2)}, u32[]{:S(2)}) collective-permute-start(bf16[64,2048]{1,0:T(8,128)(2,1)} %signals.1), channel_id=1, source_target_pairs={{0,1},{1,0},{2,3},{3,2},{4,5},{5,4},{6,7},{7,6},{8,9},{9,8},{10,11... | collective-permute-start | bytes 786440 | tf_op jit(solution)/shard_map/ppermute | solution.py:375
  4.3 0.6 copy-start.11
  8.4 9.6 %collective-permute-start.2 = (bf16[80,128]{1,0:T(8,128)(2,1)}, bf16[80,128]{1,0:T(8,128)(2,1)S(1)}, u32[]{:S(2)}, u32[]{:S(2)}) collective-permute-start(bf16[80,128]{1,0:T(8,128)(2,1)} %get-tuple-element.18), channel_id=1, source_target_pairs={{0,4},{2,6},{4,0},{6,2},{8,12},{10,14},{12,8},{14,10},{16,20},{18,... | collective-permute-start | bytes 61448 | tf_op jit(solution)/shard_map/ppermute | solution.py:380
  9.8 25.7 %all-to-all-start = ((bf16[8,8,32,128]{3,2,1,0:T(8,128)(2,1)}), bf16[8,8,32,128]{3,2,1,0:T(8,128)(2,1)S(1)}, u32[]{:S(2)}, u32[]{:S(2)}) async-start(bf16[8,8,32,128]{3,2,1,0:T(8,128)(2,1)} %get-tuple-element.19), calls=%async_computation | async-start | bytes 1048576 | tf_op jit(solution)/shard_map/all_to_all | solution.py:379
  18.8 6.7 %collective-permute-start.3 = (bf16[2,80,128]{2,1,0:T(8,128)(2,1)S(1)}, bf16[2,80,128]{2,1,0:T(8,128)(2,1)S(1)}, u32[]{:S(2)}, u32[]{:S(2)}) collective-permute-start(bf16[2,80,128]{2,1,0:T(8,128)(2,1)S(1)} %get-tuple-element.34), channel_id=1, source_target_pairs={{0,24},{2,26},{4,28},{6,30},{8,0},{10,2},{12,4},{14,6},{16,8},{18,... | collective-permute-start | bytes 122888 | tf_op jit(solution)/shard_map/ppermute | solution.py:384
  21.5 4.7 %collective-permute-start.4 = (bf16[2,80,128]{2,1,0:T(8,128)(2,1)S(1)}, bf16[2,80,128]{2,1,0:T(8,128)(2,1)S(1)}, u32[]{:S(2)}, u32[]{:S(2)}) collective-permute-start(bf16[2,80,128]{2,1,0:T(8,128)(2,1)S(1)} %get-tuple-element.34), channel_id=1, source_target_pairs={{0,16},{2,18},{4,20},{6,22},{8,24},{10,26},{12,28},{14,30},{16,0},... | collective-permute-start | bytes 122888 | tf_op jit(solution)/shard_map/ppermute | solution.py:384
  21.8 4.7 %collective-permute-start.5 = (bf16[2,80,128]{2,1,0:T(8,128)(2,1)S(1)}, bf16[2,80,128]{2,1,0:T(8,128)(2,1)S(1)}, u32[]{:S(2)}, u32[]{:S(2)}) collective-permute-start(bf16[2,80,128]{2,1,0:T(8,128)(2,1)S(1)} %get-tuple-element.34), channel_id=1, source_target_pairs={{0,8},{2,10},{4,12},{6,14},{8,16},{10,18},{12,20},{14,22},{16,24},... | collective-permute-start | bytes 122888 | tf_op jit(solution)/shard_map/ppermute | solution.py:384
  22.6 21.5 %collective-permute-start.8 = (bf16[128,1024]{1,0:T(8,128)(2,1)S(1)}, bf16[128,1024]{1,0:T(8,128)(2,1)S(1)}, u32[]{:S(2)}, u32[]{:S(2)}) collective-permute-start(bf16[128,1024]{1,0:T(8,128)(2,1)S(1)} %pad_maximum_fusion), channel_id=1, source_target_pairs={{0,2},{2,4},{4,6},{6,8},{8,10},{10,12},{12,14},{14,16},{16,18},{18... | collective-permute-start | bytes 786440 | tf_op jit(solution)/shard_map/ppermute | solution.py:396
  25.4 18.7 %collective-permute-start.9 = (bf16[128,1024]{1,0:T(8,128)(2,1)S(1)}, bf16[128,1024]{1,0:T(8,128)(2,1)S(1)}, u32[]{:S(2)}, u32[]{:S(2)}) collective-permute-start(bf16[128,1024]{1,0:T(8,128)(2,1)S(1)} %pad_maximum_fusion.1), channel_id=1, source_target_pairs={{2,0},{4,2},{6,4},{8,6},{10,8},{12,10},{14,12},{16,14},{18,16},{20... | collective-permute-start | bytes 786440 | tf_op jit(solution)/shard_map/ppermute | solution.py:399
  26.6 17.5 %collective-permute-start.6 = (bf16[16,32,128]{2,1,0:T(8,128)(2,1)S(1)}, bf16[16,32,128]{2,1,0:T(8,128)(2,1)S(1)}, u32[]{:S(2)}, u32[]{:S(2)}) collective-permute-start(bf16[16,32,128]{2,1,0:T(8,128)(2,1)S(1)} %bitcast.15), channel_id=1, source_target_pairs={{0,224},{2,226},{4,228},{6,230},{8,232},{10,234},{12,236},{14,238}... | collective-permute-start | bytes 393224 | tf_op jit(solution)/shard_map/ppermute | solution.py:392
  29.3 14.7 %collective-permute-start.7 = (bf16[16,32,128]{2,1,0:T(8,128)(2,1)S(1)}, bf16[16,32,128]{2,1,0:T(8,128)(2,1)S(1)}, u32[]{:S(2)}, u32[]{:S(2)}) collective-permute-start(bf16[16,32,128]{2,1,0:T(8,128)(2,1)S(1)} %bitcast.16), channel_id=1, source_target_pairs={{0,32},{2,34},{4,36},{6,38},{8,40},{10,42},{12,44},{14,46},{16,48}... | collective-permute-start | bytes 393224 | tf_op jit(solution)/shard_map/ppermute | solution.py:392
  37.7 8.0 %copy-start.1 = (bf16[64,2048]{1,0:T(8,128)(2,1)S(1)}, bf16[64,2048]{1,0:T(8,128)(2,1)}, u32[]{:S(2)}) copy-start(bf16[64,2048]{1,0:T(8,128)(2,1)} %signals.1) | copy-start | bytes 786436
  37.8 8.0 %copy-start.6 = (s32[8,8]{1,0:T(8,128)S(1)}, s32[8,8]{1,0:T(8,128)}, u32[]{:S(2)}) copy-start(s32[8,8]{1,0:T(8,128)} %near_list.1) | copy-start | bytes 772
  37.8 8.0 %copy-start.9 = (s32[1,256]{1,0:T(1,128)S(1)}, s32[1,256]{1,0:T(1,128)}, u32[]{:S(2)}) copy-start(s32[1,256]{1,0:T(1,128)} %get-tuple-element.17.own_row) | copy-start | bytes 3076
  37.8 33.5 %all-to-all-start.1 = ((bf16[16,16,32,128]{3,2,1,0:T(8,128)(2,1)}), bf16[16,16,32,128]{3,2,1,0:T(8,128)(2,1)}, u32[]{:S(2)}, u32[]{:S(2)}) async-start(bf16[16,16,32,128]{3,2,1,0:T(8,128)(2,1)} %select.1), calls=%async_computation.1 | async-start | bytes 4194304 | tf_op jit(solution)/shard_map/all_to_all | solution.py:405
  44.1 6.1 %collective-permute-start.10 = (bf16[16,32,128]{2,1,0:T(8,128)(2,1)S(1)}, bf16[16,32,128]{2,1,0:T(8,128)(2,1)S(1)}, u32[]{:S(2)}, u32[]{:S(2)}) collective-permute-start(bf16[16,32,128]{2,1,0:T(8,128)(2,1)S(1)} %collective-permute-done.6.refs_1_), channel_id=1, source_target_pairs={{0,224},{2,226},{4,228},{6,230},{8,232},{10,234},{12,236},{14,238}... | collective-permute-start | bytes 393224 | tf_op jit(solution)/shard_map/ppermute | solution.py:407
  44.2 6.3 %collective-permute-start.11 = (bf16[16,32,128]{2,1,0:T(8,128)(2,1)S(1)}, bf16[16,32,128]{2,1,0:T(8,128)(2,1)S(1)}, u32[]{:S(2)}, u32[]{:S(2)}) collective-permute-start(bf16[16,32,128]{2,1,0:T(8,128)(2,1)S(1)} %collective-permute-done.7.refs_2_), channel_id=1, source_target_pairs={{0,32},{2,34},{4,36},{6,38},{8,40},{10,42},{12,44},{14,46},{16,48}... | collective-permute-start | bytes 393224 | tf_op jit(solution)/shard_map/ppermute | solution.py:407
  45.7 2.2 %copy-start = (bf16[8,4,256,256]{3,2,1,0:T(8,128)(2,1)S(1)}, bf16[8,4,256,256]{3,2,1,0:T(8,128)(2,1)}, u32[]{:S(2)}) copy-start(bf16[8,4,256,256]{3,2,1,0:T(8,128)(2,1)} %tiles.1) | copy-start | bytes 12582916
  47.9 16.5 %copy-start.3 = (bf16[8,64,64]{2,1,0:T(8,128)(2,1)S(1)}, bf16[8,64,64]{2,1,0:T(8,128)(2,1)}, u32[]{:S(2)}) copy-start(bf16[8,64,64]{2,1,0:T(8,128)(2,1)} %refs_11_.1) | copy-start | bytes 196612
  47.9 16.5 %copy-start.5 = (bf16[2,64,1024]{2,1,0:T(8,128)(2,1)S(1)}, bf16[2,64,1024]{2,1,0:T(8,128)(2,1)}, u32[]{:S(2)}) copy-start(bf16[2,64,1024]{2,1,0:T(8,128)(2,1)} %refs_10_.1) | copy-start | bytes 786436
  47.9 16.5 %copy-start.7 = (s32[8]{0:T(128)S(1)}, s32[8]{0:T(128)}, u32[]{:S(2)}) copy-start(s32[8]{0:T(128)} %parent.3) | copy-start | bytes 100
  47.9 16.5 %copy-start.8 = (s32[2,16]{1,0:T(2,128)S(1)}, s32[2,16]{1,0:T(2,128)}, u32[]{:S(2)}) copy-start(s32[2,16]{1,0:T(2,128)} %parent_far.1) | copy-start | bytes 388
  50.2 13.0 %copy-start.4 = (f32[64,2048]{1,0:T(8,128)}, f32[64,2048]{1,0:T(8,128)S(1)}, u32[]{:S(2)}) copy-start(f32[64,2048]{1,0:T(8,128)S(1)} %get-tuple-element.28.near_own_in) | copy-start | bytes 1572868
  50.2 14.2 %copy-start.10 = (s32[1,256]{1,0:T(1,128)}, s32[1,256]{1,0:T(1,128)S(1)}, u32[]{:S(2)}) copy-start(s32[1,256]{1,0:T(1,128)S(1)} %get-tuple-element.22.slots) | copy-start | bytes 3076
  50.6 4.3 %collective-permute-start.12 = (bf16[16,32,128]{2,1,0:T(8,128)(2,1)S(1)}, bf16[16,32,128]{2,1,0:T(8,128)(2,1)S(1)}, u32[]{:S(2)}, u32[]{:S(2)}) collective-permute-start(bf16[16,32,128]{2,1,0:T(8,128)(2,1)S(1)} %collective-permute-done.10.refs_3_), channel_id=1, source_target_pairs={{0,224},{2,226},{4,228},{6,230},{8,232},{10,234},{12,236},{14,238}... | collective-permute-start | bytes 393224 | tf_op jit(solution)/shard_map/ppermute | solution.py:411
  51.6 5.9 %collective-permute-start.13 = (bf16[16,32,128]{2,1,0:T(8,128)(2,1)S(1)}, bf16[16,32,128]{2,1,0:T(8,128)(2,1)S(1)}, u32[]{:S(2)}, u32[]{:S(2)}) collective-permute-start(bf16[16,32,128]{2,1,0:T(8,128)(2,1)S(1)} %collective-permute-done.11.refs_4_), channel_id=1, source_target_pairs={{0,32},{2,34},{4,36},{6,38},{8,40},{10,42},{12,44},{14,46},{16,48}... | collective-permute-start | bytes 393224 | tf_op jit(solution)/shard_map/ppermute | solution.py:411
  52.4 5.9 %collective-permute-start.14 = (bf16[8,32,128]{2,1,0:T(8,128)(2,1)S(1)}, bf16[8,32,128]{2,1,0:T(8,128)(2,1)S(1)}, u32[]{:S(2)}, u32[]{:S(2)}) collective-permute-start(bf16[8,32,128]{2,1,0:T(8,128)(2,1)S(1)} %slice.30), channel_id=1, source_target_pairs={{0,192},{2,194},{4,196},{6,198},{8,200},{10,202},{12,204},{14,206}... | collective-permute-start | bytes 196616 | tf_op jit(solution)/shard_map/ppermute | solution.py:413
  53.2 5.7 %collective-permute-start.15 = (bf16[8,32,128]{2,1,0:T(8,128)(2,1)S(1)}, bf16[8,32,128]{2,1,0:T(8,128)(2,1)S(1)}, u32[]{:S(2)}, u32[]{:S(2)}) collective-permute-start(bf16[8,32,128]{2,1,0:T(8,128)(2,1)S(1)} %slice.31), channel_id=1, source_target_pairs={{0,64},{2,66},{4,68},{6,70},{8,72},{10,74},{12,76},{14,78},{16,80}... | collective-permute-start | bytes 196616 | tf_op jit(solution)/shard_map/ppermute | solution.py:414
  58.9 5.5 %collective-permute-start.16 = (bf16[128,32,128]{2,1,0:T(8,128)(2,1)S(1)}, bf16[128,32,128]{2,1,0:T(8,128)(2,1)S(1)}, u32[]{:S(2)}, u32[]{:S(2)}) collective-permute-start(bf16[128,32,128]{2,1,0:T(8,128)(2,1)S(1)} %constant_dynamic-update-slice_fusion), channel_id=1, source_target_pairs={{0,2},{2,0},{4,6},{6,4},{8,10},{10,8},{12,14},{14,12},{16,18},{18,... | collective-permute-start | bytes 3145736 | tf_op jit(solution)/shard_map/ppermute | solution.py:416
  62.1 13.9 %collective-permute-start.17 = (bf16[64,2048]{1,0:T(8,128)(2,1)S(1)}, bf16[64,2048]{1,0:T(8,128)(2,1)S(1)}, u32[]{:S(2)}, u32[]{:S(2)}) collective-permute-start(bf16[64,2048]{1,0:T(8,128)(2,1)S(1)} %get-tuple-element.25), channel_id=1, source_target_pairs={{0,1},{1,0},{2,3},{3,2},{4,5},{5,4},{6,7},{7,6},{8,9},{9,8},{10,11... | collective-permute-start | bytes 786440 | tf_op jit(solution)/shard_map/ppermute | solution.py:409
  66.2 0.7 copy-start.2

commit v6 on v5

--- a/solution.py
+++ b/solution.py
@@ -88,9 +88,40 @@
 
 
 def upward_kernel(
-    parent, own_list, peer_list, signals_in, basis_in, transfer_in, coef_out, pay_out, row_out, signals, basis, transfer, packed, sems, out_sems
+    parent_in,
+    own_list_in,
+    peer_list_in,
+    signals_in,
+    basis_in,
+    transfer_in,
+    coef_out,
+    pay_out,
+    row_out,
+    parent,
+    own_list,
+    peer_list,
+    signals,
+    basis,
+    transfer,
+    packed,
+    pay,
+    row_held,
+    sems,
+    out_sems,
 ):
-    pending = load([(signals_in, signals), (basis_in, basis), (transfer_in, transfer)], sems)
+    pending = load(
+        [
+            (signals_in, signals),
+            (basis_in, basis),
+            (own_list_in, own_list),
+            (peer_list_in, peer_list),
+            (transfer_in, transfer),
+            (parent_in, parent),
+        ],
+        sems,
+    )
+    pending[2].wait()
+    pending[3].wait()
     lists = []
     for ref in (own_list, peer_list):
         ids = ref[...]
@@ -99,11 +130,12 @@
         devices, members = row // ids.shape[0], row % ids.shape[0]
         lists += [devices[:, :128], devices[:, 128:], members[:, :128], members[:, 128:]]
         if ref is own_list:
-            row_out[...] = devices
+            row_held[...] = devices
     lists.append(jnp.zeros((8, 128), jnp.int32))
-    pay_out[64:80] = jnp.concatenate(lists, axis=0).astype(jnp.float32).astype(jnp.bfloat16)
-    for copy in pending:
-        copy.wait()
+    pay[64:80] = jnp.concatenate(lists, axis=0).astype(jnp.float32).astype(jnp.bfloat16)
+    written = load([(row_held, row_out)], out_sems)
+    pending[0].wait()
+    pending[1].wait()
     leaf_count, rank, leaf_size = basis.shape
     coefs = []
     for c in range(leaf_count):
@@ -111,14 +143,17 @@
         coefs.append(dot(basis[c], block, NT).astype(jnp.bfloat16))
     for c in range(leaf_count):
         packed[c] = pack(coefs[c])
-    written = load([(packed, coef_out.at[z]) for z in range(Z)], out_sems)
+    written += load([(packed, coef_out.at[z]) for z in range(Z)], out_sems.at[pl.ds(1, Z)])
+    pending[4].wait()
+    pending[5].wait()
     lifted = [dot(transfer[c], coefs[c], TN) for c in range(leaf_count)]
     sums = [jnp.zeros((rank, signals.shape[0]), jnp.float32) for _ in range(2)]
     for c in range(leaf_count):
         member = parent[c] - lax.axis_index("loop") * 2
         sums = [s + jnp.where(member == i, lifted[c], 0.0) for i, s in enumerate(sums)]
     for i, s in enumerate(sums):
-        pay_out[i * 32 : (i + 1) * 32] = pack(s.astype(jnp.bfloat16))
+        pay[i * 32 : (i + 1) * 32] = pack(s.astype(jnp.bfloat16))
+    written += load([(pay, pay_out)], out_sems.at[pl.ds(1 + Z, 1)])
     for copy in written:
         copy.wait()
 
@@ -132,15 +167,20 @@
             jax.ShapeDtypeStruct((80, 128), jnp.bfloat16),
             jax.ShapeDtypeStruct((1, 256), jnp.int32),
         ),
-        in_specs=[SMEM_SPEC, VMEM_SPEC, VMEM_SPEC, ANY_SPEC, ANY_SPEC, ANY_SPEC],
-        out_specs=(ANY_SPEC, VMEM_SPEC, VMEM_SPEC),
+        in_specs=[ANY_SPEC] * 6,
+        out_specs=(ANY_SPEC,) * 3,
         scratch_shapes=[
+            pltpu.SMEM(parent.shape, jnp.int32),
+            pltpu.VMEM(own_list.shape, jnp.int32),
+            pltpu.VMEM(own_list.shape, jnp.int32),
             pltpu.VMEM(signals.shape, jnp.bfloat16),
             pltpu.VMEM(basis.shape, jnp.bfloat16),
             pltpu.VMEM(transfer.shape, jnp.bfloat16),
             pltpu.VMEM((leaf_count, 32, 128), jnp.bfloat16),
-            pltpu.SemaphoreType.DMA((3,)),
-            pltpu.SemaphoreType.DMA((Z,)),
+            pltpu.VMEM((80, 128), jnp.bfloat16),
+            pltpu.VMEM((1, 256), jnp.int32),
+            pltpu.SemaphoreType.DMA((6,)),
+            pltpu.SemaphoreType.DMA((2 + Z,)),
         ],
         compiler_params=pltpu.CompilerParams(vmem_limit_bytes=56 * MIB),
         cost_estimate=cost(30_000_000, 700_000),
@@ -283,13 +323,14 @@
 
 
 def downward_kernel(
-    slots,
+    slots_in,
     blocks_in,
     coupling_in,
     descended_in,
     basis_in,
     near_own_in,
     out_hbm,
+    slots,
     blocks,
     coupling,
     descended,
@@ -305,10 +346,10 @@
     pending = load(
         [(blocks_in.at[pl.ds(i * part, part)], blocks.at[pl.ds(i * part, part)]) for i in range(8)]
         + [(coupling_in.at[c], coupling.at[c]) for c in range(leaf_count)]
-        + [(descended_in, descended), (basis_in, basis), (near_own_in, near_own)],
+        + [(descended_in, descended), (basis_in, basis), (near_own_in, near_own), (slots_in, slots)],
         sems,
     )
-    for copy in pending[:8]:
+    for copy in pending[:8] + pending[-1:]:
         copy.wait()
     sources = coupling.shape[2] // rank
     columns = out.shape[0]
@@ -316,7 +357,7 @@
         for j in range(sources):
             pieces = jnp.concatenate(unpack(blocks[slots[0, c * sources + j]]), axis=0)
             stacked[c, j * rank : (j + 1) * rank] = pieces
-    for copy in pending[8:]:
+    for copy in pending[8:-1]:
         copy.wait()
     far = [dot(coupling[c], stacked[c], NN)[:, :columns] for c in range(leaf_count)]
     combined = [(far[c] + descended[c]).astype(jnp.bfloat16) for c in range(leaf_count)]
@@ -336,13 +377,14 @@
     return pl.pallas_call(
         downward_kernel,
         out_shape=jax.ShapeDtypeStruct(near_own.shape, jnp.float32),
-        in_specs=[SMEM_SPEC] + [ANY_SPEC] * 5,
+        in_specs=[ANY_SPEC] * 6,
         out_specs=ANY_SPEC,
-        scratch_shapes=[pltpu.VMEM(a.shape, a.dtype) for a in arrays]
+        scratch_shapes=[pltpu.SMEM(slots.shape, jnp.int32)]
+        + [pltpu.VMEM(a.shape, a.dtype) for a in arrays]
         + [
             pltpu.VMEM((leaf_count, coupling.shape[2], 128), jnp.bfloat16),
             pltpu.VMEM(near_own.shape, jnp.float32),
-            pltpu.SemaphoreType.DMA((11 + leaf_count,)),
+            pltpu.SemaphoreType.DMA((12 + leaf_count,)),
             pltpu.SemaphoreType.DMA((leaf_count,)),
         ],
         compiler_params=pltpu.CompilerParams(vmem_limit_bytes=62 * MIB),

time: 78.3 us -> 76.8 us (0.981)
  Pallas kernels: 15 us -> 13.1 us
    pallas_call x1, Pallas kernels: 3.57 us -> 2.37 us  [upward(): pl.pallas_call(upward_kernel, out_shape=(jax.ShapeDtypeStruct((Z, leaf_co...]
  transfers between devices with their start and end apart: 20 -> 20, of which waited for: 9 -> 10; matrix products, arithmetic and copies ran while one was open for 3% -> 3% of each run, Pallas kernels for 19% -> 17%
where the time goes in v6:
time: 76.8 us; the launch traced here: 76.4 us
  starting transfers between devices  38.6 us (50%)
  waiting for transfers between devices  17.1 us (22%)
  Pallas kernels  13.1 us (17%)
  local copies, waits for them, and re-layouts  4.68 us (6%)
  other arithmetic  2.58 us (3%)
    all_to_all x1, starting transfers between devices, shards(): lax.all_to_all(coefs, 'loop', 0, 0, tiled=True, axis_index_groups=columns...  8.19 us
    all_to_all x1, starting transfers between devices, shards(): lax.all_to_all(send, 'loop', 0, 0, tiled=True, axis_index_groups=planes_of)  6.28 us
    all_to_all x1, waiting for transfers between devices, shards(): lax.all_to_all(coefs, 'loop', 0, 0, tiled=True, axis_index_groups=columns...  5.72 us
    all_to_all x1, waiting for transfers between devices, shards(): lax.all_to_all(send, 'loop', 0, 0, tiled=True, axis_index_groups=planes_of)  4.31 us
    pallas_call x1, Pallas kernels, downward(): pl.pallas_call(downward_kernel, out_shape=jax.ShapeDtypeStruct(near_own.s...  4.1 us
    ppermute x3, starting transfers between devices, shards(): along(pair, perm=loop_moves(lambda z, y, x, c, dy=dy: (z, y - dy, x, c)))  3.78 us
    unnamed x32, local copies, waits for them, and re-layouts  3.65 us
    ppermute x1, starting transfers between devices, shards(): theirs = [along(jnp.concatenate(mine), perm=c_swap)]  3.27 us
  transfers between devices with their start and end apart: 20, of which 10 were waited for; matrix products, arithmetic and copies ran while one was open for 3% of the time, Pallas kernels for 17%

profile of v6, /device:TPU:1, one launch (start us, length us, event | category | flops | bytes accessed | tf_op | source)
XLA Modules:
  0.0 76.4 jit_solution(13893198530645688814)
XLA Ops:
  0.0 3.2 %collective-permute-start = (s32[8,24]{1,0:T(8,128)}, s32[8,24]{1,0:T(8,128)S(1)}, u32[]{:S(2)}, u32[]{:S(2)}) collective-permute-start(s32[8,24]{1,0:T(8,128)} %own_list_in.1), channel_id=1, source_target_pairs={{0,2},{2,0},{4,6},{6,4},{8,10},{10,8},{12,14},{14,12},{16,18},{18,... | collective-permute-start | bytes 2312 | tf_op jit(solution)/shard_map/ppermute | solution.py:418
  3.2 1.0 %collective-permute-start.1 = (bf16[64,2048]{1,0:T(8,128)(2,1)}, bf16[64,2048]{1,0:T(8,128)(2,1)S(1)}, u32[]{:S(2)}, u32[]{:S(2)}) collective-permute-start(bf16[64,2048]{1,0:T(8,128)(2,1)} %signals.1), channel_id=1, source_target_pairs={{0,1},{1,0},{2,3},{3,2},{4,5},{5,4},{6,7},{7,6},{8,9},{9,8},{10,11... | collective-permute-start | bytes 786440 | tf_op jit(solution)/shard_map/ppermute | solution.py:417
  4.2 0.0 collective-permute-done.peer_list_in
  4.3 0.6 copy-done.11
  4.9 2.4 %upward.1 = (bf16[8,8,32,128]{3,2,1,0:T(8,128)(2,1)}, bf16[80,128]{1,0:T(8,128)(2,1)}, s32[1,256]{1,0:T(1,128)}) custom-call(s32[8]{0:T(128)} %parent.1, s32[8,24]{1,0:T(8,128)} %own_list_in.1, s32[8,24]{1,0:T(8,128)} %copy-done.11, bf16[64,2048]{1,0:T(8,128)(2,1)} %signals.1, bf16[8,64,256]{2,1,0:T(8,128)(2,1)} %basis_in.3, bf16[8,64,64]{2,1,0:T(8,128)(2,1)} %refs_11_.1), custom_call_target="tpu_custom_call" | custom-call | flops 30000000 | bytes 700000 | tf_op jit(solution)/shard_map/upward/pallas_call | solution.py:163
  7.2 0.4 collective-permute-start.2
  7.6 1.0 %fusion.1 = (bf16[64,1024]{1,0:T(8,128)(2,1)S(1)}, bf16[64,1024]{1,0:T(8,128)(2,1)S(1)}) fusion(bf16[64,2048]{1,0:T(8,128)(2,1)} %signals.1), kind=kLoop, calls=%fused_computation.19 | loop fusion | bytes 524288 | tf_op jit(solution)/shard_map/slice | solution.py:442
  8.6 8.2 %all-to-all-start = ((bf16[8,8,32,128]{3,2,1,0:T(8,128)(2,1)}), bf16[8,8,32,128]{3,2,1,0:T(8,128)(2,1)S(1)}, u32[]{:S(2)}, u32[]{:S(2)}) async-start(bf16[8,8,32,128]{3,2,1,0:T(8,128)(2,1)} %get-tuple-element.19), calls=%async_computation | async-start | bytes 1048576 | tf_op jit(solution)/shard_map/all_to_all | solution.py:421
  16.8 0.0 collective-permute-done.2
  16.8 0.7 fusion
  17.6 2.7 %collective-permute-start.3 = (bf16[2,80,128]{2,1,0:T(8,128)(2,1)S(1)}, bf16[2,80,128]{2,1,0:T(8,128)(2,1)S(1)}, u32[]{:S(2)}, u32[]{:S(2)}) collective-permute-start(bf16[2,80,128]{2,1,0:T(8,128)(2,1)S(1)} %get-tuple-element.34), channel_id=1, source_target_pairs={{0,24},{2,26},{4,28},{6,30},{8,0},{10,2},{12,4},{14,6},{16,8},{18,... | collective-permute-start | bytes 122888 | tf_op jit(solution)/shard_map/ppermute | solution.py:426
  20.3 0.3 collective-permute-start.4
  20.6 0.7 collective-permute-start.5
  21.4 2.8 %collective-permute-start.8 = (bf16[128,1024]{1,0:T(8,128)(2,1)S(1)}, bf16[128,1024]{1,0:T(8,128)(2,1)S(1)}, u32[]{:S(2)}, u32[]{:S(2)}) collective-permute-start(bf16[128,1024]{1,0:T(8,128)(2,1)S(1)} %pad_maximum_fusion), channel_id=1, source_target_pairs={{0,2},{2,4},{4,6},{6,8},{8,10},{10,12},{12,14},{14,16},{16,18},{18... | collective-permute-start | bytes 786440 | tf_op jit(solution)/shard_map/ppermute | solution.py:438
  24.2 0.1 collective-permute-start.9
  24.3 0.6 collective-permute-done.4
  24.9 0.4 collective-permute-done.5
  25.4 2.7 %collective-permute-start.6 = (bf16[16,32,128]{2,1,0:T(8,128)(2,1)S(1)}, bf16[16,32,128]{2,1,0:T(8,128)(2,1)S(1)}, u32[]{:S(2)}, u32[]{:S(2)}) collective-permute-start(bf16[16,32,128]{2,1,0:T(8,128)(2,1)S(1)} %bitcast.15), channel_id=1, source_target_pairs={{0,224},{2,226},{4,228},{6,230},{8,232},{10,234},{12,236},{14,238}... | collective-permute-start | bytes 393224 | tf_op jit(solution)/shard_map/ppermute | solution.py:434
  28.1 0.0 collective-permute-start.7
  28.2 0.4 tables.1.wanted
  28.6 5.7 %all-to-all-done.planes = bf16[8,8,32,128]{3,2,1,0:T(8,128)(2,1)S(1)} async-done(((bf16[8,8,32,128]{3,2,1,0:T(8,128)(2,1)}), bf16[8,8,32,128]{3,2,1,0:T(8,128)(2,1)S(1)}, u32[]{:S(2)}, u32[]{:S(2)}) %all-to-all-start) | async-done | bytes 524320 | tf_op jit(solution)/shard_map/all_to_all | solution.py:421
  34.3 2.2 %select.1 = bf16[16,16,32,128]{3,2,1,0:T(8,128)(2,1)} custom-call(s32[16,128]{1,0:T(8,128)S(1)} %tables.1.wanted, bf16[8,8,32,128]{3,2,1,0:T(8,128)(2,1)S(1)} %all-to-all-done.planes), custom_call_target="tpu_custom_call" | custom-call | flops 1000000 | bytes 2500000 | tf_op jit(solution)/shard_map/select/pallas_call | solution.py:207
  36.5 0.0 copy-start.1
  36.6 0.0 copy-start.6
  36.6 6.3 %all-to-all-start.1 = ((bf16[16,16,32,128]{3,2,1,0:T(8,128)(2,1)}), bf16[16,16,32,128]{3,2,1,0:T(8,128)(2,1)}, u32[]{:S(2)}, u32[]{:S(2)}) async-start(bf16[16,16,32,128]{3,2,1,0:T(8,128)(2,1)} %select.1), calls=%async_computation.1 | async-start | bytes 4194304 | tf_op jit(solution)/shard_map/all_to_all | solution.py:447
  42.9 0.1 collective-permute-start.10
  43.0 1.5 %collective-permute-start.11 = (bf16[16,32,128]{2,1,0:T(8,128)(2,1)S(1)}, bf16[16,32,128]{2,1,0:T(8,128)(2,1)S(1)}, u32[]{:S(2)}, u32[]{:S(2)}) collective-permute-start(bf16[16,32,128]{2,1,0:T(8,128)(2,1)S(1)} %collective-permute-done.7.refs_2_), channel_id=1, source_target_pairs={{0,32},{2,34},{4,36},{6,38},{8,40},{10,42},{12,44},{14,46},{16,48}... | collective-permute-start | bytes 393224 | tf_op jit(solution)/shard_map/ppermute | solution.py:449
  44.6 2.2 %copy-done = bf16[8,4,256,256]{3,2,1,0:T(8,128)(2,1)S(1)} copy-done((bf16[8,4,256,256]{3,2,1,0:T(8,128)(2,1)S(1)}, bf16[8,4,256,256]{3,2,1,0:T(8,128)(2,1)}, u32[]{:S(2)}) %copy-start) | copy-done | bytes 4194328
  46.7 2.2 %near_field.1 = (f32[64,2048]{1,0:T(8,128)S(1)}, bf16[64,2048]{1,0:T(8,128)(2,1)S(1)}, s32[1,256]{1,0:T(1,128)S(1)}) custom-call(s32[8,8]{1,0:T(8,128)S(1)} %copy-done.6, s32[1,256]{1,0:T(1,128)S(1)} %copy-done.9, bf16[64,2048]{1,0:T(8,128)(2,1)S(1)} %copy-done.1, bf16[64,2048]{1,0:T(8,128)(2,1)S(1)} %collective-permute-done.1.other, ...), custom_call_target="tpu_custom_call" | custom-call | flops 600000000 | bytes 10000000 | tf_op jit(solution)/shard_map/near_field/pallas_call | solution.py:259
  49.0 0.3 collective-permute-done.11.refs_4_
  49.4 1.0 %collective-permute-start.12 = (bf16[16,32,128]{2,1,0:T(8,128)(2,1)S(1)}, bf16[16,32,128]{2,1,0:T(8,128)(2,1)S(1)}, u32[]{:S(2)}, u32[]{:S(2)}) collective-permute-start(bf16[16,32,128]{2,1,0:T(8,128)(2,1)S(1)} %collective-permute-done.10.refs_3_), channel_id=1, source_target_pairs={{0,224},{2,226},{4,228},{6,230},{8,232},{10,234},{12,236},{14,238}... | collective-permute-start | bytes 393224 | tf_op jit(solution)/shard_map/ppermute | solution.py:453
  50.4 0.7 collective-permute-start.13
  51.2 0.8 %collective-permute-start.14 = (bf16[8,32,128]{2,1,0:T(8,128)(2,1)S(1)}, bf16[8,32,128]{2,1,0:T(8,128)(2,1)S(1)}, u32[]{:S(2)}, u32[]{:S(2)}) collective-permute-start(bf16[8,32,128]{2,1,0:T(8,128)(2,1)S(1)} %slice.30), channel_id=1, source_target_pairs={{0,192},{2,194},{4,196},{6,198},{8,200},{10,202},{12,204},{14,206}... | collective-permute-start | bytes 196616 | tf_op jit(solution)/shard_map/ppermute | solution.py:455
  52.0 1.6 %collective-permute-start.15 = (bf16[8,32,128]{2,1,0:T(8,128)(2,1)S(1)}, bf16[8,32,128]{2,1,0:T(8,128)(2,1)S(1)}, u32[]{:S(2)}, u32[]{:S(2)}) collective-permute-start(bf16[8,32,128]{2,1,0:T(8,128)(2,1)S(1)} %slice.31), channel_id=1, source_target_pairs={{0,64},{2,66},{4,68},{6,70},{8,72},{10,74},{12,76},{14,78},{16,80}... | collective-permute-start | bytes 196616 | tf_op jit(solution)/shard_map/ppermute | solution.py:456
  53.6 0.0 collective-permute-done.12.refs_5_
  53.6 2.6 %collective-permute-done.13.refs_6_ = bf16[16,32,128]{2,1,0:T(8,128)(2,1)S(1)} collective-permute-done((bf16[16,32,128]{2,1,0:T(8,128)(2,1)S(1)}, bf16[16,32,128]{2,1,0:T(8,128)(2,1)S(1)}, u32[]{:S(2)}, u32[]{:S(2)}) %collective-permute-start.13) | collective-permute-done | bytes 131104 | tf_op jit(solution)/shard_map/ppermute | solution.py:453
  56.3 0.8 %collective-permute-done.14.refs_7_ = bf16[8,32,128]{2,1,0:T(8,128)(2,1)S(1)} collective-permute-done((bf16[8,32,128]{2,1,0:T(8,128)(2,1)S(1)}, bf16[8,32,128]{2,1,0:T(8,128)(2,1)S(1)}, u32[]{:S(2)}, u32[]{:S(2)}) %collective-permute-start.14) | collective-permute-done | bytes 65568 | tf_op jit(solution)/shard_map/ppermute | solution.py:455
  57.0 0.6 collective-permute-done.15.refs_8_
  57.7 3.3 %collective-permute-start.16 = (bf16[128,32,128]{2,1,0:T(8,128)(2,1)S(1)}, bf16[128,32,128]{2,1,0:T(8,128)(2,1)S(1)}, u32[]{:S(2)}, u32[]{:S(2)}) collective-permute-start(bf16[128,32,128]{2,1,0:T(8,128)(2,1)S(1)} %constant_dynamic-update-slice_fusion), channel_id=1, source_target_pairs={{0,2},{2,0},{4,6},{6,4},{8,10},{10,8},{12,14},{14,12},{16,18},{18,... | collective-permute-start | bytes 3145736 | tf_op jit(solution)/shard_map/ppermute | solution.py:458
  60.9 1.0 %collective-permute-start.17 = (bf16[64,2048]{1,0:T(8,128)(2,1)S(1)}, bf16[64,2048]{1,0:T(8,128)(2,1)S(1)}, u32[]{:S(2)}, u32[]{:S(2)}) collective-permute-start(bf16[64,2048]{1,0:T(8,128)(2,1)S(1)} %get-tuple-element.25), channel_id=1, source_target_pairs={{0,1},{1,0},{2,3},{3,2},{4,5},{5,4},{6,7},{7,6},{8,9},{9,8},{10,11... | collective-permute-start | bytes 786440 | tf_op jit(solution)/shard_map/ppermute | solution.py:451
  62.0 1.2 %collective-permute-done.16.refs_9_ = bf16[128,32,128]{2,1,0:T(8,128)(2,1)S(1)} collective-permute-done((bf16[128,32,128]{2,1,0:T(8,128)(2,1)S(1)}, bf16[128,32,128]{2,1,0:T(8,128)(2,1)S(1)}, u32[]{:S(2)}, u32[]{:S(2)}) %collective-permute-start.16) | collective-permute-done | bytes 1048608 | tf_op jit(solution)/shard_map/ppermute | solution.py:458
  63.2 1.8 %fields.1.descended_in = f32[8,64,64]{2,1,0:T(8,128)S(1)} custom-call(s32[8]{0:T(128)S(1)} %copy-done.7, s32[2,16]{1,0:T(2,128)S(1)} %copy-done.8, bf16[16,32,128]{2,1,0:T(8,128)(2,1)S(1)} %bitcast.18, bf16[16,32,128]{2,1,0:T(8,128)(2,1)S(1)} %collective-permute-done.6.refs_1_, bf16[16,32,128]{2,1,0:T(8,128)(2,1)S(1)} %collective-permute-done.7.refs_2_, ...), custom_call_target="tpu_custom_call" | custom-call | flops 50000000 | bytes 4000000 | tf_op jit(solution)/shard_map/fields/pallas_call | solution.py:313
  65.1 0.0 copy-start.2
  65.1 0.7 copy-done.2
  65.8 4.3 %all-to-all-done.1 = bf16[16,16,32,128]{3,2,1,0:T(8,128)(2,1)} async-done(((bf16[16,16,32,128]{3,2,1,0:T(8,128)(2,1)}), bf16[16,16,32,128]{3,2,1,0:T(8,128)(2,1)}, u32[]{:S(2)}, u32[]{:S(2)}) %all-to-all-start.1) | async-done | bytes 2097184 | tf_op jit(solution)/shard_map/all_to_all | solution.py:447
  70.1 4.1 %downward.1 = f32[64,2048]{1,0:T(8,128)} custom-call(s32[1,256]{1,0:T(1,128)} %copy-done.10, bf16[256,32,128]{2,1,0:T(8,128)(2,1)} %bitcast.9.blocks_in, bf16[8,64,1536]{2,1,0:T(8,128)(2,1)} %coupling_in.1, f32[8,64,64]{2,1,0:T(8,128)} %copy-done.2, bf16[8,64,256]{2,1,0:T(8,128)(2,1)} %basis_in.3, f32[64,2048]{1,0:T(8,128)} %copy-done.4), custom_call_target="tpu_custom_call" | custom-call | flops 150000000 | bytes 6000000 | tf_op jit(solution)/shard_map/downward/pallas_call | solution.py:377
  74.2 0.4 collective-permute-done.17
  74.6 1.8 %add_convert_fusion = bf16[64,2048]{1,0:T(8,128)(2,1)} fusion(f32[64,2048]{1,0:T(8,128)} %downward.1, bf16[64,2048]{1,0:T(8,128)(2,1)S(1)} %collective-permute-done.17), kind=kLoop, calls=%fused_computation | loop fusion | flops 393216 | bytes 1048576 | tf_op jit(solution)/shard_map/convert_element_type | solution.py:462
  (42 shorter events, 0.3 us)
Async XLA Ops:
  0.0 4.3 %collective-permute-start = (s32[8,24]{1,0:T(8,128)}, s32[8,24]{1,0:T(8,128)S(1)}, u32[]{:S(2)}, u32[]{:S(2)}) collective-permute-start(s32[8,24]{1,0:T(8,128)} %own_list_in.1), channel_id=1, source_target_pairs={{0,2},{2,0},{4,6},{6,4},{8,10},{10,8},{12,14},{14,12},{16,18},{18,... | collective-permute-start | bytes 2312 | tf_op jit(solution)/shard_map/ppermute | solution.py:418
  3.2 18.1 %collective-permute-start.1 = (bf16[64,2048]{1,0:T(8,128)(2,1)}, bf16[64,2048]{1,0:T(8,128)(2,1)S(1)}, u32[]{:S(2)}, u32[]{:S(2)}) collective-permute-start(bf16[64,2048]{1,0:T(8,128)(2,1)} %signals.1), channel_id=1, source_target_pairs={{0,1},{1,0},{2,3},{3,2},{4,5},{5,4},{6,7},{7,6},{8,9},{9,8},{10,11... | collective-permute-start | bytes 786440 | tf_op jit(solution)/shard_map/ppermute | solution.py:417
  4.3 0.6 copy-start.11
  7.2 9.6 %collective-permute-start.2 = (bf16[80,128]{1,0:T(8,128)(2,1)}, bf16[80,128]{1,0:T(8,128)(2,1)S(1)}, u32[]{:S(2)}, u32[]{:S(2)}) collective-permute-start(bf16[80,128]{1,0:T(8,128)(2,1)} %get-tuple-element.18), channel_id=1, source_target_pairs={{0,4},{2,6},{4,0},{6,2},{8,12},{10,14},{12,8},{14,10},{16,20},{18,... | collective-permute-start | bytes 61448 | tf_op jit(solution)/shard_map/ppermute | solution.py:422
  8.6 25.7 %all-to-all-start = ((bf16[8,8,32,128]{3,2,1,0:T(8,128)(2,1)}), bf16[8,8,32,128]{3,2,1,0:T(8,128)(2,1)S(1)}, u32[]{:S(2)}, u32[]{:S(2)}) async-start(bf16[8,8,32,128]{3,2,1,0:T(8,128)(2,1)} %get-tuple-element.19), calls=%async_computation | async-start | bytes 1048576 | tf_op jit(solution)/shard_map/all_to_all | solution.py:421
  17.6 6.7 %collective-permute-start.3 = (bf16[2,80,128]{2,1,0:T(8,128)(2,1)S(1)}, bf16[2,80,128]{2,1,0:T(8,128)(2,1)S(1)}, u32[]{:S(2)}, u32[]{:S(2)}) collective-permute-start(bf16[2,80,128]{2,1,0:T(8,128)(2,1)S(1)} %get-tuple-element.34), channel_id=1, source_target_pairs={{0,24},{2,26},{4,28},{6,30},{8,0},{10,2},{12,4},{14,6},{16,8},{18,... | collective-permute-start | bytes 122888 | tf_op jit(solution)/shard_map/ppermute | solution.py:426
  20.3 4.7 %collective-permute-start.4 = (bf16[2,80,128]{2,1,0:T(8,128)(2,1)S(1)}, bf16[2,80,128]{2,1,0:T(8,128)(2,1)S(1)}, u32[]{:S(2)}, u32[]{:S(2)}) collective-permute-start(bf16[2,80,128]{2,1,0:T(8,128)(2,1)S(1)} %get-tuple-element.34), channel_id=1, source_target_pairs={{0,16},{2,18},{4,20},{6,22},{8,24},{10,26},{12,28},{14,30},{16,0},... | collective-permute-start | bytes 122888 | tf_op jit(solution)/shard_map/ppermute | solution.py:426
  20.6 4.7 %collective-permute-start.5 = (bf16[2,80,128]{2,1,0:T(8,128)(2,1)S(1)}, bf16[2,80,128]{2,1,0:T(8,128)(2,1)S(1)}, u32[]{:S(2)}, u32[]{:S(2)}) collective-permute-start(bf16[2,80,128]{2,1,0:T(8,128)(2,1)S(1)} %get-tuple-element.34), channel_id=1, source_target_pairs={{0,8},{2,10},{4,12},{6,14},{8,16},{10,18},{12,20},{14,22},{16,24},... | collective-permute-start | bytes 122888 | tf_op jit(solution)/shard_map/ppermute | solution.py:426
  21.4 21.5 %collective-permute-start.8 = (bf16[128,1024]{1,0:T(8,128)(2,1)S(1)}, bf16[128,1024]{1,0:T(8,128)(2,1)S(1)}, u32[]{:S(2)}, u32[]{:S(2)}) collective-permute-start(bf16[128,1024]{1,0:T(8,128)(2,1)S(1)} %pad_maximum_fusion), channel_id=1, source_target_pairs={{0,2},{2,4},{4,6},{6,8},{8,10},{10,12},{12,14},{14,16},{16,18},{18... | collective-permute-start | bytes 786440 | tf_op jit(solution)/shard_map/ppermute | solution.py:438
  24.2 18.7 %collective-permute-start.9 = (bf16[128,1024]{1,0:T(8,128)(2,1)S(1)}, bf16[128,1024]{1,0:T(8,128)(2,1)S(1)}, u32[]{:S(2)}, u32[]{:S(2)}) collective-permute-start(bf16[128,1024]{1,0:T(8,128)(2,1)S(1)} %pad_maximum_fusion.1), channel_id=1, source_target_pairs={{2,0},{4,2},{6,4},{8,6},{10,8},{12,10},{14,12},{16,14},{18,16},{20... | collective-permute-start | bytes 786440 | tf_op jit(solution)/shard_map/ppermute | solution.py:441
  25.4 17.5 %collective-permute-start.6 = (bf16[16,32,128]{2,1,0:T(8,128)(2,1)S(1)}, bf16[16,32,128]{2,1,0:T(8,128)(2,1)S(1)}, u32[]{:S(2)}, u32[]{:S(2)}) collective-permute-start(bf16[16,32,128]{2,1,0:T(8,128)(2,1)S(1)} %bitcast.15), channel_id=1, source_target_pairs={{0,224},{2,226},{4,228},{6,230},{8,232},{10,234},{12,236},{14,238}... | collective-permute-start | bytes 393224 | tf_op jit(solution)/shard_map/ppermute | solution.py:434
  28.1 14.7 %collective-permute-start.7 = (bf16[16,32,128]{2,1,0:T(8,128)(2,1)S(1)}, bf16[16,32,128]{2,1,0:T(8,128)(2,1)S(1)}, u32[]{:S(2)}, u32[]{:S(2)}) collective-permute-start(bf16[16,32,128]{2,1,0:T(8,128)(2,1)S(1)} %bitcast.16), channel_id=1, source_target_pairs={{0,32},{2,34},{4,36},{6,38},{8,40},{10,42},{12,44},{14,46},{16,48}... | collective-permute-start | bytes 393224 | tf_op jit(solution)/shard_map/ppermute | solution.py:434
  36.5 8.0 %copy-start.1 = (bf16[64,2048]{1,0:T(8,128)(2,1)S(1)}, bf16[64,2048]{1,0:T(8,128)(2,1)}, u32[]{:S(2)}) copy-start(bf16[64,2048]{1,0:T(8,128)(2,1)} %signals.1) | copy-start | bytes 786436
  36.6 8.0 %copy-start.6 = (s32[8,8]{1,0:T(8,128)S(1)}, s32[8,8]{1,0:T(8,128)}, u32[]{:S(2)}) copy-start(s32[8,8]{1,0:T(8,128)} %near_list.1) | copy-start | bytes 772
  36.6 8.0 %copy-start.9 = (s32[1,256]{1,0:T(1,128)S(1)}, s32[1,256]{1,0:T(1,128)}, u32[]{:S(2)}) copy-start(s32[1,256]{1,0:T(1,128)} %get-tuple-element.17.own_row) | copy-start | bytes 3076
  36.6 33.5 %all-to-all-start.1 = ((bf16[16,16,32,128]{3,2,1,0:T(8,128)(2,1)}), bf16[16,16,32,128]{3,2,1,0:T(8,128)(2,1)}, u32[]{:S(2)}, u32[]{:S(2)}) async-start(bf16[16,16,32,128]{3,2,1,0:T(8,128)(2,1)} %select.1), calls=%async_computation.1 | async-start | bytes 4194304 | tf_op jit(solution)/shard_map/all_to_all | solution.py:447
  42.9 6.1 %collective-permute-start.10 = (bf16[16,32,128]{2,1,0:T(8,128)(2,1)S(1)}, bf16[16,32,128]{2,1,0:T(8,128)(2,1)S(1)}, u32[]{:S(2)}, u32[]{:S(2)}) collective-permute-start(bf16[16,32,128]{2,1,0:T(8,128)(2,1)S(1)} %collective-permute-done.6.refs_1_), channel_id=1, source_target_pairs={{0,224},{2,226},{4,228},{6,230},{8,232},{10,234},{12,236},{14,238}... | collective-permute-start | bytes 393224 | tf_op jit(solution)/shard_map/ppermute | solution.py:449
  43.0 6.3 %collective-permute-start.11 = (bf16[16,32,128]{2,1,0:T(8,128)(2,1)S(1)}, bf16[16,32,128]{2,1,0:T(8,128)(2,1)S(1)}, u32[]{:S(2)}, u32[]{:S(2)}) collective-permute-start(bf16[16,32,128]{2,1,0:T(8,128)(2,1)S(1)} %collective-permute-done.7.refs_2_), channel_id=1, source_target_pairs={{0,32},{2,34},{4,36},{6,38},{8,40},{10,42},{12,44},{14,46},{16,48}... | collective-permute-start | bytes 393224 | tf_op jit(solution)/shard_map/ppermute | solution.py:449
  44.5 2.2 %copy-start = (bf16[8,4,256,256]{3,2,1,0:T(8,128)(2,1)S(1)}, bf16[8,4,256,256]{3,2,1,0:T(8,128)(2,1)}, u32[]{:S(2)}) copy-start(bf16[8,4,256,256]{3,2,1,0:T(8,128)(2,1)} %tiles.1) | copy-start | bytes 12582916
  46.7 16.5 %copy-start.3 = (bf16[8,64,64]{2,1,0:T(8,128)(2,1)S(1)}, bf16[8,64,64]{2,1,0:T(8,128)(2,1)}, u32[]{:S(2)}) copy-start(bf16[8,64,64]{2,1,0:T(8,128)(2,1)} %refs_11_.1) | copy-start | bytes 196612
  46.7 16.5 %copy-start.5 = (bf16[2,64,1024]{2,1,0:T(8,128)(2,1)S(1)}, bf16[2,64,1024]{2,1,0:T(8,128)(2,1)}, u32[]{:S(2)}) copy-start(bf16[2,64,1024]{2,1,0:T(8,128)(2,1)} %refs_10_.1) | copy-start | bytes 786436
  46.7 16.5 %copy-start.7 = (s32[8]{0:T(128)S(1)}, s32[8]{0:T(128)}, u32[]{:S(2)}) copy-start(s32[8]{0:T(128)} %parent.1) | copy-start | bytes 100
  46.7 16.5 %copy-start.8 = (s32[2,16]{1,0:T(2,128)S(1)}, s32[2,16]{1,0:T(2,128)}, u32[]{:S(2)}) copy-start(s32[2,16]{1,0:T(2,128)} %parent_far.1) | copy-start | bytes 388
  49.0 13.0 %copy-start.4 = (f32[64,2048]{1,0:T(8,128)}, f32[64,2048]{1,0:T(8,128)S(1)}, u32[]{:S(2)}) copy-start(f32[64,2048]{1,0:T(8,128)S(1)} %get-tuple-element.28.near_own_in) | copy-start | bytes 1572868
  49.0 14.2 %copy-start.10 = (s32[1,256]{1,0:T(1,128)}, s32[1,256]{1,0:T(1,128)S(1)}, u32[]{:S(2)}) copy-start(s32[1,256]{1,0:T(1,128)S(1)} %get-tuple-element.22.slots_in) | copy-start | bytes 3076
  49.4 4.3 %collective-permute-start.12 = (bf16[16,32,128]{2,1,0:T(8,128)(2,1)S(1)}, bf16[16,32,128]{2,1,0:T(8,128)(2,1)S(1)}, u32[]{:S(2)}, u32[]{:S(2)}) collective-permute-start(bf16[16,32,128]{2,1,0:T(8,128)(2,1)S(1)} %collective-permute-done.10.refs_3_), channel_id=1, source_target_pairs={{0,224},{2,226},{4,228},{6,230},{8,232},{10,234},{12,236},{14,238}... | collective-permute-start | bytes 393224 | tf_op jit(solution)/shard_map/ppermute | solution.py:453
  50.4 5.9 %collective-permute-start.13 = (bf16[16,32,128]{2,1,0:T(8,128)(2,1)S(1)}, bf16[16,32,128]{2,1,0:T(8,128)(2,1)S(1)}, u32[]{:S(2)}, u32[]{:S(2)}) collective-permute-start(bf16[16,32,128]{2,1,0:T(8,128)(2,1)S(1)} %collective-permute-done.11.refs_4_), channel_id=1, source_target_pairs={{0,32},{2,34},{4,36},{6,38},{8,40},{10,42},{12,44},{14,46},{16,48}... | collective-permute-start | bytes 393224 | tf_op jit(solution)/shard_map/ppermute | solution.py:453
  51.2 5.9 %collective-permute-start.14 = (bf16[8,32,128]{2,1,0:T(8,128)(2,1)S(1)}, bf16[8,32,128]{2,1,0:T(8,128)(2,1)S(1)}, u32[]{:S(2)}, u32[]{:S(2)}) collective-permute-start(bf16[8,32,128]{2,1,0:T(8,128)(2,1)S(1)} %slice.30), channel_id=1, source_target_pairs={{0,192},{2,194},{4,196},{6,198},{8,200},{10,202},{12,204},{14,206}... | collective-permute-start | bytes 196616 | tf_op jit(solution)/shard_map/ppermute | solution.py:455
  52.0 5.7 %collective-permute-start.15 = (bf16[8,32,128]{2,1,0:T(8,128)(2,1)S(1)}, bf16[8,32,128]{2,1,0:T(8,128)(2,1)S(1)}, u32[]{:S(2)}, u32[]{:S(2)}) collective-permute-start(bf16[8,32,128]{2,1,0:T(8,128)(2,1)S(1)} %slice.31), channel_id=1, source_target_pairs={{0,64},{2,66},{4,68},{6,70},{8,72},{10,74},{12,76},{14,78},{16,80}... | collective-permute-start | bytes 196616 | tf_op jit(solution)/shard_map/ppermute | solution.py:456
  57.7 5.6 %collective-permute-start.16 = (bf16[128,32,128]{2,1,0:T(8,128)(2,1)S(1)}, bf16[128,32,128]{2,1,0:T(8,128)(2,1)S(1)}, u32[]{:S(2)}, u32[]{:S(2)}) collective-permute-start(bf16[128,32,128]{2,1,0:T(8,128)(2,1)S(1)} %constant_dynamic-update-slice_fusion), channel_id=1, source_target_pairs={{0,2},{2,0},{4,6},{6,4},{8,10},{10,8},{12,14},{14,12},{16,18},{18,... | collective-permute-start | bytes 3145736 | tf_op jit(solution)/shard_map/ppermute | solution.py:458
  60.9 13.6 %collective-permute-start.17 = (bf16[64,2048]{1,0:T(8,128)(2,1)S(1)}, bf16[64,2048]{1,0:T(8,128)(2,1)S(1)}, u32[]{:S(2)}, u32[]{:S(2)}) collective-permute-start(bf16[64,2048]{1,0:T(8,128)(2,1)S(1)} %get-tuple-element.25), channel_id=1, source_target_pairs={{0,1},{1,0},{2,3},{3,2},{4,5},{5,4},{6,7},{7,6},{8,9},{9,8},{10,11... | collective-permute-start | bytes 786440 | tf_op jit(solution)/shard_map/ppermute | solution.py:451
  65.1 0.7 copy-start.2

commit v7 on v6

--- a/solution.py
+++ b/solution.py
@@ -433,13 +433,14 @@
     up = functools.partial(along, perm=loop_moves(lambda z, y, x, c: (z + 1, y, x, c)))
     one_down, one_up = down(parents), up(parents)
 
+    other, late = lax.optimization_barrier((other, signals))
     reach = width // 2
     count = Z * PLANE
     before = along(
-        jnp.concatenate([signals[:, reach:], other[:, reach:]]), perm=[(i, (i + 1) % count) for i in range(count)]
+        jnp.concatenate([late[:, reach:], other[:, reach:]]), perm=[(i, (i + 1) % count) for i in range(count)]
     )
     after = along(
-        jnp.concatenate([signals[:, :reach], other[:, :reach]]), perm=[((i + 1) % count, i) for i in range(count)]
+        jnp.concatenate([late[:, :reach], other[:, :reach]]), perm=[((i + 1) % count, i) for i in range(count)]
     )
     wanted = tables(plane_lists.astype(jnp.int32))
     send = select(wanted, planes)

time: 76.8 us -> 77 us (level)
    ppermute x1, starting transfers between devices: 1.01 us -> 3.57 us  [shards(): other = swap(signals)]
    ppermute x1, starting transfers between devices: 3.24 us -> 0.96 us  [shards(): peer_list = along(far_list, perm=c_swap)]
    ppermute x3, waiting for transfers between devices: 1.08 us -> 0.02 us  [shards(): along(pair, perm=loop_moves(lambda z, y, x, c, dy=dy: (z, y - dy, x, c)))]
    ppermute x1, waiting for transfers between devices: 0.03 us -> 1.03 us  [shards(): peer_list = along(far_list, perm=c_swap)]
  transfers between devices with their start and end apart: 20 -> 20, of which waited for: 10 -> 9; matrix products, arithmetic and copies ran while one was open for 3% -> 3% of each run, Pallas kernels for 17% -> 17%
where the time goes in v7:
time: 77 us; the launch traced here: 76.6 us
  starting transfers between devices  39.1 us (51%)
  waiting for transfers between devices  16.8 us (22%)
  Pallas kernels  13.1 us (17%)
  local copies, waits for them, and re-layouts  4.68 us (6%)
  other arithmetic  2.58 us (3%)
    all_to_all x1, starting transfers between devices, shards(): lax.all_to_all(coefs, 'loop', 0, 0, tiled=True, axis_index_groups=columns...  8.18 us
    all_to_all x1, starting transfers between devices, shards(): lax.all_to_all(send, 'loop', 0, 0, tiled=True, axis_index_groups=planes_of)  6.29 us
    all_to_all x1, waiting for transfers between devices, shards(): lax.all_to_all(coefs, 'loop', 0, 0, tiled=True, axis_index_groups=columns...  5.36 us
    all_to_all x1, waiting for transfers between devices, shards(): lax.all_to_all(send, 'loop', 0, 0, tiled=True, axis_index_groups=planes_of)  4.88 us
    pallas_call x1, Pallas kernels, downward(): pl.pallas_call(downward_kernel, out_shape=jax.ShapeDtypeStruct(near_own.s...  4.09 us
    ppermute x3, starting transfers between devices, shards(): along(pair, perm=loop_moves(lambda z, y, x, c, dy=dy: (z, y - dy, x, c)))  3.78 us
    unnamed x32, local copies, waits for them, and re-layouts  3.64 us
    ppermute x1, starting transfers between devices, shards(): other = swap(signals)  3.57 us
  transfers between devices with their start and end apart: 20, of which 9 were waited for; matrix products, arithmetic and copies ran while one was open for 3% of the time, Pallas kernels for 17%

profile of v7, /device:TPU:1, one launch (start us, length us, event | category | flops | bytes accessed | tf_op | source)
XLA Modules:
  0.0 76.6 jit_solution(12154237644528339474)
XLA Ops:
  0.0 3.6 %collective-permute-start.1 = (bf16[64,2048]{1,0:T(8,128)(2,1)}, bf16[64,2048]{1,0:T(8,128)(2,1)S(1)}, u32[]{:S(2)}, u32[]{:S(2)}) collective-permute-start(bf16[64,2048]{1,0:T(8,128)(2,1)} %signals.1), channel_id=1, source_target_pairs={{0,1},{1,0},{2,3},{3,2},{4,5},{5,4},{6,7},{7,6},{8,9},{9,8},{10,11... | collective-permute-start | bytes 786440 | tf_op jit(solution)/shard_map/ppermute | solution.py:417
  3.6 1.0 %collective-permute-start = (s32[8,24]{1,0:T(8,128)}, s32[8,24]{1,0:T(8,128)S(1)}, u32[]{:S(2)}, u32[]{:S(2)}) collective-permute-start(s32[8,24]{1,0:T(8,128)} %own_list_in.1), channel_id=1, source_target_pairs={{0,2},{2,0},{4,6},{6,4},{8,10},{10,8},{12,14},{14,12},{16,18},{18,... | collective-permute-start | bytes 2312 | tf_op jit(solution)/shard_map/ppermute | solution.py:418
  4.5 1.0 %collective-permute-done.peer_list_in = s32[8,24]{1,0:T(8,128)S(1)} collective-permute-done((s32[8,24]{1,0:T(8,128)}, s32[8,24]{1,0:T(8,128)S(1)}, u32[]{:S(2)}, u32[]{:S(2)}) %collective-permute-start) | collective-permute-done | bytes 800 | tf_op jit(solution)/shard_map/ppermute | solution.py:418
  5.6 0.6 copy-done.11
  6.2 2.4 %upward.1 = (bf16[8,8,32,128]{3,2,1,0:T(8,128)(2,1)}, bf16[80,128]{1,0:T(8,128)(2,1)}, s32[1,256]{1,0:T(1,128)}) custom-call(s32[8]{0:T(128)} %parent.1, s32[8,24]{1,0:T(8,128)} %own_list_in.1, s32[8,24]{1,0:T(8,128)} %copy-done.11, bf16[64,2048]{1,0:T(8,128)(2,1)} %signals.1, bf16[8,64,256]{2,1,0:T(8,128)(2,1)} %basis_in.3, bf16[8,64,64]{2,1,0:T(8,128)(2,1)} %refs_11_.1), custom_call_target="tpu_custom_call" | custom-call | flops 30000000 | bytes 700000 | tf_op jit(solution)/shard_map/upward/pallas_call | solution.py:163
  8.5 0.4 collective-permute-start.2
  8.9 8.2 %all-to-all-start = ((bf16[8,8,32,128]{3,2,1,0:T(8,128)(2,1)}), bf16[8,8,32,128]{3,2,1,0:T(8,128)(2,1)S(1)}, u32[]{:S(2)}, u32[]{:S(2)}) async-start(bf16[8,8,32,128]{3,2,1,0:T(8,128)(2,1)} %get-tuple-element.22), calls=%async_computation | async-start | bytes 1048576 | tf_op jit(solution)/shard_map/all_to_all | solution.py:421
  17.1 0.0 collective-permute-done.2
  17.1 0.7 fusion
  17.9 2.7 %collective-permute-start.3 = (bf16[2,80,128]{2,1,0:T(8,128)(2,1)S(1)}, bf16[2,80,128]{2,1,0:T(8,128)(2,1)S(1)}, u32[]{:S(2)}, u32[]{:S(2)}) collective-permute-start(bf16[2,80,128]{2,1,0:T(8,128)(2,1)S(1)} %get-tuple-element.38), channel_id=1, source_target_pairs={{0,24},{2,26},{4,28},{6,30},{8,0},{10,2},{12,4},{14,6},{16,8},{18,... | collective-permute-start | bytes 122888 | tf_op jit(solution)/shard_map/ppermute | solution.py:426
  20.6 0.3 collective-permute-start.4
  20.9 0.7 collective-permute-start.5
  21.6 1.0 %fusion.1 = (bf16[64,1024]{1,0:T(8,128)(2,1)S(1)}, bf16[64,1024]{1,0:T(8,128)(2,1)S(1)}, bf16[64,1024]{1,0:T(8,128)(2,1)S(1)}, bf16[64,1024]{1,0:T(8,128)(2,1)S(1)}) fusion(bf16[64,2048]{1,0:T(8,128)(2,1)} %signals.1, bf16[64,2048]{1,0:T(8,128)(2,1)S(1)} %collective-permute-done.1.other), kind=kLoop, calls=%fused_computation.19 | loop fusion | bytes 1048576 | tf_op jit(solution)/shard_map/slice | solution.py:443
  22.7 2.9 %collective-permute-start.8 = (bf16[128,1024]{1,0:T(8,128)(2,1)S(1)}, bf16[128,1024]{1,0:T(8,128)(2,1)S(1)}, u32[]{:S(2)}, u32[]{:S(2)}) collective-permute-start(bf16[128,1024]{1,0:T(8,128)(2,1)S(1)} %pad_maximum_fusion), channel_id=1, source_target_pairs={{0,2},{2,4},{4,6},{6,8},{8,10},{10,12},{12,14},{14,16},{16,18},{18... | collective-permute-start | bytes 786440 | tf_op jit(solution)/shard_map/ppermute | solution.py:439
  25.6 0.1 collective-permute-start.9
  25.7 0.0 collective-permute-done.4
  25.7 0.0 collective-permute-done.5
  25.7 3.0 %collective-permute-start.6 = (bf16[16,32,128]{2,1,0:T(8,128)(2,1)S(1)}, bf16[16,32,128]{2,1,0:T(8,128)(2,1)S(1)}, u32[]{:S(2)}, u32[]{:S(2)}) collective-permute-start(bf16[16,32,128]{2,1,0:T(8,128)(2,1)S(1)} %bitcast.15), channel_id=1, source_target_pairs={{0,224},{2,226},{4,228},{6,230},{8,232},{10,234},{12,236},{14,238}... | collective-permute-start | bytes 393224 | tf_op jit(solution)/shard_map/ppermute | solution.py:434
  28.7 0.0 collective-permute-start.7
  28.7 0.4 tables.1.wanted
  29.2 5.4 %all-to-all-done.planes = bf16[8,8,32,128]{3,2,1,0:T(8,128)(2,1)S(1)} async-done(((bf16[8,8,32,128]{3,2,1,0:T(8,128)(2,1)}), bf16[8,8,32,128]{3,2,1,0:T(8,128)(2,1)S(1)}, u32[]{:S(2)}, u32[]{:S(2)}) %all-to-all-start) | async-done | bytes 524320 | tf_op jit(solution)/shard_map/all_to_all | solution.py:421
  34.6 2.2 %select.1 = bf16[16,16,32,128]{3,2,1,0:T(8,128)(2,1)} custom-call(s32[16,128]{1,0:T(8,128)S(1)} %tables.1.wanted, bf16[8,8,32,128]{3,2,1,0:T(8,128)(2,1)S(1)} %all-to-all-done.planes), custom_call_target="tpu_custom_call" | custom-call | flops 1000000 | bytes 2500000 | tf_op jit(solution)/shard_map/select/pallas_call | solution.py:207
  36.8 0.0 copy-start.1
  36.8 0.0 copy-start.6
  36.8 6.3 %all-to-all-start.1 = ((bf16[16,16,32,128]{3,2,1,0:T(8,128)(2,1)}), bf16[16,16,32,128]{3,2,1,0:T(8,128)(2,1)}, u32[]{:S(2)}, u32[]{:S(2)}) async-start(bf16[16,16,32,128]{3,2,1,0:T(8,128)(2,1)} %select.1), calls=%async_computation.1 | async-start | bytes 4194304 | tf_op jit(solution)/shard_map/all_to_all | solution.py:448
  43.1 0.1 collective-permute-start.10
  43.3 1.5 %collective-permute-start.11 = (bf16[16,32,128]{2,1,0:T(8,128)(2,1)S(1)}, bf16[16,32,128]{2,1,0:T(8,128)(2,1)S(1)}, u32[]{:S(2)}, u32[]{:S(2)}) collective-permute-start(bf16[16,32,128]{2,1,0:T(8,128)(2,1)S(1)} %collective-permute-done.7.refs_2_), channel_id=1, source_target_pairs={{0,32},{2,34},{4,36},{6,38},{8,40},{10,42},{12,44},{14,46},{16,48}... | collective-permute-start | bytes 393224 | tf_op jit(solution)/shard_map/ppermute | solution.py:450
  44.8 2.2 %copy-done = bf16[8,4,256,256]{3,2,1,0:T(8,128)(2,1)S(1)} copy-done((bf16[8,4,256,256]{3,2,1,0:T(8,128)(2,1)S(1)}, bf16[8,4,256,256]{3,2,1,0:T(8,128)(2,1)}, u32[]{:S(2)}) %copy-start) | copy-done | bytes 4194328
  47.0 2.2 %near_field.1 = (f32[64,2048]{1,0:T(8,128)S(1)}, bf16[64,2048]{1,0:T(8,128)(2,1)S(1)}, s32[1,256]{1,0:T(1,128)S(1)}) custom-call(s32[8,8]{1,0:T(8,128)S(1)} %copy-done.6, s32[1,256]{1,0:T(1,128)S(1)} %copy-done.9, bf16[64,2048]{1,0:T(8,128)(2,1)S(1)} %copy-done.1, bf16[64,2048]{1,0:T(8,128)(2,1)S(1)} %collective-permute-done.1.other, ...), custom_call_target="tpu_custom_call" | custom-call | flops 600000000 | bytes 10000000 | tf_op jit(solution)/shard_map/near_field/pallas_call | solution.py:259
  49.3 0.3 collective-permute-done.11.refs_4_
  49.6 1.0 %collective-permute-start.12 = (bf16[16,32,128]{2,1,0:T(8,128)(2,1)S(1)}, bf16[16,32,128]{2,1,0:T(8,128)(2,1)S(1)}, u32[]{:S(2)}, u32[]{:S(2)}) collective-permute-start(bf16[16,32,128]{2,1,0:T(8,128)(2,1)S(1)} %collective-permute-done.10.refs_3_), channel_id=1, source_target_pairs={{0,224},{2,226},{4,228},{6,230},{8,232},{10,234},{12,236},{14,238}... | collective-permute-start | bytes 393224 | tf_op jit(solution)/shard_map/ppermute | solution.py:454
  50.6 0.7 collective-permute-start.13
  51.4 0.8 %collective-permute-start.14 = (bf16[8,32,128]{2,1,0:T(8,128)(2,1)S(1)}, bf16[8,32,128]{2,1,0:T(8,128)(2,1)S(1)}, u32[]{:S(2)}, u32[]{:S(2)}) collective-permute-start(bf16[8,32,128]{2,1,0:T(8,128)(2,1)S(1)} %slice.30), channel_id=1, source_target_pairs={{0,192},{2,194},{4,196},{6,198},{8,200},{10,202},{12,204},{14,206}... | collective-permute-start | bytes 196616 | tf_op jit(solution)/shard_map/ppermute | solution.py:456
  52.2 1.6 %collective-permute-start.15 = (bf16[8,32,128]{2,1,0:T(8,128)(2,1)S(1)}, bf16[8,32,128]{2,1,0:T(8,128)(2,1)S(1)}, u32[]{:S(2)}, u32[]{:S(2)}) collective-permute-start(bf16[8,32,128]{2,1,0:T(8,128)(2,1)S(1)} %slice.31), channel_id=1, source_target_pairs={{0,64},{2,66},{4,68},{6,70},{8,72},{10,74},{12,76},{14,78},{16,80}... | collective-permute-start | bytes 196616 | tf_op jit(solution)/shard_map/ppermute | solution.py:457
  53.8 0.0 collective-permute-done.12.refs_5_
  53.9 2.6 %collective-permute-done.13.refs_6_ = bf16[16,32,128]{2,1,0:T(8,128)(2,1)S(1)} collective-permute-done((bf16[16,32,128]{2,1,0:T(8,128)(2,1)S(1)}, bf16[16,32,128]{2,1,0:T(8,128)(2,1)S(1)}, u32[]{:S(2)}, u32[]{:S(2)}) %collective-permute-start.13) | collective-permute-done | bytes 131104 | tf_op jit(solution)/shard_map/ppermute | solution.py:454
  56.5 0.8 collective-permute-done.14.refs_7_
  57.3 0.5 collective-permute-done.15.refs_8_
  57.8 2.8 %collective-permute-start.16 = (bf16[128,32,128]{2,1,0:T(8,128)(2,1)S(1)}, bf16[128,32,128]{2,1,0:T(8,128)(2,1)S(1)}, u32[]{:S(2)}, u32[]{:S(2)}) collective-permute-start(bf16[128,32,128]{2,1,0:T(8,128)(2,1)S(1)} %constant_dynamic-update-slice_fusion), channel_id=1, source_target_pairs={{0,2},{2,0},{4,6},{6,4},{8,10},{10,8},{12,14},{14,12},{16,18},{18,... | collective-permute-start | bytes 3145736 | tf_op jit(solution)/shard_map/ppermute | solution.py:459
  60.6 1.4 %collective-permute-start.17 = (bf16[64,2048]{1,0:T(8,128)(2,1)S(1)}, bf16[64,2048]{1,0:T(8,128)(2,1)S(1)}, u32[]{:S(2)}, u32[]{:S(2)}) collective-permute-start(bf16[64,2048]{1,0:T(8,128)(2,1)S(1)} %get-tuple-element.29), channel_id=1, source_target_pairs={{0,1},{1,0},{2,3},{3,2},{4,5},{5,4},{6,7},{7,6},{8,9},{9,8},{10,11... | collective-permute-start | bytes 786440 | tf_op jit(solution)/shard_map/ppermute | solution.py:452
  62.0 0.9 %collective-permute-done.16.refs_9_ = bf16[128,32,128]{2,1,0:T(8,128)(2,1)S(1)} collective-permute-done((bf16[128,32,128]{2,1,0:T(8,128)(2,1)S(1)}, bf16[128,32,128]{2,1,0:T(8,128)(2,1)S(1)}, u32[]{:S(2)}, u32[]{:S(2)}) %collective-permute-start.16) | collective-permute-done | bytes 1048608 | tf_op jit(solution)/shard_map/ppermute | solution.py:459
  62.9 1.8 %fields.1.descended_in = f32[8,64,64]{2,1,0:T(8,128)S(1)} custom-call(s32[8]{0:T(128)S(1)} %copy-done.7, s32[2,16]{1,0:T(2,128)S(1)} %copy-done.8, bf16[16,32,128]{2,1,0:T(8,128)(2,1)S(1)} %bitcast.18, bf16[16,32,128]{2,1,0:T(8,128)(2,1)S(1)} %collective-permute-done.6.refs_1_, bf16[16,32,128]{2,1,0:T(8,128)(2,1)S(1)} %collective-permute-done.7.refs_2_, ...), custom_call_target="tpu_custom_call" | custom-call | flops 50000000 | bytes 4000000 | tf_op jit(solution)/shard_map/fields/pallas_call | solution.py:313
  64.7 0.0 copy-start.2
  64.7 0.7 copy-done.2
  65.4 4.9 %all-to-all-done.1 = bf16[16,16,32,128]{3,2,1,0:T(8,128)(2,1)} async-done(((bf16[16,16,32,128]{3,2,1,0:T(8,128)(2,1)}), bf16[16,16,32,128]{3,2,1,0:T(8,128)(2,1)}, u32[]{:S(2)}, u32[]{:S(2)}) %all-to-all-start.1) | async-done | bytes 2097184 | tf_op jit(solution)/shard_map/all_to_all | solution.py:448
  70.3 4.1 %downward.1 = f32[64,2048]{1,0:T(8,128)} custom-call(s32[1,256]{1,0:T(1,128)} %copy-done.10, bf16[256,32,128]{2,1,0:T(8,128)(2,1)} %bitcast.9.blocks_in, bf16[8,64,1536]{2,1,0:T(8,128)(2,1)} %coupling_in.1, f32[8,64,64]{2,1,0:T(8,128)} %copy-done.2, bf16[8,64,256]{2,1,0:T(8,128)(2,1)} %basis_in.3, f32[64,2048]{1,0:T(8,128)} %copy-done.4), custom_call_target="tpu_custom_call" | custom-call | flops 150000000 | bytes 6000000 | tf_op jit(solution)/shard_map/downward/pallas_call | solution.py:377
  74.4 0.3 collective-permute-done.17
  74.8 1.8 %add_convert_fusion = bf16[64,2048]{1,0:T(8,128)(2,1)} fusion(f32[64,2048]{1,0:T(8,128)} %downward.1, bf16[64,2048]{1,0:T(8,128)(2,1)S(1)} %collective-permute-done.17), kind=kLoop, calls=%fused_computation | loop fusion | flops 393216 | bytes 1048576 | tf_op jit(solution)/shard_map/convert_element_type | solution.py:463
  (41 shorter events, 0.3 us)
Async XLA Ops:
  0.0 21.6 %collective-permute-start.1 = (bf16[64,2048]{1,0:T(8,128)(2,1)}, bf16[64,2048]{1,0:T(8,128)(2,1)S(1)}, u32[]{:S(2)}, u32[]{:S(2)}) collective-permute-start(bf16[64,2048]{1,0:T(8,128)(2,1)} %signals.1), channel_id=1, source_target_pairs={{0,1},{1,0},{2,3},{3,2},{4,5},{5,4},{6,7},{7,6},{8,9},{9,8},{10,11... | collective-permute-start | bytes 786440 | tf_op jit(solution)/shard_map/ppermute | solution.py:417
  3.6 2.0 %collective-permute-start = (s32[8,24]{1,0:T(8,128)}, s32[8,24]{1,0:T(8,128)S(1)}, u32[]{:S(2)}, u32[]{:S(2)}) collective-permute-start(s32[8,24]{1,0:T(8,128)} %own_list_in.1), channel_id=1, source_target_pairs={{0,2},{2,0},{4,6},{6,4},{8,10},{10,8},{12,14},{14,12},{16,18},{18,... | collective-permute-start | bytes 2312 | tf_op jit(solution)/shard_map/ppermute | solution.py:418
  5.6 0.6 copy-start.11
  8.5 8.6 %collective-permute-start.2 = (bf16[80,128]{1,0:T(8,128)(2,1)}, bf16[80,128]{1,0:T(8,128)(2,1)S(1)}, u32[]{:S(2)}, u32[]{:S(2)}) collective-permute-start(bf16[80,128]{1,0:T(8,128)(2,1)} %get-tuple-element.21), channel_id=1, source_target_pairs={{0,4},{2,6},{4,0},{6,2},{8,12},{10,14},{12,8},{14,10},{16,20},{18,... | collective-permute-start | bytes 61448 | tf_op jit(solution)/shard_map/ppermute | solution.py:422
  8.9 25.6 %all-to-all-start = ((bf16[8,8,32,128]{3,2,1,0:T(8,128)(2,1)}), bf16[8,8,32,128]{3,2,1,0:T(8,128)(2,1)S(1)}, u32[]{:S(2)}, u32[]{:S(2)}) async-start(bf16[8,8,32,128]{3,2,1,0:T(8,128)(2,1)} %get-tuple-element.22), calls=%async_computation | async-start | bytes 1048576 | tf_op jit(solution)/shard_map/all_to_all | solution.py:421
  17.9 7.8 %collective-permute-start.3 = (bf16[2,80,128]{2,1,0:T(8,128)(2,1)S(1)}, bf16[2,80,128]{2,1,0:T(8,128)(2,1)S(1)}, u32[]{:S(2)}, u32[]{:S(2)}) collective-permute-start(bf16[2,80,128]{2,1,0:T(8,128)(2,1)S(1)} %get-tuple-element.38), channel_id=1, source_target_pairs={{0,24},{2,26},{4,28},{6,30},{8,0},{10,2},{12,4},{14,6},{16,8},{18,... | collective-permute-start | bytes 122888 | tf_op jit(solution)/shard_map/ppermute | solution.py:426
  20.6 5.1 %collective-permute-start.4 = (bf16[2,80,128]{2,1,0:T(8,128)(2,1)S(1)}, bf16[2,80,128]{2,1,0:T(8,128)(2,1)S(1)}, u32[]{:S(2)}, u32[]{:S(2)}) collective-permute-start(bf16[2,80,128]{2,1,0:T(8,128)(2,1)S(1)} %get-tuple-element.38), channel_id=1, source_target_pairs={{0,16},{2,18},{4,20},{6,22},{8,24},{10,26},{12,28},{14,30},{16,0},... | collective-permute-start | bytes 122888 | tf_op jit(solution)/shard_map/ppermute | solution.py:426
  20.9 4.7 %collective-permute-start.5 = (bf16[2,80,128]{2,1,0:T(8,128)(2,1)S(1)}, bf16[2,80,128]{2,1,0:T(8,128)(2,1)S(1)}, u32[]{:S(2)}, u32[]{:S(2)}) collective-permute-start(bf16[2,80,128]{2,1,0:T(8,128)(2,1)S(1)} %get-tuple-element.38), channel_id=1, source_target_pairs={{0,8},{2,10},{4,12},{6,14},{8,16},{10,18},{12,20},{14,22},{16,24},... | collective-permute-start | bytes 122888 | tf_op jit(solution)/shard_map/ppermute | solution.py:426
  22.7 20.4 %collective-permute-start.8 = (bf16[128,1024]{1,0:T(8,128)(2,1)S(1)}, bf16[128,1024]{1,0:T(8,128)(2,1)S(1)}, u32[]{:S(2)}, u32[]{:S(2)}) collective-permute-start(bf16[128,1024]{1,0:T(8,128)(2,1)S(1)} %pad_maximum_fusion), channel_id=1, source_target_pairs={{0,2},{2,4},{4,6},{6,8},{8,10},{10,12},{12,14},{14,16},{16,18},{18... | collective-permute-start | bytes 786440 | tf_op jit(solution)/shard_map/ppermute | solution.py:439
  25.6 17.6 %collective-permute-start.9 = (bf16[128,1024]{1,0:T(8,128)(2,1)S(1)}, bf16[128,1024]{1,0:T(8,128)(2,1)S(1)}, u32[]{:S(2)}, u32[]{:S(2)}) collective-permute-start(bf16[128,1024]{1,0:T(8,128)(2,1)S(1)} %pad_maximum_fusion.1), channel_id=1, source_target_pairs={{2,0},{4,2},{6,4},{8,6},{10,8},{12,10},{14,12},{16,14},{18,16},{20... | collective-permute-start | bytes 786440 | tf_op jit(solution)/shard_map/ppermute | solution.py:442
  25.7 17.4 %collective-permute-start.6 = (bf16[16,32,128]{2,1,0:T(8,128)(2,1)S(1)}, bf16[16,32,128]{2,1,0:T(8,128)(2,1)S(1)}, u32[]{:S(2)}, u32[]{:S(2)}) collective-permute-start(bf16[16,32,128]{2,1,0:T(8,128)(2,1)S(1)} %bitcast.15), channel_id=1, source_target_pairs={{0,224},{2,226},{4,228},{6,230},{8,232},{10,234},{12,236},{14,238}... | collective-permute-start | bytes 393224 | tf_op jit(solution)/shard_map/ppermute | solution.py:434
  28.7 14.4 %collective-permute-start.7 = (bf16[16,32,128]{2,1,0:T(8,128)(2,1)S(1)}, bf16[16,32,128]{2,1,0:T(8,128)(2,1)S(1)}, u32[]{:S(2)}, u32[]{:S(2)}) collective-permute-start(bf16[16,32,128]{2,1,0:T(8,128)(2,1)S(1)} %bitcast.16), channel_id=1, source_target_pairs={{0,32},{2,34},{4,36},{6,38},{8,40},{10,42},{12,44},{14,46},{16,48}... | collective-permute-start | bytes 393224 | tf_op jit(solution)/shard_map/ppermute | solution.py:434
  36.8 8.0 %copy-start.1 = (bf16[64,2048]{1,0:T(8,128)(2,1)S(1)}, bf16[64,2048]{1,0:T(8,128)(2,1)}, u32[]{:S(2)}) copy-start(bf16[64,2048]{1,0:T(8,128)(2,1)} %signals.1) | copy-start | bytes 786436
  36.8 8.0 %copy-start.6 = (s32[8,8]{1,0:T(8,128)S(1)}, s32[8,8]{1,0:T(8,128)}, u32[]{:S(2)}) copy-start(s32[8,8]{1,0:T(8,128)} %near_list.1) | copy-start | bytes 772
  36.8 8.0 %copy-start.9 = (s32[1,256]{1,0:T(1,128)S(1)}, s32[1,256]{1,0:T(1,128)}, u32[]{:S(2)}) copy-start(s32[1,256]{1,0:T(1,128)} %get-tuple-element.19.own_row) | copy-start | bytes 3076
  36.8 33.5 %all-to-all-start.1 = ((bf16[16,16,32,128]{3,2,1,0:T(8,128)(2,1)}), bf16[16,16,32,128]{3,2,1,0:T(8,128)(2,1)}, u32[]{:S(2)}, u32[]{:S(2)}) async-start(bf16[16,16,32,128]{3,2,1,0:T(8,128)(2,1)} %select.1), calls=%async_computation.1 | async-start | bytes 4194304 | tf_op jit(solution)/shard_map/all_to_all | solution.py:448
  43.1 6.1 %collective-permute-start.10 = (bf16[16,32,128]{2,1,0:T(8,128)(2,1)S(1)}, bf16[16,32,128]{2,1,0:T(8,128)(2,1)S(1)}, u32[]{:S(2)}, u32[]{:S(2)}) collective-permute-start(bf16[16,32,128]{2,1,0:T(8,128)(2,1)S(1)} %collective-permute-done.6.refs_1_), channel_id=1, source_target_pairs={{0,224},{2,226},{4,228},{6,230},{8,232},{10,234},{12,236},{14,238}... | collective-permute-start | bytes 393224 | tf_op jit(solution)/shard_map/ppermute | solution.py:450
  43.3 6.3 %collective-permute-start.11 = (bf16[16,32,128]{2,1,0:T(8,128)(2,1)S(1)}, bf16[16,32,128]{2,1,0:T(8,128)(2,1)S(1)}, u32[]{:S(2)}, u32[]{:S(2)}) collective-permute-start(bf16[16,32,128]{2,1,0:T(8,128)(2,1)S(1)} %collective-permute-done.7.refs_2_), channel_id=1, source_target_pairs={{0,32},{2,34},{4,36},{6,38},{8,40},{10,42},{12,44},{14,46},{16,48}... | collective-permute-start | bytes 393224 | tf_op jit(solution)/shard_map/ppermute | solution.py:450
  44.8 2.2 %copy-start = (bf16[8,4,256,256]{3,2,1,0:T(8,128)(2,1)S(1)}, bf16[8,4,256,256]{3,2,1,0:T(8,128)(2,1)}, u32[]{:S(2)}) copy-start(bf16[8,4,256,256]{3,2,1,0:T(8,128)(2,1)} %tiles.1) | copy-start | bytes 12582916
  47.0 15.9 %copy-start.3 = (bf16[8,64,64]{2,1,0:T(8,128)(2,1)S(1)}, bf16[8,64,64]{2,1,0:T(8,128)(2,1)}, u32[]{:S(2)}) copy-start(bf16[8,64,64]{2,1,0:T(8,128)(2,1)} %refs_11_.1) | copy-start | bytes 196612
  47.0 15.9 %copy-start.5 = (bf16[2,64,1024]{2,1,0:T(8,128)(2,1)S(1)}, bf16[2,64,1024]{2,1,0:T(8,128)(2,1)}, u32[]{:S(2)}) copy-start(bf16[2,64,1024]{2,1,0:T(8,128)(2,1)} %refs_10_.1) | copy-start | bytes 786436
  47.0 15.9 %copy-start.7 = (s32[8]{0:T(128)S(1)}, s32[8]{0:T(128)}, u32[]{:S(2)}) copy-start(s32[8]{0:T(128)} %parent.1) | copy-start | bytes 100
  47.0 15.9 %copy-start.8 = (s32[2,16]{1,0:T(2,128)S(1)}, s32[2,16]{1,0:T(2,128)}, u32[]{:S(2)}) copy-start(s32[2,16]{1,0:T(2,128)} %parent_far.1) | copy-start | bytes 388
  49.2 12.8 %copy-start.4 = (f32[64,2048]{1,0:T(8,128)}, f32[64,2048]{1,0:T(8,128)S(1)}, u32[]{:S(2)}) copy-start(f32[64,2048]{1,0:T(8,128)S(1)} %get-tuple-element.32.near_own_in) | copy-start | bytes 1572868
  49.2 13.7 %copy-start.10 = (s32[1,256]{1,0:T(1,128)}, s32[1,256]{1,0:T(1,128)S(1)}, u32[]{:S(2)}) copy-start(s32[1,256]{1,0:T(1,128)S(1)} %get-tuple-element.26.slots_in) | copy-start | bytes 3076
  49.6 4.3 %collective-permute-start.12 = (bf16[16,32,128]{2,1,0:T(8,128)(2,1)S(1)}, bf16[16,32,128]{2,1,0:T(8,128)(2,1)S(1)}, u32[]{:S(2)}, u32[]{:S(2)}) collective-permute-start(bf16[16,32,128]{2,1,0:T(8,128)(2,1)S(1)} %collective-permute-done.10.refs_3_), channel_id=1, source_target_pairs={{0,224},{2,226},{4,228},{6,230},{8,232},{10,234},{12,236},{14,238}... | collective-permute-start | bytes 393224 | tf_op jit(solution)/shard_map/ppermute | solution.py:454
  50.6 5.9 %collective-permute-start.13 = (bf16[16,32,128]{2,1,0:T(8,128)(2,1)S(1)}, bf16[16,32,128]{2,1,0:T(8,128)(2,1)S(1)}, u32[]{:S(2)}, u32[]{:S(2)}) collective-permute-start(bf16[16,32,128]{2,1,0:T(8,128)(2,1)S(1)} %collective-permute-done.11.refs_4_), channel_id=1, source_target_pairs={{0,32},{2,34},{4,36},{6,38},{8,40},{10,42},{12,44},{14,46},{16,48}... | collective-permute-start | bytes 393224 | tf_op jit(solution)/shard_map/ppermute | solution.py:454
  51.4 5.9 %collective-permute-start.14 = (bf16[8,32,128]{2,1,0:T(8,128)(2,1)S(1)}, bf16[8,32,128]{2,1,0:T(8,128)(2,1)S(1)}, u32[]{:S(2)}, u32[]{:S(2)}) collective-permute-start(bf16[8,32,128]{2,1,0:T(8,128)(2,1)S(1)} %slice.30), channel_id=1, source_target_pairs={{0,192},{2,194},{4,196},{6,198},{8,200},{10,202},{12,204},{14,206}... | collective-permute-start | bytes 196616 | tf_op jit(solution)/shard_map/ppermute | solution.py:456
  52.2 5.6 %collective-permute-start.15 = (bf16[8,32,128]{2,1,0:T(8,128)(2,1)S(1)}, bf16[8,32,128]{2,1,0:T(8,128)(2,1)S(1)}, u32[]{:S(2)}, u32[]{:S(2)}) collective-permute-start(bf16[8,32,128]{2,1,0:T(8,128)(2,1)S(1)} %slice.31), channel_id=1, source_target_pairs={{0,64},{2,66},{4,68},{6,70},{8,72},{10,74},{12,76},{14,78},{16,80}... | collective-permute-start | bytes 196616 | tf_op jit(solution)/shard_map/ppermute | solution.py:457
  57.8 5.1 %collective-permute-start.16 = (bf16[128,32,128]{2,1,0:T(8,128)(2,1)S(1)}, bf16[128,32,128]{2,1,0:T(8,128)(2,1)S(1)}, u32[]{:S(2)}, u32[]{:S(2)}) collective-permute-start(bf16[128,32,128]{2,1,0:T(8,128)(2,1)S(1)} %constant_dynamic-update-slice_fusion), channel_id=1, source_target_pairs={{0,2},{2,0},{4,6},{6,4},{8,10},{10,8},{12,14},{14,12},{16,18},{18,... | collective-permute-start | bytes 3145736 | tf_op jit(solution)/shard_map/ppermute | solution.py:459
  60.6 14.2 %collective-permute-start.17 = (bf16[64,2048]{1,0:T(8,128)(2,1)S(1)}, bf16[64,2048]{1,0:T(8,128)(2,1)S(1)}, u32[]{:S(2)}, u32[]{:S(2)}) collective-permute-start(bf16[64,2048]{1,0:T(8,128)(2,1)S(1)} %get-tuple-element.29), channel_id=1, source_target_pairs={{0,1},{1,0},{2,3},{3,2},{4,5},{5,4},{6,7},{7,6},{8,9},{9,8},{10,11... | collective-permute-start | bytes 786440 | tf_op jit(solution)/shard_map/ppermute | solution.py:452
  64.7 0.7 copy-start.2
